TPU v7x, 32 devices: a whole 2x2x4 slice. The times are simulated.
32 devices in a mesh: rows: 16 (over z, y, x), mp: 2 (over core).
Axes of the slice: x: 2, y: 2, z: 4, core: 2. Of those that a mesh axis runs over, the one named last changes fastest.
Arguments:
- atoms: bfloat16 [16384, 768], P(('rows', 'mp')), may hold values from -6 to 6
- time_embedding: bfloat16 [48, 768], replicated, may hold values from -6 to 6
- coordinates: int32 [3, 16384], P(None, ('rows', 'mp')), may hold values from -24 to 24
- item_lengths: int32 [48], replicated, may hold values from 1 to 896, as said below
- item_group: int32 [48], replicated, may hold values from 0 to 15, as said below
- query_weight: bfloat16 [768, 768], P(('rows', 'mp')), may hold values from -0.21875 to 0.21875
- key_weight: bfloat16 [768, 768], P(('rows', 'mp')), may hold values from -0.21875 to 0.21875
- value_weight: bfloat16 [768, 768], P(('rows', 'mp')), may hold values from -0.21875 to 0.21875
- out_weight: bfloat16 [768, 768], P(('rows', 'mp')), may hold values from -0.625 to 0.625
- up_weight: bfloat16 [768, 3072], P(('rows', 'mp')), may hold values from -0.21875 to 0.21875
- down_weight: bfloat16 [3072, 768], P(('rows', 'mp')), may hold values from -0.109375 to 0.109375
- value_bias: bfloat16 [768], P(('rows', 'mp')), may hold values from -2 to 2
- out_bias: bfloat16 [768], P(('rows', 'mp')), may hold values from -2 to 2
- up_bias: bfloat16 [3072], P(('rows', 'mp')), may hold values from -3 to 3
- down_bias: bfloat16 [768], P(('rows', 'mp')), may hold values from -2 to 2
- first_gain: bfloat16 [768], P(('rows', 'mp')), may hold values from 0.099609375 to 1.8984375
- first_shift: bfloat16 [768], P(('rows', 'mp')), may hold values from -2 to 2
- second_gain: bfloat16 [768], P(('rows', 'mp')), may hold values from 0.099609375 to 1.8984375
- second_shift: bfloat16 [768], P(('rows', 'mp')), may hold values from -2 to 2
- kernel_params: bfloat16 [4352], P(('rows', 'mp')), may hold values from -4 to 12, as said below
- cotangent: bfloat16 [16384, 768], P(('rows', 'mp')), may hold values from -6 to 6
Outputs:
- layer_out: bfloat16 [16384, 768], P(('rows', 'mp'))
- atoms_grad: float32 [16384, 768], P(('rows', 'mp'))
- query_weight_grad: float32 [768, 768], P(('rows', 'mp'))
- key_weight_grad: float32 [768, 768], P(('rows', 'mp'))
- value_weight_grad: float32 [768, 768], P(('rows', 'mp'))
- out_weight_grad: float32 [768, 768], P(('rows', 'mp'))
- up_weight_grad: float32 [768, 3072], P(('rows', 'mp'))
- down_weight_grad: float32 [3072, 768], P(('rows', 'mp'))
- value_bias_grad: float32 [768], P(('rows', 'mp'))
- out_bias_grad: float32 [768], P(('rows', 'mp'))
- up_bias_grad: float32 [3072], P(('rows', 'mp'))
- down_bias_grad: float32 [768], P(('rows', 'mp'))
- first_gain_grad: float32 [768], P(('rows', 'mp'))
- first_shift_grad: float32 [768], P(('rows', 'mp'))
- second_gain_grad: float32 [768], P(('rows', 'mp'))
- second_shift_grad: float32 [768], P(('rows', 'mp'))
- kernel_params_grad: float32 [4352], P(('rows', 'mp'))
Inputs may be any that keep to these rules, and one draw needn't show every extreme that they name: `item_group`: each row group is named by exactly 3 items. `item_lengths`: in every row group one item has more than 512 rows and the others at most 64; a group's items fill at most 1024 rows. `kernel_params`: widths lie in 0.5 to 4.
All inputs are finite; a program needn't handle non-finite values.
Results may differ from a plain program's by a relative error of at most 0.02.
Values may be sent and summed in bfloat16 or wider, within the bound.
A program may use at most 576 MiB of HBM per device.

v0:
```python
import math

import jax
import jax.numpy as jnp
from jax import lax
from jax.sharding import PartitionSpec as P

HEADS = 32
KERN = 128


def from_partner(block, axis, distance):
    count = lax.axis_size(axis)
    route = []
    for low in range(count):
        high = low | 1 << distance
        if high != low and high < count:
            route += [(low, high), (high, low)]
    return lax.ppermute(block, axis, route)


def row_items(global_rows, group_rows, lengths, groups):
    count = lengths.shape[0]
    order = jnp.arange(count, dtype=jnp.int32)
    earlier = (groups[:, None] == groups[None, :]) & (order[None, :] < order[:, None])
    starts = jnp.sum(jnp.where(earlier, lengths[None, :], 0), axis=1)
    group_of = global_rows // group_rows
    place = global_rows - group_of * group_rows
    hits = (
        (groups[None, :] == group_of[:, None])
        & (place[:, None] >= starts[None, :])
        & (place[:, None] < starts[None, :] + lengths[None, :])
    )
    item = jnp.sum(jnp.where(hits, order[None, :], 0), axis=1)
    return (item, jnp.any(hits, axis=1))


def layer_norm(value, gain, shift):
    centre = value - jnp.mean(value, axis=-1, keepdims=True)
    spread = jnp.mean(centre * centre, axis=-1, keepdims=True)
    return centre * lax.rsqrt(spread + 1e-05) * gain + shift


def densities(coord_near, coord_all, means, widths):
    diff = coord_near[:, :, None] - coord_all[:, None, :]
    dist = jnp.sqrt(jnp.sum(diff * diff, axis=0)) * 0.25
    scaled = (dist[:, :, None] - means) / widths
    return jnp.exp(-0.5 * scaled * scaled) / (widths * math.sqrt(2.0 * math.pi))


def exact_gelu(value):
    return jax.nn.gelu(value, approximate=False)


def kernel_split(kernel_full):
    table = kernel_full.astype(jnp.float32)
    return (table[:KERN], table[KERN : 2 * KERN], kernel_full[2 * KERN :].reshape(KERN, HEADS))


def pair_bias(coord_near, coord_all, kernel_full):
    means, widths, mix = kernel_split(kernel_full)
    rows = coord_near.shape[1]
    step = math.gcd(rows, 64)
    span = coord_all.shape[1]
    pieces = coord_near.reshape(3, rows // step, step).transpose(1, 0, 2)

    def one_piece(piece):
        phi = densities(piece, coord_all, means, widths).astype(jnp.bfloat16)
        return jnp.dot(
            phi.reshape(step * span, KERN), mix, preferred_element_type=jnp.float32
        ).reshape(step, span, HEADS)

    bias = lax.map(one_piece, pieces)
    return bias.reshape(rows, span, HEADS).transpose(2, 0, 1)


def pair_bias_grads(coord_near, coord_all, kernel_full, grad_scores):
    means, widths, mix = kernel_split(kernel_full)
    rows = coord_near.shape[1]
    step = math.gcd(rows, 64)
    span = coord_all.shape[1]
    pieces = coord_near.reshape(3, rows // step, step).transpose(1, 0, 2)
    grads = grad_scores.transpose(1, 2, 0).reshape(rows // step, step, span, HEADS)

    def one_piece(carry, inputs):
        piece, grad = inputs

        def local_density(centre, spread):
            return densities(piece, coord_all, centre, spread)

        phi, pull = jax.vjp(local_density, means, widths)
        phi_low = phi.astype(jnp.bfloat16).reshape(step * span, KERN)
        flat = grad.reshape(step * span, HEADS)
        mix_grad = lax.dot_general(
            phi_low, flat, (((0,), (0,)), ((), ())), preferred_element_type=jnp.float32
        )
        phi_grad = lax.dot_general(
            flat, mix, (((1,), (1,)), ((), ())), preferred_element_type=jnp.float32
        )
        mean_grad, width_grad = pull(phi_grad.reshape(step, span, KERN))
        return ((carry[0] + mean_grad, carry[1] + width_grad, carry[2] + mix_grad), None)

    start = (
        jnp.zeros((KERN,), jnp.float32),
        jnp.zeros((KERN,), jnp.float32),
        jnp.zeros((KERN, HEADS), jnp.float32),
    )
    totals, unused = lax.scan(one_piece, start, (pieces, grads))
    return jnp.concatenate([totals[0], totals[1], totals[2].reshape(-1)])


def front(full, atoms, embed):
    h_zero = atoms.astype(jnp.float32) + embed
    normed, pull_one = jax.vjp(
        layer_norm, h_zero, full[10].astype(jnp.float32), full[11].astype(jnp.float32)
    )
    normed_low = normed.astype(jnp.bfloat16)
    query = jnp.dot(normed_low, full[0], preferred_element_type=jnp.float32).astype(jnp.bfloat16)
    keys = jnp.dot(normed_low, full[1], preferred_element_type=jnp.float32).astype(jnp.bfloat16)
    values = (
        jnp.dot(normed_low, full[2], preferred_element_type=jnp.float32)
        + full[6].astype(jnp.float32)
    ).astype(jnp.bfloat16)
    return (h_zero, normed_low, pull_one, query, keys, values)


def middle(full, h_zero, query, keys, values, far_keys, far_values, coord_near, coord_far, allowed):
    keys_all = jnp.concatenate([keys, far_keys], axis=0)
    values_all = jnp.concatenate([values, far_values], axis=0)
    coord_all = jnp.concatenate([coord_near, coord_far], axis=1)
    bias = pair_bias(coord_near, coord_all, full[14])
    rows = query.shape[0]
    size = query.shape[1] // HEADS
    query_heads = query.reshape(rows, HEADS, size)
    key_heads = keys_all.reshape(-1, HEADS, size)
    value_heads = values_all.reshape(-1, HEADS, size)
    raw = jnp.einsum("ihd,jhd->hij", query_heads, key_heads, preferred_element_type=jnp.float32)
    scores = jnp.where(allowed[None], raw * size ** (-0.5) + bias, -1e30)
    top = jnp.max(scores, axis=-1, keepdims=True)
    expo = jnp.exp(scores - top)
    probs = expo / jnp.sum(expo, axis=-1, keepdims=True)
    probs_low = probs.astype(jnp.bfloat16)
    mixed = jnp.einsum("hij,jhd->ihd", probs_low, value_heads, preferred_element_type=jnp.float32)
    mixed_low = mixed.reshape(rows, -1).astype(jnp.bfloat16)
    h_one = (
        h_zero
        + jnp.dot(mixed_low, full[3], preferred_element_type=jnp.float32)
        + full[7].astype(jnp.float32)
    )
    second, pull_two = jax.vjp(
        layer_norm, h_one, full[12].astype(jnp.float32), full[13].astype(jnp.float32)
    )
    second_low = second.astype(jnp.bfloat16)
    up_pre = jnp.dot(second_low, full[4], preferred_element_type=jnp.float32) + full[8].astype(
        jnp.float32
    )
    act, gelu_pull = jax.vjp(exact_gelu, up_pre)
    act_low = act.astype(jnp.bfloat16)
    h_two = (
        h_one
        + jnp.dot(act_low, full[5], preferred_element_type=jnp.float32)
        + full[9].astype(jnp.float32)
    )
    return (
        keys_all,
        values_all,
        coord_all,
        probs,
        probs_low,
        mixed_low,
        pull_two,
        second_low,
        gelu_pull,
        act_low,
        h_two,
    )


def attention_back(query, keys_all, values_all, probs, probs_low, grad_mixed):
    rows = query.shape[0]
    width = query.shape[1]
    size = width // HEADS
    scale = size ** (-0.5)
    query_heads = query.reshape(rows, HEADS, size)
    key_heads = keys_all.reshape(-1, HEADS, size)
    value_heads = values_all.reshape(-1, HEADS, size)
    grad_heads = grad_mixed.reshape(rows, HEADS, size)
    grad_probs = (
        jnp.einsum("ihd,jhd->hij", grad_heads, value_heads, preferred_element_type=jnp.float32)
        .astype(jnp.bfloat16)
        .astype(jnp.float32)
    )
    delta = jnp.sum(probs * grad_probs, axis=-1, keepdims=True)
    grad_scores = (probs * (grad_probs - delta)).astype(jnp.bfloat16)
    grad_query = (
        (
            jnp.einsum("hij,jhd->ihd", grad_scores, key_heads, preferred_element_type=jnp.float32)
            * scale
        )
        .reshape(rows, width)
        .astype(jnp.bfloat16)
    )
    grad_keys = (
        jnp.einsum(
            "hij,ihd->jhd", grad_scores, query_heads, preferred_element_type=jnp.float32
        ).reshape(-1, width)
        * scale
    )
    grad_values = jnp.einsum(
        "hij,ihd->jhd", probs_low, grad_heads, preferred_element_type=jnp.float32
    ).reshape(-1, width)
    return (grad_query, grad_keys, grad_values, grad_scores)


def col_sum(value):
    return jnp.sum(value.astype(jnp.float32), axis=0)


def left_dot(left, right):
    return lax.dot_general(
        left, right, (((0,), (0,)), ((), ())), preferred_element_type=jnp.float32
    )


def right_dot(left, right):
    return lax.dot_general(
        left, right, (((1,), (1,)), ((), ())), preferred_element_type=jnp.float32
    )


def on_device(
    atoms,
    time_embedding,
    coordinates,
    item_lengths,
    item_group,
    query_weight,
    key_weight,
    value_weight,
    out_weight,
    up_weight,
    down_weight,
    value_bias,
    out_bias,
    up_bias,
    down_bias,
    first_gain,
    first_shift,
    second_gain,
    second_shift,
    kernel_params,
    cotangent,
):
    rows_here = atoms.shape[0]
    pair_size = lax.axis_size("mp")
    side = lax.axis_index("mp")
    pair_index = lax.axis_index("rows")
    group_rows = rows_here * pair_size
    counter = jnp.arange(rows_here, dtype=jnp.int32)
    near_rows = (pair_index * pair_size + side) * rows_here + counter
    far_rows = (pair_index * pair_size + 1 - side) * rows_here + counter
    near_item, near_valid = row_items(near_rows, group_rows, item_lengths, item_group)
    far_item, far_valid = row_items(far_rows, group_rows, item_lengths, item_group)
    key_item = jnp.concatenate([near_item, far_item])
    key_valid = jnp.concatenate([near_valid, far_valid])
    key_rows = jnp.concatenate([near_rows, far_rows])
    allowed = jnp.where(
        near_valid[:, None],
        (near_item[:, None] == key_item[None, :]) & key_valid[None, :],
        near_rows[:, None] == key_rows[None, :],
    )
    count = item_lengths.shape[0]
    picks = (
        (near_item[:, None] == jnp.arange(count, dtype=jnp.int32)[None, :]) & near_valid[:, None]
    ).astype(jnp.bfloat16)
    embed = jnp.dot(picks, time_embedding, preferred_element_type=jnp.float32)
    coord_near = coordinates.astype(jnp.float32)
    coord_low = coordinates.astype(jnp.bfloat16)
    full = (
        lax.all_gather(query_weight, ("rows", "mp"), axis=0, tiled=True),
        lax.all_gather(key_weight, ("rows", "mp"), axis=0, tiled=True),
        lax.all_gather(value_weight, ("rows", "mp"), axis=0, tiled=True),
        lax.all_gather(out_weight, ("rows", "mp"), axis=0, tiled=True),
        lax.all_gather(up_weight, ("rows", "mp"), axis=0, tiled=True),
        lax.all_gather(down_weight, ("rows", "mp"), axis=0, tiled=True),
        lax.all_gather(value_bias, ("rows", "mp"), axis=0, tiled=True),
        lax.all_gather(out_bias, ("rows", "mp"), axis=0, tiled=True),
        lax.all_gather(up_bias, ("rows", "mp"), axis=0, tiled=True),
        lax.all_gather(down_bias, ("rows", "mp"), axis=0, tiled=True),
        lax.all_gather(first_gain, ("rows", "mp"), axis=0, tiled=True),
        lax.all_gather(first_shift, ("rows", "mp"), axis=0, tiled=True),
        lax.all_gather(second_gain, ("rows", "mp"), axis=0, tiled=True),
        lax.all_gather(second_shift, ("rows", "mp"), axis=0, tiled=True),
        lax.all_gather(kernel_params, ("rows", "mp"), axis=0, tiled=True),
    )
    h_zero, normed_low, pull_one, query, keys, values = front(full, atoms, embed)
    far_keys, far_values, far_coord = from_partner((keys, values, coord_low), "mp", 0)
    state = middle(
        full,
        h_zero,
        query,
        keys,
        values,
        far_keys,
        far_values,
        coord_near,
        far_coord.astype(jnp.float32),
        allowed,
    )
    layer_out = jnp.where(near_valid[:, None], state[10], 0.0).astype(jnp.bfloat16)
    full_back = (
        lax.all_gather(query_weight, ("rows", "mp"), axis=0, tiled=True),
        lax.all_gather(key_weight, ("rows", "mp"), axis=0, tiled=True),
        lax.all_gather(value_weight, ("rows", "mp"), axis=0, tiled=True),
        lax.all_gather(out_weight, ("rows", "mp"), axis=0, tiled=True),
        lax.all_gather(up_weight, ("rows", "mp"), axis=0, tiled=True),
        lax.all_gather(down_weight, ("rows", "mp"), axis=0, tiled=True),
        lax.all_gather(value_bias, ("rows", "mp"), axis=0, tiled=True),
        lax.all_gather(out_bias, ("rows", "mp"), axis=0, tiled=True),
        lax.all_gather(up_bias, ("rows", "mp"), axis=0, tiled=True),
        lax.all_gather(down_bias, ("rows", "mp"), axis=0, tiled=True),
        lax.all_gather(first_gain, ("rows", "mp"), axis=0, tiled=True),
        lax.all_gather(first_shift, ("rows", "mp"), axis=0, tiled=True),
        lax.all_gather(second_gain, ("rows", "mp"), axis=0, tiled=True),
        lax.all_gather(second_shift, ("rows", "mp"), axis=0, tiled=True),
        lax.all_gather(kernel_params, ("rows", "mp"), axis=0, tiled=True),
    )
    h_back, normed_back, pull_back, query_back, keys_back, values_back = front(
        full_back, atoms, embed
    )
    far_keys_back, far_values_back, far_coord_back = from_partner(
        (keys_back, values_back, coord_low), "mp", 0
    )
    state_back = middle(
        full_back,
        h_back,
        query_back,
        keys_back,
        values_back,
        far_keys_back,
        far_values_back,
        coord_near,
        far_coord_back.astype(jnp.float32),
        allowed,
    )
    (
        keys_all,
        values_all,
        coord_all,
        probs,
        probs_low,
        mixed_low,
        pull_two,
        second_low,
        gelu_pull,
        act_low,
        unused_two,
    ) = state_back
    grad_two = jnp.where(near_valid[:, None], cotangent.astype(jnp.float32), 0.0)
    grad_ffn = grad_two.astype(jnp.bfloat16)
    down_bias_grad = col_sum(grad_ffn)
    down_weight_grad = left_dot(act_low, grad_ffn)
    grad_act = right_dot(grad_ffn, full_back[5])
    grad_up = gelu_pull(grad_act)[0].astype(jnp.bfloat16)
    up_bias_grad = col_sum(grad_up)
    up_weight_grad = left_dot(second_low, grad_up)
    grad_second = right_dot(grad_up, full_back[4])
    grad_part, second_gain_grad, second_shift_grad = pull_two(grad_second)
    grad_one = grad_two + grad_part
    grad_att = grad_one.astype(jnp.bfloat16)
    out_bias_grad = col_sum(grad_att)
    out_weight_grad = left_dot(mixed_low, grad_att)
    grad_mixed = right_dot(grad_att, full_back[3]).astype(jnp.bfloat16)
    grad_query, grad_keys, grad_values, grad_scores = attention_back(
        query_back, keys_all, values_all, probs, probs_low, grad_mixed
    )
    back_keys, back_values = (
        from_partner(grad_keys[rows_here:].astype(jnp.bfloat16), "mp", 0).astype(jnp.float32),
        from_partner(grad_values[rows_here:].astype(jnp.bfloat16), "mp", 0).astype(jnp.float32),
    )
    grad_keys_low = (grad_keys[:rows_here] + back_keys).astype(jnp.bfloat16)
    grad_values_low = (grad_values[:rows_here] + back_values).astype(jnp.bfloat16)
    kernel_params_grad = pair_bias_grads(coord_near, coord_all, full_back[14], grad_scores)
    query_weight_grad = left_dot(normed_back, grad_query)
    key_weight_grad = left_dot(normed_back, grad_keys_low)
    value_weight_grad = left_dot(normed_back, grad_values_low)
    value_bias_grad = col_sum(grad_values_low)
    grad_normed = (
        right_dot(grad_query, full_back[0])
        + right_dot(grad_keys_low, full_back[1])
        + right_dot(grad_values_low, full_back[2])
    )
    grad_zero, first_gain_grad, first_shift_grad = pull_back(grad_normed)
    atoms_grad = grad_one + grad_zero
    sums = (
        lax.psum_scatter(query_weight_grad, ("rows", "mp"), scatter_dimension=0, tiled=True),
        lax.psum_scatter(key_weight_grad, ("rows", "mp"), scatter_dimension=0, tiled=True),
        lax.psum_scatter(value_weight_grad, ("rows", "mp"), scatter_dimension=0, tiled=True),
        lax.psum_scatter(out_weight_grad, ("rows", "mp"), scatter_dimension=0, tiled=True),
        lax.psum_scatter(up_weight_grad, ("rows", "mp"), scatter_dimension=0, tiled=True),
        lax.psum_scatter(down_weight_grad, ("rows", "mp"), scatter_dimension=0, tiled=True),
        lax.psum_scatter(value_bias_grad, ("rows", "mp"), scatter_dimension=0, tiled=True),
        lax.psum_scatter(out_bias_grad, ("rows", "mp"), scatter_dimension=0, tiled=True),
        lax.psum_scatter(up_bias_grad, ("rows", "mp"), scatter_dimension=0, tiled=True),
        lax.psum_scatter(down_bias_grad, ("rows", "mp"), scatter_dimension=0, tiled=True),
        lax.psum_scatter(first_gain_grad, ("rows", "mp"), scatter_dimension=0, tiled=True),
        lax.psum_scatter(first_shift_grad, ("rows", "mp"), scatter_dimension=0, tiled=True),
        lax.psum_scatter(second_gain_grad, ("rows", "mp"), scatter_dimension=0, tiled=True),
        lax.psum_scatter(second_shift_grad, ("rows", "mp"), scatter_dimension=0, tiled=True),
        lax.psum_scatter(kernel_params_grad, ("rows", "mp"), scatter_dimension=0, tiled=True),
    )
    return (
        layer_out,
        atoms_grad,
        sums[0],
        sums[1],
        sums[2],
        sums[3],
        sums[4],
        sums[5],
        sums[6],
        sums[7],
        sums[8],
        sums[9],
        sums[10],
        sums[11],
        sums[12],
        sums[13],
        sums[14],
    )


def solution(mesh):
    in_specs = (
        P(("rows", "mp"), None),
        P(),
        P(None, ("rows", "mp")),
        P(),
        P(),
        P(("rows", "mp"), None),
        P(("rows", "mp"), None),
        P(("rows", "mp"), None),
        P(("rows", "mp"), None),
        P(("rows", "mp"), None),
        P(("rows", "mp"), None),
        P(("rows", "mp")),
        P(("rows", "mp")),
        P(("rows", "mp")),
        P(("rows", "mp")),
        P(("rows", "mp")),
        P(("rows", "mp")),
        P(("rows", "mp")),
        P(("rows", "mp")),
        P(("rows", "mp")),
        P(("rows", "mp"), None),
    )
    out_specs = (
        P(("rows", "mp"), None),
        P(("rows", "mp"), None),
        P(("rows", "mp"), None),
        P(("rows", "mp"), None),
        P(("rows", "mp"), None),
        P(("rows", "mp"), None),
        P(("rows", "mp"), None),
        P(("rows", "mp"), None),
        P(("rows", "mp")),
        P(("rows", "mp")),
        P(("rows", "mp")),
        P(("rows", "mp")),
        P(("rows", "mp")),
        P(("rows", "mp")),
        P(("rows", "mp")),
        P(("rows", "mp")),
        P(("rows", "mp")),
    )
    return jax.shard_map(
        on_device, mesh=mesh, in_specs=in_specs, out_specs=out_specs, check_vma=False
    )
```

profile of v0, /device:TPU:11, one launch (start us, length us, event | category | flops | bytes accessed | tf_op | source)
XLA Modules:
  0.0 1343.4 jit_solution(6346601415646372265)
XLA Ops:
  23.0 40.3 %all-reduce.19 = (bf16[768]{0:T(1024)(128)(2,1)S(1)}, bf16[768]{0:T(1024)(128)(2,1)S(1)}, bf16[768]{0:T(1024)(128)(2,1)S(1)}, bf16[4352]{0:T(1024)(128)(2,1)S(1)...) all-reduce(bf16[768]{0:T(1024)(128)(2,1)S(1)} %dynamic-update-slice, ...), channel_id=1, replica_groups=mesh['rows'=16,'mp'=2] {'rows','mp'}, use_global_device_ids=true, to_apply=%add.1 | all-reduce | flops 12800 | bytes 51200
  75.2 46.4 %all-gather.7.cloned.1.call-done = bf16[768,768]{1,0:T(8,128)(2,1)} async-done(((bf16[24,768]{1,0:T(8,128)(2,1)}), bf16[768,768]{1,0:T(8,128)(2,1)}) %all-gather.7.cloned.1.call-update) | async-done | bytes 1179664 | tf_op jit(solution)/shard_map/all_gather | solution.py:282
  124.8 197.3 %while.30 = (s32[]{:T(128)}, f32[8,64,1024,32]{2,1,0,3:T(8,128)}, f32[8,3,64]{2,1,0:T(4,128)S(1)}, f32[3,1024]{1,0:T(4,128)S(1)}, f32[128]{0:T(128)S(1)}, /*inde...) while((s32[]{:T(128)}, f32[8,64,1024,32]{2,1,0,3:T(8,128)}, f32[8,3,64]{2,1,0:T(4,128)S(1)}, ...), condition=%wide.region_9.10_spmd, body=%wide.region_7.9_spmd.sunk | while | flops 587792512 | bytes 26239844 | solution.py:73
  125.1 16.4 %fusion.162 = f32[1,64,1024,32]{2,3,1,0:T(8,128)S(1)} fusion(f32[128]{0:T(128)S(1)} %broadcast_multiply_fusion.5, f32[128]{0:T(128)S(1)} %get-tuple-element.534, f32[128]{0:T(128)S(1)} %get-tuple-element.533, f32[64,1024]{1,0:T(8,128)S(1)} %sqrt_multiply_fusion.3, bf16[128,32]{0,1:T(8,128)(2,1)S(1)} %get-tuple-element.535), kind=kOutput, calls=%fused_computation.6.clone.1 | convolution fusion | flops 587202560 | bytes 8660480 | tf_op jit(solution)/shard_map/while/body/eval_jaxpr/dot_general | solution.py:69
  174.4 16.4 %fusion.162 = f32[1,64,1024,32]{2,3,1,0:T(8,128)S(1)} fusion(f32[128]{0:T(128)S(1)} %broadcast_multiply_fusion.5, f32[128]{0:T(128)S(1)} %get-tuple-element.534, f32[128]{0:T(128)S(1)} %get-tuple-element.533, f32[64,1024]{1,0:T(8,128)S(1)} %sqrt_multiply_fusion.3, bf16[128,32]{0,1:T(8,128)(2,1)S(1)} %get-tuple-element.535), kind=kOutput, calls=%fused_computation.6.clone.1 | convolution fusion | flops 587202560 | bytes 8660480 | tf_op jit(solution)/shard_map/while/body/eval_jaxpr/dot_general | solution.py:69
  273.0 16.4 %fusion.162 = f32[1,64,1024,32]{2,3,1,0:T(8,128)S(1)} fusion(f32[128]{0:T(128)S(1)} %broadcast_multiply_fusion.5, f32[128]{0:T(128)S(1)} %get-tuple-element.534, f32[128]{0:T(128)S(1)} %get-tuple-element.533, f32[64,1024]{1,0:T(8,128)S(1)} %sqrt_multiply_fusion.3, bf16[128,32]{0,1:T(8,128)(2,1)S(1)} %get-tuple-element.535), kind=kOutput, calls=%fused_computation.6.clone.1 | convolution fusion | flops 587202560 | bytes 8660480 | tf_op jit(solution)/shard_map/while/body/eval_jaxpr/dot_general | solution.py:69
  335.4 65.9 %fusion.92 = (f32[32,512]{1,0:T(8,128)S(1)}, f32[32,512,1024]{2,1,0:T(8,128)}, f32[32,512,1024]{2,1,0:T(8,128)}) fusion(f32[8,64,1024,32]{2,1,0,3:T(8,128)} %get-tuple-element.167, pred[512,1024]{1,0:T(8,128)(4,1)S(1)} %copy-done.13, bf16[512,32,24]{0,2,1:T(8,128)(2,1)S(1)} %bitcast.168, bf16[1024,32,24]{0,2,1:T(8,128)(2,1)S(1)} %bitcast.166), kind=kOutput, calls=%fused_computation.182 | convolution fusion | flops 872398848 | bytes 204275712 | tf_op jit(solution)/shard_map/ihd,jhd->hij/dot_general | solution.py:137
  401.2 21.5 %fusion.41 = f32[32,512]{1,0:T(8,128)S(1)} fusion(f32[32,512,1024]{2,1,0:T(8,128)} %get-tuple-element.350, f32[32,512]{1,0:T(8,128)S(1)} %get-tuple-element.349), kind=kLoop, calls=%fused_computation.63 | loop fusion | flops 33538048 | bytes 67239936 | tf_op jit(solution)/shard_map/reduce_sum | solution.py:141
  422.7 24.0 %fusion.58 = bf16[32,24,512]{2,1,0:T(8,128)(2,1)} fusion(bf16[1024,32,24]{0,2,1:T(8,128)(2,1)S(1)} %bitcast.173, f32[32,512,1024]{2,1,0:T(8,128)} %get-tuple-element.350, f32[32,512]{1,0:T(8,128)S(1)} %fusion.41, f32[32,512]{1,0:T(8,128)S(1)} %get-tuple-element.349), kind=kOutput, calls=%fused_computation.124 | convolution fusion | flops 856031232 | bytes 69599232 | tf_op jit(solution)/shard_map/hij,jhd->ihd/dot_general | solution.py:143
  449.6 19.9 %multiply_convert_fusion = (bf16[512,3072]{1,0:T(8,128)(2,1)}, f32[512,3072]{1,0:T(8,128)}, f32[512,3072]{1,0:T(8,128)}) fusion(f32[3072]{0:T(1024)S(1)} %copy-done.69, bf16[768,3072]{1,0:T(8,128)(2,1)} %all-gather.15.cloned.1.call-done, f32[512,768]{1,0:T(8,128)S(1)} %get-tuple-element.369, f32[768]{0:T(1024)S(1)} %copy-done.75, f32[768]{0:T(1024)S(1)} %copy-done.65, ...), kind=kOutput, calls=%fused_computation.73 | convolution fusion | flops 2521694208 | bytes 22042624 | tf_op jit(solution)/shard_map/dot_general | solution.py:154
  492.8 37.0 %fusion.29 = (f32[32,512]{1,0:T(8,128)S(1)}, bf16[32,512,1024]{2,1,0:T(8,128)(2,1)}) fusion(f32[32,512]{1,0:T(8,128)S(1)} %fusion.41, f32[32,512,1024]{2,1,0:T(8,128)} %get-tuple-element.350, f32[32,512]{1,0:T(8,128)S(1)} %get-tuple-element.349, bf16[512,32,24]{0,2,1:T(8,128)(2,1)S(1)} %bitcast.176, bf16[1024,32,24]{0,2,1:T(8,128)(2,1)S(1)} %bitcast.174), kind=kOutput, calls=%fused_computation.48 | convolution fusion | flops 905953280 | bytes 103219200 | tf_op jit(solution)/shard_map/ihd,jhd->hij/dot_general | solution.py:189
  529.8 43.5 %fusion.31 = bf16[32,512,1024]{2,1,0:T(8,128)(2,1)} fusion(bf16[32,512,1024]{2,1,0:T(8,128)(2,1)} %get-tuple-element.373, f32[32,512]{1,0:T(8,128)S(1)} %get-tuple-element.372, f32[32,512]{1,0:T(8,128)S(1)} %fusion.41, f32[32,512,1024]{2,1,0:T(8,128)} %get-tuple-element.350, f32[32,512]{1,0:T(8,128)S(1)} %get-tuple-element.349), kind=kLoop, calls=%fused_computation.50 | loop fusion | flops 100663296 | bytes 134414336 | tf_op jit(solution)/shard_map/convert_element_type | solution.py:194
  589.9 22.7 %fusion.52 = f32[1024,32,24]{0,2,1:T(8,128)S(1)} fusion(bf16[512,32,24]{0,2,1:T(8,128)(2,1)S(1)} %bitcast.177, f32[32,512,1024]{2,1,0:T(8,128)} %get-tuple-element.350, f32[32,512]{1,0:T(8,128)S(1)} %fusion.41, f32[32,512]{1,0:T(8,128)S(1)} %get-tuple-element.349), kind=kOutput, calls=%fused_computation.91 | convolution fusion | flops 855638016 | bytes 71172096 | tf_op jit(solution)/shard_map/hij,ihd->jhd/dot_general | solution.py:209
  655.8 64.2 %fusion.34 = bf16[512,1024,32]{1,0,2:T(8,128)(2,1)} fusion(bf16[32,512,1024]{2,1,0:T(8,128)(2,1)} %get-tuple-element.373, f32[8,64,1024,32]{2,1,0,3:T(8,128)} %get-tuple-element.167, f32[32,512,1024]{2,1,0:T(8,128)} %get-tuple-element.367, f32[512,32]{0,1:T(8,128)S(1)} %bitcast.183, f32[512,32]{0,1:T(8,128)S(1)} %bitcast.182, f32[512,32]{0,1:T(8,128)S(1)} %bitcast.175, ...), kind=kLoop, calls=%fused_computation.53 | loop fusion | flops 150994944 | bytes 202047488 | tf_op jit(solution)/shard_map/convert_element_type | solution.py:194
  720.1 555.6 %while.31 = (s32[]{:T(128)}, f32[128]{0:T(128)}, f32[128]{0:T(128)}, f32[128,32]{0,1:T(8,128)S(1)}, f32[8,3,64]{2,1,0:T(4,128)}, /*index=5*/f32[3,1024]{1,0:T(4,...) while((s32[]{:T(128)}, f32[128]{0:T(128)}, ...), condition=%wide.region_46.47_spmd.clone, body=%wide.region_41.46_spmd.clone.sunk | while | flops 1309222144 | bytes 170265792 | solution.py:108
  740.2 26.9 %fusion.167 = (f32[64,1024,128]{2,1,0:T(8,128)}, f32[64,1024,128]{2,1,0:T(8,128)}) fusion(f32[128]{0:T(128)S(1)} %get-tuple-element.502, f32[128]{0:T(128)S(1)} %get-tuple-element.570, f32[128]{0:T(128)S(1)} %get-tuple-element.569, f32[64,1024]{1,0:T(8,128)S(1)} %get-tuple-element.503, bf16[128,32]{0,1:T(8,128)(2,1)S(1)} %get-tuple-element.572, ...), kind=kOutput, calls=%fused_computation.20.clone.1 | convolution fusion | flops 620756992 | bytes 71575040 | tf_op jit(solution)/shard_map/while/body/eval_jaxpr/dot_general | solution.py:97
  767.1 21.4 %fusion.168 = (f32[128]{0:T(128)S(1)}, f32[128]{0:T(128)S(1)}, f32[128]{0:T(128)S(1)}) fusion(f32[64,1024,128]{2,1,0:T(8,128)} %get-tuple-element.504, f32[128]{0:T(128)S(1)} %copy-done.67, f32[128]{0:T(128)S(1)} %get-tuple-element.569, f32[64,1024]{1,0:T(8,128)S(1)} %get-tuple-element.503, f32[128]{0:T(128)S(1)} %get-tuple-element.570, ...), kind=kLoop, calls=%fused_computation.18.clone.1 | loop fusion | flops 100662912 | bytes 67374592 | tf_op jit(solution)/shard_map/while/body/eval_jaxpr/transpose(jvp())/reduce_sum | solution.py:47
  809.1 26.9 %fusion.167 = (f32[64,1024,128]{2,1,0:T(8,128)}, f32[64,1024,128]{2,1,0:T(8,128)}) fusion(f32[128]{0:T(128)S(1)} %get-tuple-element.502, f32[128]{0:T(128)S(1)} %get-tuple-element.570, f32[128]{0:T(128)S(1)} %get-tuple-element.569, f32[64,1024]{1,0:T(8,128)S(1)} %get-tuple-element.503, bf16[128,32]{0,1:T(8,128)(2,1)S(1)} %get-tuple-element.572, ...), kind=kOutput, calls=%fused_computation.20.clone.1 | convolution fusion | flops 620756992 | bytes 71575040 | tf_op jit(solution)/shard_map/while/body/eval_jaxpr/dot_general | solution.py:97
  836.0 21.9 %fusion.168 = (f32[128]{0:T(128)S(1)}, f32[128]{0:T(128)S(1)}, f32[128]{0:T(128)S(1)}) fusion(f32[64,1024,128]{2,1,0:T(8,128)} %get-tuple-element.504, f32[128]{0:T(128)S(1)} %copy-done.67, f32[128]{0:T(128)S(1)} %get-tuple-element.569, f32[64,1024]{1,0:T(8,128)S(1)} %get-tuple-element.503, f32[128]{0:T(128)S(1)} %get-tuple-element.570, ...), kind=kLoop, calls=%fused_computation.18.clone.1 | loop fusion | flops 100662912 | bytes 67374592 | tf_op jit(solution)/shard_map/while/body/eval_jaxpr/transpose(jvp())/reduce_sum | solution.py:47
  878.5 26.9 %fusion.167 = (f32[64,1024,128]{2,1,0:T(8,128)}, f32[64,1024,128]{2,1,0:T(8,128)}) fusion(f32[128]{0:T(128)S(1)} %get-tuple-element.502, f32[128]{0:T(128)S(1)} %get-tuple-element.570, f32[128]{0:T(128)S(1)} %get-tuple-element.569, f32[64,1024]{1,0:T(8,128)S(1)} %get-tuple-element.503, bf16[128,32]{0,1:T(8,128)(2,1)S(1)} %get-tuple-element.572, ...), kind=kOutput, calls=%fused_computation.20.clone.1 | convolution fusion | flops 620756992 | bytes 71575040 | tf_op jit(solution)/shard_map/while/body/eval_jaxpr/dot_general | solution.py:97
  905.4 22.5 %fusion.168 = (f32[128]{0:T(128)S(1)}, f32[128]{0:T(128)S(1)}, f32[128]{0:T(128)S(1)}) fusion(f32[64,1024,128]{2,1,0:T(8,128)} %get-tuple-element.504, f32[128]{0:T(128)S(1)} %copy-done.67, f32[128]{0:T(128)S(1)} %get-tuple-element.569, f32[64,1024]{1,0:T(8,128)S(1)} %get-tuple-element.503, f32[128]{0:T(128)S(1)} %get-tuple-element.570, ...), kind=kLoop, calls=%fused_computation.18.clone.1 | loop fusion | flops 100662912 | bytes 67374592 | tf_op jit(solution)/shard_map/while/body/eval_jaxpr/transpose(jvp())/reduce_sum | solution.py:47
  948.8 26.9 %fusion.167 = (f32[64,1024,128]{2,1,0:T(8,128)}, f32[64,1024,128]{2,1,0:T(8,128)}) fusion(f32[128]{0:T(128)S(1)} %get-tuple-element.502, f32[128]{0:T(128)S(1)} %get-tuple-element.570, f32[128]{0:T(128)S(1)} %get-tuple-element.569, f32[64,1024]{1,0:T(8,128)S(1)} %get-tuple-element.503, bf16[128,32]{0,1:T(8,128)(2,1)S(1)} %get-tuple-element.572, ...), kind=kOutput, calls=%fused_computation.20.clone.1 | convolution fusion | flops 620756992 | bytes 71575040 | tf_op jit(solution)/shard_map/while/body/eval_jaxpr/dot_general | solution.py:97
  975.8 22.2 %fusion.168 = (f32[128]{0:T(128)S(1)}, f32[128]{0:T(128)S(1)}, f32[128]{0:T(128)S(1)}) fusion(f32[64,1024,128]{2,1,0:T(8,128)} %get-tuple-element.504, f32[128]{0:T(128)S(1)} %copy-done.67, f32[128]{0:T(128)S(1)} %get-tuple-element.569, f32[64,1024]{1,0:T(8,128)S(1)} %get-tuple-element.503, f32[128]{0:T(128)S(1)} %get-tuple-element.570, ...), kind=kLoop, calls=%fused_computation.18.clone.1 | loop fusion | flops 100662912 | bytes 67374592 | tf_op jit(solution)/shard_map/while/body/eval_jaxpr/transpose(jvp())/reduce_sum | solution.py:47
  1018.5 26.9 %fusion.167 = (f32[64,1024,128]{2,1,0:T(8,128)}, f32[64,1024,128]{2,1,0:T(8,128)}) fusion(f32[128]{0:T(128)S(1)} %get-tuple-element.502, f32[128]{0:T(128)S(1)} %get-tuple-element.570, f32[128]{0:T(128)S(1)} %get-tuple-element.569, f32[64,1024]{1,0:T(8,128)S(1)} %get-tuple-element.503, bf16[128,32]{0,1:T(8,128)(2,1)S(1)} %get-tuple-element.572, ...), kind=kOutput, calls=%fused_computation.20.clone.1 | convolution fusion | flops 620756992 | bytes 71575040 | tf_op jit(solution)/shard_map/while/body/eval_jaxpr/dot_general | solution.py:97
  1045.4 22.2 %fusion.168 = (f32[128]{0:T(128)S(1)}, f32[128]{0:T(128)S(1)}, f32[128]{0:T(128)S(1)}) fusion(f32[64,1024,128]{2,1,0:T(8,128)} %get-tuple-element.504, f32[128]{0:T(128)S(1)} %copy-done.67, f32[128]{0:T(128)S(1)} %get-tuple-element.569, f32[64,1024]{1,0:T(8,128)S(1)} %get-tuple-element.503, f32[128]{0:T(128)S(1)} %get-tuple-element.570, ...), kind=kLoop, calls=%fused_computation.18.clone.1 | loop fusion | flops 100662912 | bytes 67374592 | tf_op jit(solution)/shard_map/while/body/eval_jaxpr/transpose(jvp())/reduce_sum | solution.py:47
  1088.5 26.9 %fusion.167 = (f32[64,1024,128]{2,1,0:T(8,128)}, f32[64,1024,128]{2,1,0:T(8,128)}) fusion(f32[128]{0:T(128)S(1)} %get-tuple-element.502, f32[128]{0:T(128)S(1)} %get-tuple-element.570, f32[128]{0:T(128)S(1)} %get-tuple-element.569, f32[64,1024]{1,0:T(8,128)S(1)} %get-tuple-element.503, bf16[128,32]{0,1:T(8,128)(2,1)S(1)} %get-tuple-element.572, ...), kind=kOutput, calls=%fused_computation.20.clone.1 | convolution fusion | flops 620756992 | bytes 71575040 | tf_op jit(solution)/shard_map/while/body/eval_jaxpr/dot_general | solution.py:97
  1115.5 22.3 %fusion.168 = (f32[128]{0:T(128)S(1)}, f32[128]{0:T(128)S(1)}, f32[128]{0:T(128)S(1)}) fusion(f32[64,1024,128]{2,1,0:T(8,128)} %get-tuple-element.504, f32[128]{0:T(128)S(1)} %copy-done.67, f32[128]{0:T(128)S(1)} %get-tuple-element.569, f32[64,1024]{1,0:T(8,128)S(1)} %get-tuple-element.503, f32[128]{0:T(128)S(1)} %get-tuple-element.570, ...), kind=kLoop, calls=%fused_computation.18.clone.1 | loop fusion | flops 100662912 | bytes 67374592 | tf_op jit(solution)/shard_map/while/body/eval_jaxpr/transpose(jvp())/reduce_sum | solution.py:47
  1158.2 26.9 %fusion.167 = (f32[64,1024,128]{2,1,0:T(8,128)}, f32[64,1024,128]{2,1,0:T(8,128)}) fusion(f32[128]{0:T(128)S(1)} %get-tuple-element.502, f32[128]{0:T(128)S(1)} %get-tuple-element.570, f32[128]{0:T(128)S(1)} %get-tuple-element.569, f32[64,1024]{1,0:T(8,128)S(1)} %get-tuple-element.503, bf16[128,32]{0,1:T(8,128)(2,1)S(1)} %get-tuple-element.572, ...), kind=kOutput, calls=%fused_computation.20.clone.1 | convolution fusion | flops 620756992 | bytes 71575040 | tf_op jit(solution)/shard_map/while/body/eval_jaxpr/dot_general | solution.py:97
  1185.1 21.2 %fusion.168 = (f32[128]{0:T(128)S(1)}, f32[128]{0:T(128)S(1)}, f32[128]{0:T(128)S(1)}) fusion(f32[64,1024,128]{2,1,0:T(8,128)} %get-tuple-element.504, f32[128]{0:T(128)S(1)} %copy-done.67, f32[128]{0:T(128)S(1)} %get-tuple-element.569, f32[64,1024]{1,0:T(8,128)S(1)} %get-tuple-element.503, f32[128]{0:T(128)S(1)} %get-tuple-element.570, ...), kind=kLoop, calls=%fused_computation.18.clone.1 | loop fusion | flops 100662912 | bytes 67374592 | tf_op jit(solution)/shard_map/while/body/eval_jaxpr/transpose(jvp())/reduce_sum | solution.py:47
  1226.8 26.9 %fusion.167 = (f32[64,1024,128]{2,1,0:T(8,128)}, f32[64,1024,128]{2,1,0:T(8,128)}) fusion(f32[128]{0:T(128)S(1)} %get-tuple-element.502, f32[128]{0:T(128)S(1)} %get-tuple-element.570, f32[128]{0:T(128)S(1)} %get-tuple-element.569, f32[64,1024]{1,0:T(8,128)S(1)} %get-tuple-element.503, bf16[128,32]{0,1:T(8,128)(2,1)S(1)} %get-tuple-element.572, ...), kind=kOutput, calls=%fused_computation.20.clone.1 | convolution fusion | flops 620756992 | bytes 71575040 | tf_op jit(solution)/shard_map/while/body/eval_jaxpr/dot_general | solution.py:97
  1253.7 21.2 %fusion.168 = (f32[128]{0:T(128)S(1)}, f32[128]{0:T(128)S(1)}, f32[128]{0:T(128)S(1)}) fusion(f32[64,1024,128]{2,1,0:T(8,128)} %get-tuple-element.504, f32[128]{0:T(128)S(1)} %copy-done.67, f32[128]{0:T(128)S(1)} %get-tuple-element.569, f32[64,1024]{1,0:T(8,128)S(1)} %get-tuple-element.503, f32[128]{0:T(128)S(1)} %get-tuple-element.570, ...), kind=kLoop, calls=%fused_computation.18.clone.1 | loop fusion | flops 100662912 | bytes 67374592 | tf_op jit(solution)/shard_map/while/body/eval_jaxpr/transpose(jvp())/reduce_sum | solution.py:47
  1290.6 40.1 %all-reduce.18 = (f32[768]{0:T(1024)S(1)}, f32[768]{0:T(1024)S(1)}, f32[3072]{0:T(1024)S(1)}, f32[768]{0:T(1024)S(1)}, f32[768]{0:T(1024)S(1)}, /*index=5*/f32[7...) all-reduce(f32[768]{0:T(1024)S(1)} %copy-done.64, ...), channel_id=8, replica_groups=mesh['rows'=16,'mp'=2] {'rows','mp'}, use_global_device_ids=true, to_apply=%region_26.27.clone | all-reduce | flops 12800 | bytes 102400
  (590 shorter events, 461.3 us)
Async XLA Ops:
  7.2 56.2 %copy-start = (bf16[48,768]{1,0:T(8,128)(2,1)S(1)}, bf16[48,768]{1,0:T(8,128)(2,1)}, u32[]{:S(2)}) copy-start(bf16[48,768]{1,0:T(8,128)(2,1)} %param.26) | copy-start | bytes 221188
  7.2 62.9 %all-gather.11.cloned.1.call-start = ((), (), s32[]{:S(2)}) async-start(), calls=%async_computation.8 | async-start | bytes 1216512 | tf_op jit(solution)/shard_map/all_gather | solution.py:281
  7.9 113.7 %all-gather.7.cloned.1.call-start = ((), (), s32[]{:S(2)}) async-start(), calls=%async_computation.6 | async-start | bytes 1216512 | tf_op jit(solution)/shard_map/all_gather | solution.py:282
  8.7 313.5 %all-gather.9.cloned.1.call-start = ((), (), s32[]{:S(2)}) async-start(), calls=%async_computation.7 | async-start | bytes 1216512 | tf_op jit(solution)/shard_map/all_gather | solution.py:280
  9.4 437.3 %all-gather.13.cloned.1.call-start = ((), (), s32[]{:S(2)}) async-start(), calls=%async_computation.9 | async-start | bytes 1216512 | tf_op jit(solution)/shard_map/all_gather | solution.py:283
  10.0 439.6 %all-gather.15.cloned.1.call-start = ((), (), s32[]{:S(2)}) async-start(), calls=%async_computation.10 | async-start | bytes 4866048 | tf_op jit(solution)/shard_map/all_gather | solution.py:284
  10.6 459.0 %all-gather.17.cloned.1.call-start = ((), (), s32[]{:S(2)}) async-start(), calls=%async_computation.11 | async-start | bytes 4866048 | tf_op jit(solution)/shard_map/all_gather | solution.py:285
  11.4 58.6 %collective-permute-start.2 = (bf16[3,512]{1,0:T(4,128)(2,1)S(1)}, bf16[3,512]{1,0:T(4,128)(2,1)S(1)}, u32[]{:S(2)}, u32[]{:S(2)}) collective-permute-start(bf16[3,512]{1,0:T(4,128)(2,1)S(1)} %get-tuple-element.363), channel_id=1, source_target_pairs={{0,1},{1,0},{2,3},{3,2},{4,5},{5,4},{6,7},{7,6},{8,9},{9,8},{10,11... | collective-permute-start | bytes 9224 | tf_op jit(solution)/shard_map/ppermute | solution.py:19
  12.1 1323.9 %reduce-scatter.13.cloned.1.call-start = ((), (), s32[]{:S(2)}) async-start(), calls=%async_computation.15 | async-start | bytes 2433024 | tf_op jit(solution)/shard_map/reduce_scatter | solution.py:399
  14.6 50.8 %copy-start.59 = (pred[512]{0:T(512)(128)(4,1)}, pred[512]{0:T(512)(128)(4,1)S(1)}, u32[]{:S(2)}) copy-start(pred[512]{0:T(512)(128)(4,1)S(1)} %get-tuple-element.282) | copy-start | bytes 1540
  63.3 61.3 %copy-start.41 = (bf16[4352]{0:T(1024)(128)(2,1)}, bf16[4352]{0:T(1024)(128)(2,1)S(1)}, u32[]{:S(2)}) copy-start(bf16[4352]{0:T(1024)(128)(2,1)S(1)} %get-tuple-element.333) | copy-start | bytes 26116
  67.3 57.6 %copy-start.9 = (bf16[512,768]{1,0:T(8,128)(2,1)}, bf16[512,768]{1,0:T(8,128)(2,1)S(1)}, u32[]{:S(2)}) copy-start(bf16[512,768]{1,0:T(8,128)(2,1)S(1)} %add_convert_fusion.3) | copy-start | bytes 2359300
  73.0 251.7 %collective-permute-start.1 = (bf16[512,768]{1,0:T(8,128)(2,1)}, bf16[512,768]{1,0:T(8,128)(2,1)}, u32[]{:S(2)}, u32[]{:S(2)}) collective-permute-start(bf16[512,768]{1,0:T(8,128)(2,1)} %convolution_convert_fusion.2), channel_id=1, source_target_pairs={{0,1},{1,0},{2,3},{3,2},{4,5},{5,4},{6,7},{7,6},{8,9},{9,8},{10,11... | collective-permute-start | bytes 2359304 | tf_op jit(solution)/shard_map/ppermute | solution.py:19
  124.6 204.9 %collective-permute-start = (bf16[512,768]{1,0:T(8,128)(2,1)}, bf16[512,768]{1,0:T(8,128)(2,1)}, u32[]{:S(2)}, u32[]{:S(2)}) collective-permute-start(bf16[512,768]{1,0:T(8,128)(2,1)} %add_convert_fusion.2), channel_id=1, source_target_pairs={{0,1},{1,0},{2,3},{3,2},{4,5},{5,4},{6,7},{7,6},{8,9},{9,8},{10,11... | collective-permute-start | bytes 2359304 | tf_op jit(solution)/shard_map/ppermute | solution.py:19
  329.5 71.8 %copy-start.5 = (bf16[1024,768]{0,1:T(8,128)(2,1)}, bf16[1024,768]{0,1:T(8,128)(2,1)S(1)}, u32[]{:S(2)}) copy-start(bf16[1024,768]{0,1:T(8,128)(2,1)S(1)} %copy.74) | copy-start | bytes 4718596
  492.7 843.3 %reduce-scatter.7.cloned.1.call-start = ((), (), s32[]{:S(2)}) async-start(), calls=%async_computation.12 | async-start | bytes 2433024 | tf_op jit(solution)/shard_map/reduce_scatter | solution.py:396
  529.8 43.5 %copy-start.6 = (bf16[1024,768]{0,1:T(8,128)(2,1)S(1)}, bf16[1024,768]{0,1:T(8,128)(2,1)}, u32[]{:S(2)}) copy-start(bf16[1024,768]{0,1:T(8,128)(2,1)} %copy-done.5) | copy-start | bytes 4718596
  589.9 746.2 %reduce-scatter.11.cloned.1.call-start = ((), (), s32[]{:S(2)}) async-start(), calls=%async_computation.14 | async-start | bytes 2433024 | tf_op jit(solution)/shard_map/reduce_scatter | solution.py:398
  612.8 2.4 collective-permute-start.4
  618.3 717.7 %reduce-scatter.9.cloned.1.call-start = ((), (), s32[]{:S(2)}) async-start(), calls=%async_computation.13 | async-start | bytes 2433024 | tf_op jit(solution)/shard_map/reduce_scatter | solution.py:397
  632.1 2.4 collective-permute-start.3
  637.8 698.2 %reduce-scatter.15.cloned.1.call-start = ((), (), s32[]{:S(2)}) async-start(), calls=%async_computation.16 | async-start | bytes 9732096 | tf_op jit(solution)/shard_map/reduce_scatter | solution.py:400
  645.2 690.8 %reduce-scatter.17.cloned.1.call-start = ((), (), s32[]{:S(2)}) async-start(), calls=%async_computation.17 | async-start | bytes 9732096 | tf_op jit(solution)/shard_map/reduce_scatter | solution.py:401
  655.8 64.2 %copy-start.28 = (f32[3,1024]{1,0:T(4,128)S(1)}, f32[3,1024]{1,0:T(4,128)}, u32[]{:S(2)}) copy-start(f32[3,1024]{1,0:T(4,128)} %copy-done.27) | copy-start | bytes 36868
  655.8 64.2 %copy-start.46 = (f32[128]{0:T(128)S(1)}, f32[128]{0:T(128)}, u32[]{:S(2)}) copy-start(f32[128]{0:T(128)} %copy-done.45) | copy-start | bytes 1540
  655.8 64.2 %copy-start.48 = (f32[128]{0:T(128)S(1)}, f32[128]{0:T(128)}, u32[]{:S(2)}) copy-start(f32[128]{0:T(128)} %copy-done.47) | copy-start | bytes 1540
  655.8 64.2 %copy-start.74 = (bf16[128,32]{0,1:T(8,128)(2,1)S(1)}, bf16[128,32]{0,1:T(8,128)(2,1)}, u32[]{:S(2)}) copy-start(bf16[128,32]{0,1:T(8,128)(2,1)} %copy-done.73) | copy-start | bytes 24580
  720.1 556.5 %copy-start.21 = (bf16[32,24,512]{2,1,0:T(8,128)(2,1)S(1)}, bf16[32,24,512]{2,1,0:T(8,128)(2,1)}, u32[]{:S(2)}) copy-start(bf16[32,24,512]{2,1,0:T(8,128)(2,1)} %copy-done.20) | copy-start | bytes 2359300
  720.1 558.6 %copy-start.19 = (f32[512,768]{1,0:T(8,128)S(1)}, f32[512,768]{1,0:T(8,128)}, u32[]{:S(2)}) copy-start(f32[512,768]{1,0:T(8,128)} %copy-done.17) | copy-start | bytes 4718596
  720.1 558.6 %copy-start.62 = (pred[512]{0:T(512)(128)(4,1)S(1)}, pred[512]{0:T(512)(128)(4,1)}, u32[]{:S(2)}) copy-start(pred[512]{0:T(512)(128)(4,1)} %copy-done.59) | copy-start | bytes 1540
  720.1 558.6 %copy-start.77 = (f32[768]{0:T(1024)S(1)}, f32[768]{0:T(1024)}, u32[]{:S(2)}) copy-start(f32[768]{0:T(1024)} %convert_element_type.204) | copy-start | bytes 9220
  1286.7 49.4 %copy-start.1 = (bf16[48,768]{1,0:T(8,128)(2,1)S(1)}, bf16[48,768]{1,0:T(8,128)(2,1)}, u32[]{:S(2)}) copy-start(bf16[48,768]{1,0:T(8,128)(2,1)} %param.26) | copy-start | bytes 221188
  (135 other events, 1708.6 us)
Sparse Core Ops, SparseCore 0:
  10.9 54.6 all-gather.10
  68.5 53.0 all-gather.6
  124.6 53.1 all-gather.8
  180.5 53.1 all-gather.12
  236.4 63.8 all-gather.14
  303.1 62.6 all-gather.16
  492.9 96.7 reduce-scatter.12
  596.3 98.6 reduce-scatter.6
  700.9 97.9 reduce-scatter.10
  805.5 98.0 reduce-scatter.8
  910.0 134.2 reduce-scatter.14
  1051.7 134.4 reduce-scatter.16
where the time goes:
time: 1350 us; the launch traced here: 1340 us
  matrix products  686 us (51%)
  other arithmetic  337 us (25%)
  local copies, waits for them, and re-layouts  165 us (12%)
  blocking collectives  80.5 us (6%)
  waiting for transfers between devices  53.7 us (4%)
  between operations  15.9 us (1%)
    dot_general x8, matrix products, one_piece(): lax.dot_general(flat, mix, (((1,), (1,)), ((), ())), preferred_element_ty...  215 us
    reduce_sum x8, other arithmetic, densities(): scaled = (dist[:, :, None] - means) / widths  175 us
    dot_general x8, matrix products, one_piece(): jnp.dot(phi.reshape(step * span, KERN), mix, preferred_element_type=jnp.f...  131 us
    convert_element_type x2, other arithmetic, attention_back(): grad_scores = (probs * (grad_probs - delta)).astype(jnp.bfloat16)  108 us
    unnamed x2, blocking collectives  80.5 us
    dot_general x8, matrix products, one_piece(): lax.dot_general(phi_low, flat, (((0,), (0,)), ((), ())), preferred_elemen...  77.8 us
    dot_general x1, matrix products, middle(): jnp.einsum('ihd,jhd->hij', query_heads, key_heads, preferred_element_type...  65.9 us
    dynamic_update_slice x8, local copies, waits for them, and re-layouts, pair_bias(): bias = lax.map(one_piece, pieces)  64.4 us
  transfers between devices with their start and end apart: 17, of which 3 were waited for; matrix products, arithmetic and copies ran while one was open for 86% of the time, Pallas kernels for 0%

commit v1 on v0

v1 whole, which is shorter than its diff:
```python
import functools
import math

import jax
import jax.numpy as jnp
import numpy as np
from jax import lax
from jax.experimental import pallas as pl
from jax.experimental.pallas import tpu as pltpu
from jax.sharding import PartitionSpec as P

HEADS = 32
KERN = 128
HEAD = 24
GH = 8
NG = HEADS // GH
GW = GH * HEAD
MIB = 2**20
CENTRE = 6.0
STORED = 1
AXES = ("rows", "mp")
f32 = jnp.float32
bf16 = jnp.bfloat16


def dot(left, right):
    return jnp.dot(left, right, preferred_element_type=f32)


def whole(shape):
    return pl.BlockSpec(shape, lambda i: (0,) * len(shape))


def high_low(value):
    high = value.astype(bf16)
    return high, (value - high.astype(f32)).astype(bf16)


def distances(near_ref, all_ref):
    total = None
    for c in range(3):
        diff = near_ref[:, c : c + 1] - all_ref[c : c + 1, :]
        total = diff * diff if total is None else total + diff * diff
    return jnp.sqrt(total) * 0.25


def bias_kernel(
    pairs_step, near_ref, all_ref, code_near_ref, code_all_ref, means_ref, curve_ref, mix_ref,
    bias_ref, phi_ref, dist_ref, mask_ref,
):
    dist_ref[...] = distances(near_ref, all_ref)
    mask_ref[...] = jnp.where(code_near_ref[:, 0:1] == code_all_ref[0:1, :], 0.0, -1e30)
    rows, span = dist_ref.shape

    def body(step, carry):
        for q in range(pairs_step):
            pair = step * pairs_step + q
            drow = [dist_ref[pl.ds(pair * 2 + e, 1), :] for e in range(2)]
            mrow = [mask_ref[pl.ds(pair * 2 + e, 1), :] for e in range(2)]
            for lane in range(0, span, 256):
                tall = []
                for e in range(2):
                    wide = []
                    for low in (lane, lane + 128):
                        u = drow[e][:, low : low + 128] - means_ref[...]
                        wide.append(jnp.exp2((u * curve_ref[...]) * u).astype(bf16))
                    wide = jnp.concatenate(wide, axis=1)
                    if e < STORED:
                        phi_ref[pair * STORED + e, :, lane : lane + 256] = wide
                    tall.append(wide)
                out = dot(mix_ref[...], jnp.concatenate(tall, axis=0)).reshape(NG, 2, GH, 256)
                out = jnp.concatenate(
                    [out[:, e : e + 1] + mrow[e][:, lane : lane + 256].reshape(1, 1, 1, 256) for e in range(2)],
                    axis=1,
                )
                bias_ref[:, pl.ds(pl.multiple_of(pair * 16, 16), 16), lane : lane + 256] = out.reshape(
                    NG, 16, 256
                ).astype(bf16)
        return carry

    lax.fori_loop(0, rows // 2 // pairs_step, body, 0)


def lane_wide(values):
    return jnp.broadcast_to(values[:, None], (KERN, 128))


def pair_bias(near, coord_all, code_near, code_all, means, curve, mix_low, tile=32, pairs_step=8):
    rows, span = near.shape[0], coord_all.shape[1]
    m4 = mix_low.T.reshape(NG, GH, KERN)
    zero = jnp.zeros_like(m4)
    left = jnp.stack([jnp.concatenate([m4, zero], -1), jnp.concatenate([zero, m4], -1)], axis=1)
    left = left.reshape(2 * HEADS, 2 * KERN)
    return pl.pallas_call(
        functools.partial(bias_kernel, pairs_step),
        grid=(rows // tile,),
        in_specs=[
            pl.BlockSpec((tile, 3), lambda i: (i, 0)),
            whole((3, span)),
            pl.BlockSpec((tile, 1), lambda i: (i, 0)),
            whole((1, span)),
            whole((KERN, 128)),
            whole((KERN, 128)),
            whole((2 * HEADS, 2 * KERN)),
        ],
        out_specs=[
            pl.BlockSpec((NG, tile * GH, span), lambda i: (0, i, 0)),
            pl.BlockSpec((tile * STORED // 2, KERN, span), lambda i: (i, 0, 0)),
        ],
        out_shape=[
            jax.ShapeDtypeStruct((NG, rows * GH, span), bf16),
            jax.ShapeDtypeStruct((rows * STORED // 2, KERN, span), bf16),
        ],
        scratch_shapes=[pltpu.VMEM((tile, span), f32), pltpu.VMEM((tile, span), f32)],
        compiler_params=pltpu.CompilerParams(vmem_limit_bytes=50 * MIB),
        cost_estimate=pl.CostEstimate(
            flops=2 * rows * span * KERN * HEADS * 8,
            bytes_accessed=rows * span * (KERN * STORED + 2 * HEADS),
            transcendentals=rows * span * KERN,
        ),
        name="bias",
    )(near, coord_all, code_near, code_all, lane_wide(means), lane_wide(curve), left)


def repeat_tables(tile):
    row = np.arange(tile * GH)
    repeat = row[:, None] // GH == np.arange(tile)[None, :]
    own = row[:, None] % GH == np.arange(GW)[None, :] // HEAD
    return repeat, own


def attend_kernel(
    tiles, q_ref, kt_ref, v_ref, b_ref, rep_ref, rept_ref, own_ref, scaled_ref,
    e_ref, mixed_ref, inv_ref, qa, qb, sa, sb, ea, oa, ob, wa, wb,
):
    query, scores, outs, wides = (qa, qb), (sa, sb), (oa, ob), (wa, wb)
    rows, span = sa.shape
    held = rows // GH
    units = NG * tiles
    parts, chunk, ahead = 4, 8, 3
    step, some = span // parts, rows // parts
    pid = pl.program_id(0)

    def place(unit):
        unit = jnp.clip(unit, 0, units - 1)
        group = unit // tiles
        return group, pl.ds(pl.multiple_of((unit - group * tiles) * held, held), held)

    def spread(unit, par):
        g, i = place(unit)
        query[par][...] = (dot(rep_ref[...], q_ref[g, i, :]) * scaled_ref[...]).astype(bf16)

    def score(unit, par, part):
        g, _ = place(unit)
        cols = slice(part * step, (part + 1) * step)
        scores[par][:, cols] = dot(query[par][...], kt_ref[g, :, cols])

    def soften(par, part):
        chunks = range(part * some, (part + 1) * some, chunk)
        held_x = {}
        for n in range(len(chunks) + ahead):
            if n < len(chunks):
                here = slice(chunks[n], chunks[n] + chunk)
                x = scores[par][here, :] + b_ref[par, here, :].astype(f32)
                held_x[n] = x, jnp.max(x, axis=1, keepdims=True)
            if n >= ahead:
                here = slice(chunks[n - ahead], chunks[n - ahead] + chunk)
                x, top = held_x.pop(n - ahead)
                e = jnp.exp2(x - top).astype(bf16)
                e_ref[par, here, :] = e
                if par == 1:
                    ea[here, :] = e

    def mix(unit, par, part):
        g, _ = place(unit)
        here = slice(part * some, (part + 1) * some)
        source = e_ref.at[0] if par == 0 else ea
        outs[par][here, :] = dot(source[here, :], v_ref[g])

    def scale(par, part):
        here = slice(part * some, (part + 1) * some)
        out = outs[par][here, :]
        inv = 1.0 / out[:, GW : GW + 1]
        own = own_ref[here, :]
        wides[par][here, :] = jnp.concatenate(
            [*high_low(out[:, :GW] * inv * own), *high_low(inv * own)], axis=1
        )

    def gather(unit, par):
        g, i = place(unit)
        out = dot(rept_ref[...], wides[par][...])
        mixed_ref[g, i, :] = out[:, :GW] + out[:, GW : 2 * GW]
        inv_ref[g, i, :] = out[:, 2 * GW : 3 * GW] + out[:, 3 * GW :]

    @pl.when(pid == 0)
    def _():
        spread(0, 0)
        for part in range(parts):
            score(0, 0, part)
        spread(1, 1)
        ea[...] = jnp.ones_like(ea)
        for ref in (oa, ob):
            ref[...] = jnp.ones_like(ref)
        for ref in (wa, wb):
            ref[...] = jnp.zeros_like(ref)

    for par in range(2):
        unit = pid * 2 + par
        gather(unit - 3, 1 - par)
        for part in range(parts):
            score(unit + 1, 1 - par, part)
            scale(par, part)
            mix(unit - 1, 1 - par, part)
            soften(par, part)
        spread(unit + 2, par)

    @pl.when(pid == units // 2 - 1)
    def _():
        for part in range(parts):
            scale(0, part)
            mix(units - 1, 1, part)
        gather(units - 3, 1)
        gather(units - 2, 0)
        for part in range(parts):
            scale(1, part)
        gather(units - 1, 1)


def attend(q4, kt4, vx4, bias, tile=64):
    rows, span = q4.shape[1], kt4.shape[2]
    tiles = rows // tile
    repeat, own = repeat_tables(tile)
    deep = tile * GH
    bias = bias.reshape(NG * tiles, deep, span)
    big = pl.BlockSpec((2, deep, span), lambda i: (i, 0, 0))
    scale = HEAD**-0.5 * math.log2(math.e)
    e, mixed, inv = pl.pallas_call(
        functools.partial(attend_kernel, tiles),
        grid=(NG * tiles // 2,),
        in_specs=[
            whole((NG, rows, GW)),
            whole((NG, GW, span)),
            whole(vx4.shape),
            big,
            whole((deep, tile)),
            whole((tile, deep)),
            whole((deep, GW)),
            whole((deep, GW)),
        ],
        out_specs=[big, whole((NG, rows, GW)), whole((NG, rows, GW))],
        out_shape=[
            jax.ShapeDtypeStruct((NG * tiles, deep, span), bf16),
            jax.ShapeDtypeStruct((NG, rows, GW), f32),
            jax.ShapeDtypeStruct((NG, rows, GW), f32),
        ],
        scratch_shapes=[pltpu.VMEM((deep, GW), bf16)] * 2
        + [pltpu.VMEM((deep, span), f32)] * 2
        + [pltpu.VMEM((deep, span), bf16)]
        + [pltpu.VMEM((deep, 256), f32)] * 2
        + [pltpu.VMEM((deep, 4 * GW), bf16)] * 2,
        compiler_params=pltpu.CompilerParams(vmem_limit_bytes=50 * MIB),
        cost_estimate=pl.CostEstimate(
            flops=4 * rows * GH * NG * span * GW,
            bytes_accessed=rows * span * HEADS * 4,
            transcendentals=rows * span * HEADS,
        ),
        name="attend",
    )(
        q4, kt4, vx4, bias, jnp.asarray(repeat, bf16), jnp.asarray(repeat.T, bf16),
        jnp.asarray(own, f32), jnp.asarray(own * scale, f32),
    )
    return e.reshape(NG, rows * GH, span), mixed, inv


def attend_back_kernel(
    chunk, q_ref, gs_ref, mx_ref, k_ref, vt_ref, e_ref, rep_ref, rept_ref, own_ref, ownt_ref,
    ds_ref, dq_ref, dkt_ref, dvt_ref, s0, s1,
):
    groups_here = q_ref.shape[0]
    rows, span = s0.shape
    scores = (s0, s1)
    parts = 4
    step = span // parts
    count = rows // chunk
    scale = HEAD**-0.5

    @pl.when(pl.program_id(0) == 0)
    def _():
        dkt_ref[...] = jnp.zeros_like(dkt_ref)
        dvt_ref[...] = jnp.zeros_like(dvt_ref)

    def begin(g):
        grad = dot(rep_ref[...], gs_ref[g]) * own_ref[...]
        high, low = high_low(gs_ref[g].astype(f32) * mx_ref[g])
        wide = dot(rep_ref[...], jnp.concatenate([high, low], axis=1))
        delta = jnp.sum((wide[:, :GW] + wide[:, GW:]) * own_ref[...], axis=1, keepdims=True)
        return grad.astype(bf16), delta

    def across(value):
        wide = lax.dot_general(value, rept_ref[...], (((0,), (0,)), ((), ())), preferred_element_type=f32)
        return (wide * ownt_ref[...]).astype(bf16)

    def grad_probs(g, grad, part):
        cols = slice(part * step, (part + 1) * step)
        scores[g % 2][:, cols] = dot(grad, vt_ref[g, :, cols])

    def soft_back(g, delta, part):
        for c in range(part * count // parts, (part + 1) * count // parts):
            here = slice(c * chunk, (c + 1) * chunk)
            ds_ref[g, here, :] = (
                e_ref[g, here, :].astype(f32) * (scores[g % 2][here, :] - delta[here])
            ).astype(bf16)

    def finish(g, query_t, grad_t, part):
        cols = slice(part * step, (part + 1) * step)
        dvt_ref[g, :, cols] += dot(grad_t, e_ref[g, :, cols])
        dkt_ref[g, :, cols] += dot(query_t, ds_ref[g, :, cols])

    def query_grad(g):
        out = dot(ds_ref[g], k_ref[g])
        dq_ref[g] = (dot(rept_ref[...], (out * own_ref[...]).astype(bf16)) * scale).astype(bf16)

    begun = [begin(g) for g in range(groups_here)]
    for part in range(parts):
        grad_probs(0, begun[0][0], part)
    turned = None
    for g in range(groups_here):
        for part in range(parts):
            if g + 1 < groups_here:
                grad_probs(g + 1, begun[g + 1][0], part)
            if g > 0:
                if part == 0:
                    turned = across(q_ref[g - 1]), across(gs_ref[g - 1])
                finish(g - 1, *turned, part)
                if part == 2:
                    query_grad(g - 1)
            soft_back(g, begun[g][1], part)
    turned = across(q_ref[groups_here - 1]), across(gs_ref[groups_here - 1])
    for part in range(parts):
        finish(groups_here - 1, *turned, part)
    query_grad(groups_here - 1)


def attend_back(q4, gs4, mx4, k4, vt4, e, first, groups, tile=64, chunk=8):
    rows, span = q4.shape[1], k4.shape[1]
    repeat, own = repeat_tables(tile)
    block = first // groups
    big = pl.BlockSpec((groups, tile * GH, span), lambda i: (block, i, 0))
    small = pl.BlockSpec((groups, tile, GW), lambda i: (block, i, 0))
    held = lambda shape: pl.BlockSpec(shape, lambda i: (block, 0, 0))
    return pl.pallas_call(
        functools.partial(attend_back_kernel, chunk),
        grid=(rows // tile,),
        in_specs=[
            small,
            small,
            small,
            held((groups, span, GW)),
            held((groups, GW, span)),
            big,
            whole((tile * GH, tile)),
            whole((tile, tile * GH)),
            whole((tile * GH, GW)),
            whole((GW, tile * GH)),
        ],
        out_specs=[
            pl.BlockSpec((groups, tile * GH, span), lambda i: (0, i, 0)),
            pl.BlockSpec((groups, tile, GW), lambda i: (0, i, 0)),
            whole((groups, GW, span)),
            whole((groups, GW, span)),
        ],
        out_shape=[
            jax.ShapeDtypeStruct((groups, rows * GH, span), bf16),
            jax.ShapeDtypeStruct((groups, rows, GW), bf16),
            jax.ShapeDtypeStruct((groups, GW, span), f32),
            jax.ShapeDtypeStruct((groups, GW, span), f32),
        ],
        scratch_shapes=[pltpu.VMEM((tile * GH, span), f32)] * 2,
        compiler_params=pltpu.CompilerParams(vmem_limit_bytes=58 * MIB),
        cost_estimate=pl.CostEstimate(
            flops=8 * rows * GH * groups * span * GW,
            bytes_accessed=rows * span * HEADS * 4,
            transcendentals=0,
        ),
        name="attend_back",
    )(
        q4, gs4, mx4, k4, vt4, e, jnp.asarray(repeat, bf16), jnp.asarray(repeat.T, bf16),
        jnp.asarray(own, f32), jnp.asarray(own.T, f32),
    )


def bias_back_kernel(
    pairs_step, near_ref, all_ref, means_ref, curve_ref, ds0_ref, ds1_ref, phi_ref, out_ref, dist_ref
):
    dist_ref[...] = distances(near_ref, all_ref)
    rows, span = dist_ref.shape

    @pl.when(pl.program_id(0) == 0)
    def _():
        out_ref[...] = jnp.zeros_like(out_ref)

    def body(step, acc):
        for q in range(pairs_step):
            pair = step * pairs_step + q
            here = pl.ds(pl.multiple_of(pair * 16, 16), 16)
            both = jnp.concatenate([ds0_ref[:, here, :].astype(f32), ds1_ref[:, here, :].astype(f32)], axis=0)
            for e in range(2):
                d = dist_ref[pl.ds(pair * 2 + e, 1), :]
                if e < STORED:
                    phi = phi_ref[pair * STORED + e]
                else:
                    wide = []
                    for lane in range(0, span, 128):
                        u = d[:, lane : lane + 128] - means_ref[...]
                        wide.append(jnp.exp2((u * curve_ref[...]) * u).astype(bf16))
                    phi = jnp.concatenate(wide, axis=1)
                d = d - CENTRE
                s = both[:, e * GH : (e + 1) * GH, :].reshape(HEADS, span)
                one = s * d
                x = jnp.concatenate([s.astype(bf16), *high_low(one), *high_low(one * d)], axis=0)
                acc = acc + lax.dot_general(
                    x, phi, (((1,), (1,)), ((), ())), preferred_element_type=f32
                )
        return acc

    out_ref[...] += lax.fori_loop(0, rows // 2 // pairs_step, body, jnp.zeros(out_ref.shape, f32))


def bias_back(near, coord_all, means, curve, ds, phi, first, count, tile=32, pairs_step=4):
    span = coord_all.shape[1]
    rows = count * tile
    return pl.pallas_call(
        functools.partial(bias_back_kernel, pairs_step),
        grid=(count,),
        in_specs=[
            pl.BlockSpec((tile, 3), lambda i: (i + first, 0)),
            whole((3, span)),
            whole((KERN, 128)),
            whole((KERN, 128)),
            pl.BlockSpec((NG // 2, tile * GH, span), lambda i: (0, i + first, 0)),
            pl.BlockSpec((NG // 2, tile * GH, span), lambda i: (0, i + first, 0)),
            pl.BlockSpec((tile * STORED // 2, KERN, span), lambda i: (i + first, 0, 0)),
        ],
        out_specs=whole((5 * HEADS, KERN)),
        out_shape=jax.ShapeDtypeStruct((5 * HEADS, KERN), f32),
        scratch_shapes=[pltpu.VMEM((tile, span), f32)],
        compiler_params=pltpu.CompilerParams(vmem_limit_bytes=50 * MIB),
        cost_estimate=pl.CostEstimate(
            flops=4 * rows * span * KERN * 5 * HEADS,
            bytes_accessed=rows * span * (KERN * STORED + 2 * HEADS),
            transcendentals=0,
        ),
        name="bias_back",
    )(near, coord_all, lane_wide(means), lane_wide(curve), *ds, phi)


def row_items(global_rows, group_rows, lengths, groups):
    count = lengths.shape[0]
    order = jnp.arange(count, dtype=jnp.int32)
    earlier = (groups[:, None] == groups[None, :]) & (order[None, :] < order[:, None])
    starts = jnp.sum(jnp.where(earlier, lengths[None, :], 0), axis=1)
    group_of = global_rows // group_rows
    place = global_rows - group_of * group_rows
    hits = (
        (groups[None, :] == group_of[:, None])
        & (place[:, None] >= starts[None, :])
        & (place[:, None] < starts[None, :] + lengths[None, :])
    )
    item = jnp.sum(jnp.where(hits, order[None, :], 0), axis=1)
    return (item, jnp.any(hits, axis=1))


def layer_norm(value, gain, shift):
    centre = value - jnp.mean(value, axis=-1, keepdims=True)
    spread = jnp.mean(centre * centre, axis=-1, keepdims=True)
    return centre * lax.rsqrt(spread + 1e-05) * gain + shift


def col_sum(value):
    return jnp.sum(value.astype(f32), axis=0)


def left_dot(left, right):
    return lax.dot_general(left, right, (((0,), (0,)), ((), ())), preferred_element_type=f32)


def right_dot(left, right):
    return lax.dot_general(left, right, (((1,), (1,)), ((), ())), preferred_element_type=f32)


AXES = ("rows", "mp")


def swap_sides(block):
    return lax.ppermute(block, "mp", [(0, 1), (1, 0)])


def halves(pair, axis, mine):
    kept, come = pair

    def half(index, dtype):
        part = lax.dynamic_index_in_dim(kept, index, axis, keepdims=False)
        if come is not None:
            part = part + lax.dynamic_index_in_dim(come, index, axis, keepdims=False).astype(f32)
        return part.astype(dtype)

    return half(1 - mine, bf16), half(mine, f32)


class Shards:
    def __init__(self, partial, first_bits):
        chips = lax.axis_size("rows")
        bits = chips.bit_length() - 1
        stack, rows, columns = partial.shape
        kept = partial.reshape(stack, *[2] * bits, 2, rows // (2 * chips), columns)
        self.pair = (kept, None)
        self.left = list(range(bits))[::-1]
        self.order = [None] + [b for b in first_bits if b < bits] + [b for b in range(bits) if b not in first_bits]

    def exchange(self):
        if not self.order:
            return
        bit = self.order.pop(0)
        if bit is None:
            send, kept = halves(self.pair, 1 + len(self.left), lax.axis_index("mp"))
            self.pair = kept, swap_sides(send)
            return
        chips = lax.axis_size("rows")
        send, kept = halves(self.pair, 1 + self.left.index(bit), (lax.axis_index("rows") >> bit) & 1)
        self.pair = kept, lax.ppermute(send, "rows", [(n, n ^ (1 << bit)) for n in range(chips)])
        self.left.remove(bit)

    def total(self):
        while self.order:
            self.exchange()
        return self.pair[0] + self.pair[1].astype(f32)


def tied(shards, value, begin):
    which = 0 if begin else 1
    flat = [s.pair[which] for s in shards]
    flat, value = lax.optimization_barrier((flat, value))
    for s, new in zip(shards, flat):
        s.pair = (new, s.pair[1]) if begin else (s.pair[0], new)
    return value


def by_group(value):
    return value.reshape(-1, NG, GW).transpose(1, 0, 2)


def from_group(value):
    return value.transpose(1, 0, 2).reshape(-1, NG * GW)


def by_group_t(value):
    return value.T.reshape(NG, GW, -1)


def everyone(visit):
    side_count = lax.axis_size("mp")
    count = lax.axis_size("rows") * side_count
    me = lax.axis_index("rows") * side_count + lax.axis_index("mp")

    def body(step, carry):
        visit(step, lax.rem(me + step, count), lax.rem(me + count - step, count))
        return carry

    lax.fori_loop(1, count, body, 0)
    return me


def address(device):
    side_count = lax.axis_size("mp")
    return (device // side_count, lax.rem(device, side_count))


def meet_everyone():
    barrier = pltpu.get_barrier_semaphore()

    def greet(step, target, source):
        pl.semaphore_signal(
            barrier, inc=1, device_id=address(target), device_id_type=pl.DeviceIdType.MESH
        )

    everyone(greet)
    pl.semaphore_wait(barrier, lax.axis_size("rows") * lax.axis_size("mp") - 1)


def remote(source_ref, target_ref, send_sem, recv_sem, device):
    return pltpu.make_async_remote_copy(
        src_ref=source_ref,
        dst_ref=target_ref,
        send_sem=send_sem,
        recv_sem=recv_sem,
        device_id=address(device),
        device_id_type=pl.DeviceIdType.MESH,
    )


def gather_kernel(x_ref, out_ref, send_sem, recv_sem):
    count = out_ref.shape[0]
    side_count = lax.axis_size("mp")
    me = lax.axis_index("rows") * side_count + lax.axis_index("mp")
    meet_everyone()
    out_ref[me] = x_ref[...]

    def send(step, target, source):
        remote(x_ref, out_ref.at[me], send_sem.at[step], recv_sem.at[step], target).start()

    def wait(step, target, source):
        remote(x_ref, out_ref.at[source], send_sem.at[step], recv_sem.at[step], target).wait()

    everyone(send)
    everyone(wait)


def gather_small(block, count):
    return pl.pallas_call(
        gather_kernel,
        out_shape=jax.ShapeDtypeStruct((count, *block.shape), block.dtype),
        in_specs=[pl.BlockSpec(memory_space=pltpu.VMEM)],
        out_specs=pl.BlockSpec(memory_space=pltpu.VMEM),
        scratch_shapes=[pltpu.SemaphoreType.DMA((count,)), pltpu.SemaphoreType.DMA((count,))],
        compiler_params=pltpu.CompilerParams(
            collective_id=1, has_side_effects=True, vmem_limit_bytes=16 * MIB
        ),
        name="gather_small",
    )(block)


def sum_kernel(x_ref, out_ref, come_ref, send_sem, recv_sem):
    side_count = lax.axis_size("mp")
    me = lax.axis_index("rows") * side_count + lax.axis_index("mp")
    meet_everyone()

    def send(step, target, source):
        remote(x_ref.at[target], come_ref.at[step], send_sem.at[step], recv_sem.at[step], target).start()

    def wait(step, target, source):
        remote(x_ref.at[target], come_ref.at[step], send_sem.at[step], recv_sem.at[step], target).wait()

    everyone(send)
    come_ref[0] = x_ref[me]
    everyone(wait)
    out_ref[...] = jnp.sum(come_ref[...].astype(f32), axis=0)


def sum_small(blocks):
    count = blocks.shape[0]
    return pl.pallas_call(
        sum_kernel,
        out_shape=jax.ShapeDtypeStruct(blocks.shape[1:], f32),
        in_specs=[pl.BlockSpec(memory_space=pltpu.VMEM)],
        out_specs=pl.BlockSpec(memory_space=pltpu.VMEM),
        scratch_shapes=[
            pltpu.VMEM(blocks.shape, blocks.dtype),
            pltpu.SemaphoreType.DMA((count,)),
            pltpu.SemaphoreType.DMA((count,)),
        ],
        compiler_params=pltpu.CompilerParams(
            collective_id=2, has_side_effects=True, vmem_limit_bytes=16 * MIB
        ),
        name="sum_small",
    )(blocks)


def lay_tables(share, count):
    lane = np.arange(share * count)
    place = lane[None, :] % share == np.arange(share)[:, None]
    mark = lane[None, :] // share == np.arange(count)[:, None]
    return jnp.asarray(place, bf16), jnp.asarray(mark, f32)


def joined(shares):
    count, vectors, share = shares.shape
    place, mark = lay_tables(share, count)
    wide = dot(shares.reshape(count * vectors, share), place).reshape(count, vectors, count * share)
    return jnp.sum(wide * mark[:, None, :], axis=0)


def cut(vectors, share):
    number, size = vectors.shape
    place, mark = lay_tables(share, size // share)
    wide = (vectors[None] * mark[:, None, :]).astype(bf16)
    out = lax.dot_general(wide, place, (((2,), (1,)), ((), ())), preferred_element_type=f32)
    return out.astype(bf16)


def on_device(
    atoms,
    time_embedding,
    coordinates,
    item_lengths,
    item_group,
    query_weight,
    key_weight,
    value_weight,
    out_weight,
    up_weight,
    down_weight,
    value_bias,
    out_bias,
    up_bias,
    down_bias,
    first_gain,
    first_shift,
    second_gain,
    second_shift,
    kernel_params,
    cotangent,
):
    rows_here = atoms.shape[0]
    pair_size = lax.axis_size("mp")
    side = lax.axis_index("mp")
    pair_index = lax.axis_index("rows")
    group_rows = rows_here * pair_size
    counter = jnp.arange(rows_here, dtype=jnp.int32)
    near_rows = (pair_index * pair_size + side) * rows_here + counter
    far_rows = (pair_index * pair_size + 1 - side) * rows_here + counter
    items = item_lengths.shape[0]
    near_item, near_valid = row_items(near_rows, group_rows, item_lengths, item_group)
    far_item, far_valid = row_items(far_rows, group_rows, item_lengths, item_group)
    near_code = jnp.where(near_valid, near_item, items + near_rows)
    far_code = jnp.where(far_valid, far_item, items + far_rows)
    all_code = jnp.concatenate([near_code, far_code])
    picks = (
        (near_item[:, None] == jnp.arange(items, dtype=jnp.int32)[None, :]) & near_valid[:, None]
    ).astype(bf16)
    embed = jnp.dot(picks, time_embedding, preferred_element_type=f32)

    count = lax.axis_size("rows") * pair_size
    share, hidden = up_weight.shape
    width = query_weight.shape[1]
    blocks = hidden // width
    small = (value_bias, out_bias, down_bias, first_gain, first_shift, second_gain, second_shift)
    table_share = kernel_params.shape[0]
    block = jnp.concatenate(
        [
            jnp.pad(jnp.stack(small), ((0, 0), (0, 256 - share))),
            jnp.pad(up_bias.reshape(1, -1), ((0, 0), (0, 256 - blocks * share))),
            jnp.pad(kernel_params[None], ((0, 7), (0, 256 - table_share))),
        ]
    )
    gathered = gather_small(block, count)
    value_b, out_b, down_b, gain_one, shift_one, gain_two, shift_two = joined(gathered[:, :7, :share])
    up_b = joined(gathered[:, 7:8, : blocks * share])[0]
    table = joined(gathered[:, 8:9, :table_share])[0]
    wide = lax.all_gather(
        jnp.concatenate([query_weight, key_weight, value_weight, out_weight], axis=1), AXES, axis=0, tiled=True
    )
    stack = jnp.concatenate([up_weight[:, n * width : (n + 1) * width] for n in range(blocks)] + [down_weight], axis=0)
    stack = lax.all_gather(stack, AXES, axis=0, tiled=False)
    up_w = jnp.concatenate(
        [stack[:, n * share : (n + 1) * share].reshape(width, width) for n in range(blocks)], axis=1
    )
    down_w = stack[:, blocks * share :].reshape(hidden, width)

    means, widths, mix = table[:KERN], table[KERN : 2 * KERN], table[2 * KERN :].reshape(KERN, HEADS)
    norm = 1.0 / (widths * math.sqrt(2.0 * math.pi))
    curve = (-0.5 * math.log2(math.e)) / (widths * widths)
    mix_low = (mix * norm[:, None] * math.log2(math.e)).astype(bf16)
    coord_low = coordinates.astype(bf16)
    coord_all = jnp.concatenate([coord_low, swap_sides(coord_low)], axis=1).astype(f32)
    near = coordinates.astype(f32).T
    bias, phi = pair_bias(near, coord_all, near_code[:, None], all_code[None], means, curve, mix_low)

    bias, wide = lax.optimization_barrier((bias, wide))
    query_w, key_w, value_w, out_w = [wide[:, n * width : (n + 1) * width] for n in range(4)]
    h_zero = atoms.astype(f32) + embed
    normed, pull_one = jax.vjp(layer_norm, h_zero, gain_one, shift_one)
    normed_low = normed.astype(bf16)
    query = jnp.dot(normed_low, query_w, preferred_element_type=f32).astype(bf16)
    keys = jnp.dot(normed_low, key_w, preferred_element_type=f32).astype(bf16)
    values = (jnp.dot(normed_low, value_w, preferred_element_type=f32) + value_b).astype(bf16)
    keys_all = jnp.concatenate([keys, swap_sides(keys)], axis=0)
    values_all = jnp.concatenate([values, swap_sides(values)], axis=0)
    q4, k4, v4 = by_group(query), by_group(keys_all), by_group(values_all)
    kt4, vt4 = by_group_t(keys_all), by_group_t(values_all)
    ones = jnp.ones((NG, group_rows, 1), bf16)
    vx4 = jnp.concatenate([v4, ones, jnp.zeros((NG, group_rows, 256 - GW - 1), bf16)], axis=2)
    expo, mixed4, inverse4 = attend(q4, kt4, vx4, bias)
    mixed = from_group(mixed4.astype(bf16))

    h_one = h_zero + jnp.dot(mixed, out_w, preferred_element_type=f32) + out_b
    second, pull_two = jax.vjp(layer_norm, h_one, gain_two, shift_two)
    second_low = second.astype(bf16)
    up_pre = jnp.dot(second_low, up_w, preferred_element_type=f32) + up_b
    below = 0.5 + 0.5 * lax.erf(up_pre * (2.0**-0.5))
    act_low = (up_pre * below).astype(bf16)
    slope = (below + up_pre * jnp.exp(-0.5 * up_pre * up_pre) * (2.0 * math.pi) ** -0.5).astype(bf16)
    h_two = h_one + jnp.dot(act_low, down_w, preferred_element_type=f32) + down_b
    layer_out = jnp.where(near_valid[:, None], h_two, 0.0).astype(bf16)

    grad_two = jnp.where(near_valid[:, None], cotangent.astype(f32), 0.0)
    grad_ffn = grad_two.astype(bf16)
    down_bias_grad = col_sum(grad_ffn)
    down_shards = Shards(left_dot(act_low, grad_ffn)[None], (0, 1))
    down_shards.exchange()
    grad_up = (right_dot(grad_ffn, down_w) * slope.astype(f32)).astype(bf16)
    up_bias_grad = col_sum(grad_up)
    up_shards = Shards(left_dot(second_low, grad_up)[None], (1, 0))
    up_shards.exchange()
    grad_part, second_gain_grad, second_shift_grad = pull_two(right_dot(grad_up, up_w))
    grad_one = grad_two + grad_part
    grad_att = grad_one.astype(bf16)
    out_bias_grad = col_sum(grad_att)
    out_weight_grad = left_dot(mixed, grad_att)
    grad_mixed = right_dot(grad_att, out_w).astype(bf16)
    scaled4 = (by_group(grad_mixed).astype(f32) * inverse4).astype(bf16)
    down_shards.exchange()
    up_shards.exchange()

    half = NG // 2
    done = []
    for n in range(2):
        scaled4 = tied((down_shards, up_shards), scaled4, begin=True)
        done.append(attend_back(q4, scaled4, mixed4, k4, vt4, expo, n * half, half))
        if n == 0:
            scaled4 = tied((down_shards, up_shards), (scaled4, done[0]), begin=False)[0]
            down_shards.exchange()
            up_shards.exchange()
    scores_grad = [d[0] for d in done]
    dq4, dkt, dvt = [jnp.concatenate([d[m] for d in done], axis=0) for m in (1, 2, 3)]
    dq4, dkt, dvt = tied((down_shards, up_shards), (dq4, dkt, dvt), begin=False)
    down_shards.exchange()
    up_shards.exchange()

    grad_query = from_group(dq4)
    dkt = dkt.reshape(-1, group_rows) * (HEAD**-0.5)
    dvt = dvt.reshape(-1, group_rows)
    back_keys = swap_sides(dkt[:, rows_here:].astype(bf16)).astype(f32)
    back_values = swap_sides(dvt[:, rows_here:].astype(bf16)).astype(f32)
    grad_keys = (dkt[:, :rows_here] + back_keys).astype(bf16).T
    grad_values = (dvt[:, :rows_here] + back_values).astype(bf16).T
    value_bias_grad = col_sum(grad_values)
    square_shards = Shards(
        jnp.stack(
            [
                left_dot(normed_low, grad_query),
                left_dot(normed_low, grad_keys),
                left_dot(normed_low, grad_values),
                out_weight_grad,
            ]
        ),
        (0, 1),
    )
    square_shards.exchange()
    grad_normed = (
        right_dot(grad_query, query_w) + right_dot(grad_keys, key_w) + right_dot(grad_values, value_w)
    )
    grad_zero, first_gain_grad, first_shift_grad = pull_one(grad_normed)
    atoms_grad = grad_one + grad_zero

    tiles = rows_here // 32
    pieces = 4
    moments = 0.0
    square_shards.exchange()
    down_shards.exchange()
    up_shards.exchange()
    shards = (square_shards, down_shards, up_shards)
    for n in range(pieces):
        near = tied(shards, (near, atoms_grad), begin=True)[0]
        piece = bias_back(near, coord_all, means, curve, scores_grad, phi, n * tiles // pieces, tiles // pieces)
        piece = tied(shards, piece, begin=False)
        for s in shards:
            s.exchange()
        moments = moments + piece
    zeroth = moments[:HEADS].T * norm[:, None]
    first = (moments[HEADS : 2 * HEADS] + moments[2 * HEADS : 3 * HEADS]).T * norm[:, None]
    twice = (moments[3 * HEADS : 4 * HEADS] + moments[4 * HEADS :]).T * norm[:, None]
    m_zero, m_one, m_two = [jnp.sum(mix * r, axis=1) for r in (zeroth, first, twice)]
    offset = means - CENTRE
    mean_grad = (m_one - offset * m_zero) / widths**2
    width_grad = (m_two - 2.0 * offset * m_one + offset * offset * m_zero) / widths**3 - m_zero / widths
    table_grad = jnp.concatenate([mean_grad, width_grad, zeroth.reshape(-1)])

    cuts = jnp.concatenate(
        [
            jnp.pad(
                cut(
                    jnp.stack(
                        [
                            value_bias_grad,
                            out_bias_grad,
                            down_bias_grad,
                            first_gain_grad,
                            first_shift_grad,
                            second_gain_grad,
                            second_shift_grad,
                        ]
                    ),
                    share,
                ),
                ((0, 0), (0, 0), (0, 256 - share)),
            ),
            jnp.pad(cut(up_bias_grad[None], blocks * share), ((0, 0), (0, 0), (0, 256 - blocks * share))),
            jnp.pad(cut(table_grad[None], table_share), ((0, 0), (0, 7), (0, 256 - table_share))),
        ],
        axis=1,
    )
    sums = sum_small(cuts)
    square_sum = square_shards.total()
    return (
        layer_out,
        atoms_grad,
        square_sum[0],
        square_sum[1],
        square_sum[2],
        square_sum[3],
        up_shards.total()[0],
        down_shards.total()[0],
        sums[0, :share],
        sums[1, :share],
        sums[7, : blocks * share],
        sums[2, :share],
        sums[3, :share],
        sums[4, :share],
        sums[5, :share],
        sums[6, :share],
        sums[8, :table_share],
    )


def solution(mesh):
    row = P(AXES, None)
    vec = P(AXES)
    in_specs = (row, P(), P(None, AXES), P(), P(), *[row] * 6, *[vec] * 9, row)
    out_specs = (*[row] * 8, *[vec] * 9)
    return jax.shard_map(on_device, mesh=mesh, in_specs=in_specs, out_specs=out_specs, check_vma=False)
```

time: 1350 us -> 511 us (0.38)
  matrix products: 686 us -> 55.7 us
  Pallas kernels: 0 us -> 288 us
  other arithmetic: 337 us -> 60.4 us
  local copies, waits for them, and re-layouts: 165 us -> 61.9 us
  blocking collectives: 80.5 us -> 0 us
  waiting for transfers between devices: 53.7 us -> 5.15 us
    dot_general x37 -> x13, matrix products: 640 us -> 23 us  [the longest x1 5.47 us: on_device(): up_pre = jnp.dot(second_low, up_w, preferred_element_type=f32) + up_b]
    pallas_call x0 -> x10, Pallas kernels: none -> 288 us  [the longest x4 76 us: bias_back(): pl.pallas_call(functools.partial(bias_back_kernel, pairs_step), grid=(cou...]
    reduce_sum x28 -> x4, other arithmetic: 202 us -> 3.47 us  [the longest x3 3.44 us: col_sum(): return jnp.sum(value.astype(f32), axis=0)]
    convert_element_type x15 -> x14, other arithmetic: 112 us -> 16.7 us  [the longest x10 12.6 us: half(): return part.astype(dtype)]
    unnamed x2 -> x0, blocking collectives: 80.5 us -> none
    dynamic_update_slice x8 -> x0, local copies, waits for them, and re-layouts: 64.4 us -> none  [pair_bias(): bias = lax.map(one_piece, pieces)]
    all_gather x6 -> x2, waiting for transfers between devices: 46.5 us -> 0.02 us  [the longest x1 0.02 us: on_device(): stack = lax.all_gather(stack, AXES, axis=0, tiled=False)]
    dynamic_slice x16 -> x2, local copies, waits for them, and re-layouts: 43.4 us -> 5.76 us  [half(): part = lax.dynamic_index_in_dim(kept, index, axis, keepdims=False)]
  transfers between devices with their start and end apart: 17 -> 22, of which waited for: 3 -> 1; matrix products, arithmetic and copies ran while one was open for 86% -> 24% of each run, Pallas kernels for 0% -> 55%
where the time goes in v1:
time: 511 us; the launch traced here: 502 us
  Pallas kernels  288 us (56%)
  local copies, waits for them, and re-layouts  61.9 us (12%)
  other arithmetic  60.4 us (12%)
  matrix products  55.7 us (11%)
  between operations  16.1 us (3%)
  starting transfers between devices  14.8 us (3%)
  waiting for transfers between devices  5.15 us (1%)
    pallas_call x4, Pallas kernels, bias_back(): pl.pallas_call(functools.partial(bias_back_kernel, pairs_step), grid=(cou...  76 us
    pallas_call x2, Pallas kernels, attend_back(): pl.pallas_call(functools.partial(attend_back_kernel, chunk), grid=(rows /...  75.6 us
    pallas_call x1, Pallas kernels, pair_bias(): pl.pallas_call(functools.partial(bias_kernel, pairs_step), grid=(rows //...  61.5 us
    pallas_call x1, Pallas kernels, attend(): pl.pallas_call(functools.partial(attend_kernel, tiles), grid=(NG * tiles...  47.3 us
    dot_general x6, matrix products, right_dot(): lax.dot_general(left, right, (((1,), (1,)), ((), ())), preferred_element_...  20.9 us
    unnamed x170, local copies, waits for them, and re-layouts  14.3 us
    pallas_call x1, Pallas kernels, sum_small(): pl.pallas_call(sum_kernel, out_shape=jax.ShapeDtypeStruct(blocks.shape[1:...  13.9 us
    pallas_call x1, Pallas kernels, gather_small(): pl.pallas_call(gather_kernel, out_shape=jax.ShapeDtypeStruct((count, *blo...  13.8 us
  transfers between devices with their start and end apart: 22, of which 1 were waited for; matrix products, arithmetic and copies ran while one was open for 24% of the time, Pallas kernels for 55%

profile of v1, /device:TPU:11, one launch (start us, length us, event | category | flops | bytes accessed | tf_op | source)
XLA Modules:
  0.0 502.2 jit_solution(17008152437986215521)
XLA Ops:
  17.3 13.8 %gather_small.1 = bf16[32,16,256]{2,1,0:T(8,128)(2,1)S(1)} custom-call(bf16[16,256]{1,0:T(8,128)(2,1)S(1)} %fusion.82.x_ref), custom_call_target="tpu_custom_call" | custom-call | tf_op jit(solution)/shard_map/gather_small/pallas_call | solution.py:619
  36.4 61.5 %bias.1 = (bf16[4,4096,1024]{2,1,0:T(8,128)(2,1)}, bf16[256,128,1024]{2,1,0:T(8,128)(2,1)}) custom-call(f32[512,3]{1,0:T(8,128)S(1)} %bitcast.267, f32[3,1024]{1,0:T(4,128)S(1)} %maximum_convert_fusion.all_ref, s32[512,1]{1,0:T(8,128)S(1)} %add_select_fusion.code_near_ref, s32[1,1024]{1,0:T(1,128)S(1)} %bitcast.277, ...), custom_call_target="tpu_custom_call" | custom-call | flops 34359738368 | bytes 100663296 | tf_op jit(solution)/shard_map/bias/pallas_call | solution.py:94
  98.5 2.9 convolution_convert_fusion.1
  101.9 3.0 add_convert_fusion.1
  110.8 3.7 pad_maximum_fusion.4
  116.2 3.3 fusion.103
  122.1 3.7 copy.216
  125.9 3.6 maximum_maximum_fusion.v_ref
  129.5 47.3 %attend.1 = (bf16[32,512,1024]{2,1,0:T(8,128)(2,1)}, f32[4,512,192]{2,1,0:T(8,128)}, f32[4,512,192]{2,1,0:T(8,128)}) custom-call(bf16[4,512,192]{2,1,0:T(8,128)(2,1)S(1)} %bitcast.273, bf16[4,192,1024]{2,1,0:T(8,128)(2,1)S(1)} %bitcast.272, bf16[4,1024,256]{2,1,0:T(8,128)(2,1)} %maximum_maximum_fusion.v_ref, bf16[32,512,1024]{2,1,0:T(8,128)(2,1)} %bitcast.333, ...), custom_call_target="tpu_custom_call" | custom-call | flops 12884901888 | bytes 67108864 | tf_op jit(solution)/shard_map/attend/pallas_call | solution.py:237
  193.7 5.5 %multiply_convert_fusion.1 = (bf16[512,3072]{1,0:T(8,128)(2,1)S(1)}, f32[512,3072]{1,0:T(8,128)}) fusion(f32[3072]{0:T(1024)S(1)} %fusion.19, bf16[768,768]{1,0:T(8,128)(2,1)S(1)} %bitcast.312, bf16[768,768]{1,0:T(8,128)(2,1)S(1)} %bitcast.314, bf16[768,768]{1,0:T(8,128)(2,1)S(1)} %bitcast.316, bf16[768,768]{1,0:T(8,128)(2,1)S(1)} %bitcast.310, ...), kind=kOutput, calls=%fused_computation.9 | convolution fusion | flops 2446196736 | bytes 15751168 | tf_op jit(solution)/shard_map/dot_general | solution.py:788
  199.2 10.1 %convert_reduce_fusion = (f32[3072]{0:T(1024)S(1)}, bf16[512,3072]{1,0:T(8,128)(2,1)S(1)}) fusion(f32[512,3072]{1,0:T(8,128)} %get-tuple-element.226, f32[3072]{0:T(1024)S(1)} %fusion.19, bf16[3072,768]{1,0:T(8,128)(2,1)S(1)} %bitcast.295, bf16[512,768]{1,0:T(8,128)(2,1)S(1)} %copy-done.39, pred[512]{0:T(512)(128)(4,1)S(1)} %get-tuple-element.158), kind=kOutput, calls=%fused_computation.7 | convolution fusion | flops 2440688640 | bytes 14967296 | tf_op jit(solution)/shard_map/dot_general | solution.py:488
  209.3 2.9 fusion.105
  212.2 2.9 multiply_reduce_fusion
  225.7 3.3 fusion.15
  229.3 3.1 copy.222
  232.4 3.0 copy.223
  236.0 3.8 convolution_bitcast_fusion
  239.7 2.9 fusion.11.gs_ref
  242.7 3.0 constant_dynamic-slice_fusion.4
  246.6 3.5 select_convert_fusion
  250.1 3.4 fusion.10
  253.5 4.2 fusion.9
  260.3 37.6 %attend_back.2 = (bf16[2,4096,1024]{2,1,0:T(8,128)(2,1)}, bf16[2,512,192]{2,1,0:T(8,128)(2,1)}, f32[2,192,1024]{2,1,0:T(8,128)}, f32[2,192,1024]{2,1,0:T(8,128)}) custom-call(bf16[4,512,192]{2,1,0:T(8,128)(2,1)} %bitcast.274, bf16[4,512,192]{2,1,0:T(8,128)(2,1)} %fusion.11.gs_ref, f32[4,512,192]{2,1,0:T(8,128)} %get-tuple-element.81.mx_ref, ...), custom_call_target="tpu_custom_call" | custom-call | flops 12884901888 | bytes 67108864 | tf_op jit(solution)/shard_map/attend_back/pallas_call | solution.py:351
  298.0 3.0 add_bitcast_fusion.2
  305.0 37.9 %attend_back.3 = (bf16[2,4096,1024]{2,1,0:T(8,128)(2,1)}, bf16[2,512,192]{2,1,0:T(8,128)(2,1)}, f32[2,192,1024]{2,1,0:T(8,128)}, f32[2,192,1024]{2,1,0:T(8,128)}) custom-call(bf16[4,512,192]{2,1,0:T(8,128)(2,1)} %bitcast.275, bf16[4,512,192]{2,1,0:T(8,128)(2,1)} %fusion.11.gs_ref, f32[4,512,192]{2,1,0:T(8,128)} %get-tuple-element.81.mx_ref, ...), custom_call_target="tpu_custom_call" | custom-call | flops 12884901888 | bytes 67108864 | tf_op jit(solution)/shard_map/attend_back/pallas_call | solution.py:351
  345.2 3.8 pad_maximum_fusion.2
  388.4 19.0 %bias_back.4 = f32[160,128]{1,0:T(8,128)S(1)} custom-call(f32[512,3]{1,0:T(8,128)S(1)} %bitcast.268, f32[3,1024]{1,0:T(4,128)S(1)} %copy-done.8, f32[128,128]{1,0:T(8,128)S(1)} %copy-done.3, f32[128,128]{1,0:T(8,128)S(1)} %copy-done.5, bf16[2,4096,1024]{2,1,0:T(8,128)(2,1)} %get-tuple-element.86.ds0_ref, bf16[2,4096,1024]{2,1,0:T(8,128)(2,1)} %get-tuple-element.107.ds1_ref, ...), custom_call_target="tpu_custom_call" | custom-call | flops 10737418240 | bytes 25165824 | tf_op jit(solution)/shard_map/bias_back/pallas_call | solution.py:432
  407.5 5.0 %collective-permute-done.14 = bf16[4,2,2,2,24,768]{5,4,3,2,1,0:T(8,128)(2,1)S(1)} collective-permute-done((bf16[4,2,2,2,24,768]{5,4,3,2,1,0:T(8,128)(2,1)S(1)}, bf16[4,2,2,2,24,768]{5,4,3,2,1,0:T(8,128)(2,1)S(1)}, u32[]{:S(2)}, u32[]{:S(2)}) %collective-permute-start.14) | collective-permute-done | bytes 1179680 | tf_op jit(solution)/shard_map/ppermute | solution.py:530
  414.8 19.0 %bias_back.5 = f32[160,128]{1,0:T(8,128)S(1)} custom-call(f32[512,3]{1,0:T(8,128)S(1)} %bitcast.269, f32[3,1024]{1,0:T(4,128)S(1)} %copy-done.8, f32[128,128]{1,0:T(8,128)S(1)} %copy-done.3, f32[128,128]{1,0:T(8,128)S(1)} %copy-done.5, bf16[2,4096,1024]{2,1,0:T(8,128)(2,1)} %get-tuple-element.86.ds0_ref, bf16[2,4096,1024]{2,1,0:T(8,128)(2,1)} %get-tuple-element.107.ds1_ref, ...), custom_call_target="tpu_custom_call" | custom-call | flops 10737418240 | bytes 25165824 | tf_op jit(solution)/shard_map/bias_back/pallas_call | solution.py:432
  434.0 19.0 %bias_back.6 = f32[160,128]{1,0:T(8,128)S(1)} custom-call(f32[512,3]{1,0:T(8,128)S(1)} %bitcast.270, f32[3,1024]{1,0:T(4,128)S(1)} %copy-done.8, f32[128,128]{1,0:T(8,128)S(1)} %copy-done.3, f32[128,128]{1,0:T(8,128)S(1)} %copy-done.5, bf16[2,4096,1024]{2,1,0:T(8,128)(2,1)} %get-tuple-element.86.ds0_ref, bf16[2,4096,1024]{2,1,0:T(8,128)(2,1)} %get-tuple-element.107.ds1_ref, ...), custom_call_target="tpu_custom_call" | custom-call | flops 10737418240 | bytes 25165824 | tf_op jit(solution)/shard_map/bias_back/pallas_call | solution.py:432
  454.6 19.0 %bias_back.7 = f32[160,128]{1,0:T(8,128)S(1)} custom-call(f32[512,3]{1,0:T(8,128)S(1)} %bitcast.271, f32[3,1024]{1,0:T(4,128)S(1)} %copy-done.8, f32[128,128]{1,0:T(8,128)S(1)} %copy-done.3, f32[128,128]{1,0:T(8,128)S(1)} %copy-done.5, bf16[2,4096,1024]{2,1,0:T(8,128)(2,1)} %get-tuple-element.86.ds0_ref, bf16[2,4096,1024]{2,1,0:T(8,128)(2,1)} %get-tuple-element.107.ds1_ref, ...), custom_call_target="tpu_custom_call" | custom-call | flops 10737418240 | bytes 25165824 | tf_op jit(solution)/shard_map/bias_back/pallas_call | solution.py:432
  475.3 13.9 %sum_small.1 = f32[16,256]{1,0:T(8,128)S(1)} custom-call(bf16[32,16,256]{2,1,0:T(8,128)(2,1)S(1)} %fusion.56.x_ref), custom_call_target="tpu_custom_call" | custom-call | tf_op jit(solution)/shard_map/sum_small/pallas_call | solution.py:651
  (350 shorter events, 114.4 us)
Async XLA Ops:
  7.2 25.8 %copy-start = (bf16[48,768]{1,0:T(8,128)(2,1)S(1)}, bf16[48,768]{1,0:T(8,128)(2,1)}, u32[]{:S(2)}) copy-start(bf16[48,768]{1,0:T(8,128)(2,1)} %param.46) | copy-start | bytes 221188
  7.2 24.6 %copy-start.43 = (f32[32,4352]{1,0:T(8,128)S(1)}, f32[32,4352]{1,0:T(8,128)}, u32[]{:S(2)}) copy-start(f32[32,4352]{1,0:T(8,128)} %constant.503.clone) | copy-start | bytes 1671172
  7.2 24.5 %copy-start.32 = (bf16[136,4352]{1,0:T(8,128)(2,1)S(1)}, bf16[136,4352]{1,0:T(8,128)(2,1)}, u32[]{:S(2)}) copy-start(bf16[136,4352]{1,0:T(8,128)(2,1)} %constant.502.clone) | copy-start | bytes 3551236
  7.3 91.3 %all-gather.4.cloned.1.call-start = ((), (), s32[]{:S(2)}) async-start(), calls=%async_computation | async-start | bytes 4866048 | tf_op jit(solution)/shard_map/all_gather | solution.py:749
  8.9 179.0 %all-gather.6.cloned.1.call-start = ((), (), s32[]{:S(2)}) async-start(), calls=%async_computation.1 | async-start | bytes 9732096 | tf_op jit(solution)/shard_map/all_gather | solution.py:753
  14.5 21.1 %collective-permute-start = (bf16[3,512]{1,0:T(4,128)(2,1)S(1)}, bf16[3,512]{1,0:T(4,128)(2,1)S(1)}, u32[]{:S(2)}, u32[]{:S(2)}) collective-permute-start(bf16[3,512]{1,0:T(4,128)(2,1)S(1)} %get-tuple-element.219), channel_id=1, source_target_pairs={{0,1},{1,0},{2,3},{3,2},{4,5},{5,4},{6,7},{7,6},{8,9},{9,8},{10,11... | collective-permute-start | bytes 9224 | tf_op jit(solution)/shard_map/ppermute | solution.py:495
  32.8 72.2 %copy-start.58 = (f32[768]{0:T(1024)}, f32[768]{0:T(1024)S(1)}, u32[]{:S(2)}) copy-start(f32[768]{0:T(1024)S(1)} %get-tuple-element.153) | copy-start | bytes 9220
  33.6 71.4 %copy-start.13 = (f32[512,768]{1,0:T(8,128)}, f32[512,768]{1,0:T(8,128)S(1)}, u32[]{:S(2)}) copy-start(f32[512,768]{1,0:T(8,128)S(1)} %get-tuple-element.222) | copy-start | bytes 4718596
  33.6 71.4 %copy-start.60 = (f32[512]{0:T(512)}, f32[512]{0:T(512)S(1)}, u32[]{:S(2)}) copy-start(f32[512]{0:T(512)S(1)} %broadcast_multiply_fusion.2) | copy-start | bytes 6148
  33.9 71.1 %copy-start.65 = (f32[512]{0:T(512)}, f32[512]{0:T(512)S(1)}, u32[]{:S(2)}) copy-start(f32[512]{0:T(512)S(1)} %fusion.91) | copy-start | bytes 6148
  34.4 73.5 %copy-start.24 = (bf16[512,768]{1,0:T(8,128)(2,1)}, bf16[512,768]{1,0:T(8,128)(2,1)S(1)}, u32[]{:S(2)}) copy-start(bf16[512,768]{1,0:T(8,128)(2,1)S(1)} %add_convert_fusion.2) | copy-start | bytes 2359300
  101.5 9.3 %collective-permute-start.1 = (bf16[512,768]{1,0:T(8,128)(2,1)}, bf16[512,768]{1,0:T(8,128)(2,1)}, u32[]{:S(2)}, u32[]{:S(2)}) collective-permute-start(bf16[512,768]{1,0:T(8,128)(2,1)} %convolution_convert_fusion.1), channel_id=1, source_target_pairs={{0,1},{1,0},{2,3},{3,2},{4,5},{5,4},{6,7},{7,6},{8,9},{9,8},{10,11... | collective-permute-start | bytes 2359304 | tf_op jit(solution)/shard_map/ppermute | solution.py:495
  104.9 11.3 %collective-permute-start.2 = (bf16[512,768]{1,0:T(8,128)(2,1)}, bf16[512,768]{1,0:T(8,128)(2,1)}, u32[]{:S(2)}, u32[]{:S(2)}) collective-permute-start(bf16[512,768]{1,0:T(8,128)(2,1)} %add_convert_fusion.1), channel_id=1, source_target_pairs={{0,1},{1,0},{2,3},{3,2},{4,5},{5,4},{6,7},{7,6},{8,9},{9,8},{10,11... | collective-permute-start | bytes 2359304 | tf_op jit(solution)/shard_map/ppermute | solution.py:495
  187.6 24.6 %copy-start.26 = (f32[512,768]{1,0:T(8,128)}, f32[512,768]{1,0:T(8,128)S(1)}, u32[]{:S(2)}) copy-start(f32[512,768]{1,0:T(8,128)S(1)} %get-tuple-element.224) | copy-start | bytes 4718596
  219.7 30.5 %collective-permute-start.3 = (bf16[1,2,2,2,2,96,768]{6,5,1,2,3,4,0:T(8,128)(2,1)}, bf16[1,2,2,2,2,96,768]{6,5,1,2,3,4,0:T(8,128)(2,1)}, u32[]{:S(2)}, u32[]{:S(2)}) collective-permute-start(bf16[1,2,2,2,2,96,768]{6,5,1,2,3,4,0:T(8,128)(2,1)} %fusion.6), channel_id=1, source_target_pairs={{0,1},{1,0},{2,3},{3,2},{4,5},{5,4},{6,7},{7,6},{8,9},{9,8},{10,11... | collective-permute-start | bytes 7077896 | tf_op jit(solution)/shard_map/ppermute | solution.py:495
  221.9 31.6 %collective-permute-start.4 = (bf16[1,2,2,2,2,24,3072]{6,5,1,2,4,3,0:T(8,128)(2,1)}, bf16[1,2,2,2,2,24,3072]{6,5,1,2,4,3,0:T(8,128)(2,1)}, u32[]{:S(2)}, u32[]{:S(2)}) collective-permute-start(bf16[1,2,2,2,2,24,3072]{6,5,1,2,4,3,0:T(8,128)(2,1)} %fusion.7), channel_id=1, source_target_pairs={{0,1},{1,0},{2,3},{3,2},{4,5},{5,4},{6,7},{7,6},{8,9},{9,8},{10,11... | collective-permute-start | bytes 7077896 | tf_op jit(solution)/shard_map/ppermute | solution.py:495
  257.7 40.3 %collective-permute-start.5 = (bf16[1,2,2,2,96,768]{5,4,1,2,3,0:T(8,128)(2,1)}, bf16[1,2,2,2,96,768]{5,4,1,2,3,0:T(8,128)(2,1)}, u32[]{:S(2)}, u32[]{:S(2)}) collective-permute-start(bf16[1,2,2,2,96,768]{5,4,1,2,3,0:T(8,128)(2,1)} %get-tuple-element.184), channel_id=1, source_target_pairs={{0,2},{2,0},{4,6},{6,4},{8,10},{10,8},{12,14},{14,12},{16,18},{18,... | collective-permute-start | bytes 3538952 | tf_op jit(solution)/shard_map/ppermute | solution.py:530
  257.7 40.3 %collective-permute-start.6 = (bf16[1,2,2,2,24,3072]{5,4,1,2,3,0:T(8,128)(2,1)}, bf16[1,2,2,2,24,3072]{5,4,1,2,3,0:T(8,128)(2,1)}, u32[]{:S(2)}, u32[]{:S(2)}) collective-permute-start(bf16[1,2,2,2,24,3072]{5,4,1,2,3,0:T(8,128)(2,1)} %get-tuple-element.182), channel_id=1, source_target_pairs={{0,4},{2,6},{4,0},{6,2},{8,12},{10,14},{12,8},{14,10},{16,20},{18,... | collective-permute-start | bytes 3538952 | tf_op jit(solution)/shard_map/ppermute | solution.py:530
  300.9 48.5 %collective-permute-start.7 = (bf16[1,2,2,96,768]{4,3,1,2,0:T(8,128)(2,1)}, bf16[1,2,2,96,768]{4,3,1,2,0:T(8,128)(2,1)S(1)}, u32[]{:S(2)}, u32[]{:S(2)}) collective-permute-start(bf16[1,2,2,96,768]{4,3,1,2,0:T(8,128)(2,1)} %get-tuple-element.179), channel_id=1, source_target_pairs={{0,4},{2,6},{4,0},{6,2},{8,12},{10,14},{12,8},{14,10},{16,20},{18,... | collective-permute-start | bytes 1769480 | tf_op jit(solution)/shard_map/ppermute | solution.py:530
  303.5 45.9 %collective-permute-start.8 = (bf16[1,2,2,24,3072]{4,3,1,2,0:T(8,128)(2,1)S(1)}, bf16[1,2,2,24,3072]{4,3,1,2,0:T(8,128)(2,1)S(1)}, u32[]{:S(2)}, u32[]{:S(2)}) collective-permute-start(bf16[1,2,2,24,3072]{4,3,1,2,0:T(8,128)(2,1)S(1)} %get-tuple-element.177), channel_id=1, source_target_pairs={{0,2},{2,0},{4,6},{6,4},{8,10},{10,8},{12,14},{14,12},{16,18},{18,... | collective-permute-start | bytes 1769480 | tf_op jit(solution)/shard_map/ppermute | solution.py:530
  305.0 37.9 %copy-start.56 = (bf16[2,512,192]{2,1,0:T(8,128)(2,1)S(1)}, bf16[2,512,192]{2,1,0:T(8,128)(2,1)}, u32[]{:S(2)}) copy-start(bf16[2,512,192]{2,1,0:T(8,128)(2,1)} %get-tuple-element.87) | copy-start | bytes 1179652
  352.0 12.2 %collective-permute-start.10 = (bf16[768,512]{1,0:T(8,128)(2,1)}, bf16[768,512]{1,0:T(8,128)(2,1)}, u32[]{:S(2)}, u32[]{:S(2)}) collective-permute-start(bf16[768,512]{1,0:T(8,128)(2,1)} %slice.273), channel_id=1, source_target_pairs={{0,1},{1,0},{2,3},{3,2},{4,5},{5,4},{6,7},{7,6},{8,9},{9,8},{10,11... | collective-permute-start | bytes 2359304 | tf_op jit(solution)/shard_map/ppermute | solution.py:495
  358.2 9.3 %collective-permute-start.9 = (bf16[768,512]{1,0:T(8,128)(2,1)S(1)}, bf16[768,512]{1,0:T(8,128)(2,1)S(1)}, u32[]{:S(2)}, u32[]{:S(2)}) collective-permute-start(bf16[768,512]{1,0:T(8,128)(2,1)S(1)} %slice.274), channel_id=1, source_target_pairs={{0,1},{1,0},{2,3},{3,2},{4,5},{5,4},{6,7},{7,6},{8,9},{9,8},{10,11... | collective-permute-start | bytes 2359304 | tf_op jit(solution)/shard_map/ppermute | solution.py:495
  359.5 13.6 %collective-permute-start.12 = (bf16[1,2,96,768]{3,2,1,0:T(8,128)(2,1)S(1)}, bf16[1,2,96,768]{3,2,1,0:T(8,128)(2,1)S(1)}, u32[]{:S(2)}, u32[]{:S(2)}) collective-permute-start(bf16[1,2,96,768]{3,2,1,0:T(8,128)(2,1)S(1)} %get-tuple-element.188), channel_id=1, source_target_pairs={{0,8},{2,10},{4,12},{6,14},{8,0},{10,2},{12,4},{14,6},{16,24},{18,... | collective-permute-start | bytes 884744 | tf_op jit(solution)/shard_map/ppermute | solution.py:530
  360.0 15.9 %collective-permute-start.13 = (bf16[1,2,24,3072]{3,2,1,0:T(8,128)(2,1)S(1)}, bf16[1,2,24,3072]{3,2,1,0:T(8,128)(2,1)S(1)}, u32[]{:S(2)}, u32[]{:S(2)}) collective-permute-start(bf16[1,2,24,3072]{3,2,1,0:T(8,128)(2,1)S(1)} %get-tuple-element.186), channel_id=1, source_target_pairs={{0,8},{2,10},{4,12},{6,14},{8,0},{10,2},{12,4},{14,6},{16,24},{18,... | collective-permute-start | bytes 884744 | tf_op jit(solution)/shard_map/ppermute | solution.py:530
  372.5 10.6 %collective-permute-start.11 = (bf16[4,2,2,2,2,24,768]{6,5,4,3,2,1,0:T(8,128)(2,1)}, bf16[4,2,2,2,2,24,768]{6,5,4,3,2,1,0:T(8,128)(2,1)}, u32[]{:S(2)}, u32[]{:S(2)}) collective-permute-start(bf16[4,2,2,2,2,24,768]{6,5,4,3,2,1,0:T(8,128)(2,1)} %fusion.5), channel_id=1, source_target_pairs={{0,1},{1,0},{2,3},{3,2},{4,5},{5,4},{6,7},{7,6},{8,9},{9,8},{10,11... | collective-permute-start | bytes 7077896 | tf_op jit(solution)/shard_map/ppermute | solution.py:495
  374.5 32.9 %collective-permute-start.15 = (bf16[1,96,768]{2,1,0:T(8,128)(2,1)}, bf16[1,96,768]{2,1,0:T(8,128)(2,1)}, u32[]{:S(2)}, u32[]{:S(2)}) collective-permute-start(bf16[1,96,768]{2,1,0:T(8,128)(2,1)} %get-tuple-element.198), channel_id=1, source_target_pairs={{0,16},{2,18},{4,20},{6,22},{8,24},{10,26},{12,28},{14,30},{16,0},... | collective-permute-start | bytes 442376 | tf_op jit(solution)/shard_map/ppermute | solution.py:530
  376.7 30.8 %collective-permute-start.16 = (bf16[1,24,3072]{2,1,0:T(8,128)(2,1)}, bf16[1,24,3072]{2,1,0:T(8,128)(2,1)}, u32[]{:S(2)}, u32[]{:S(2)}) collective-permute-start(bf16[1,24,3072]{2,1,0:T(8,128)(2,1)} %get-tuple-element.196), channel_id=1, source_target_pairs={{0,16},{2,18},{4,20},{6,22},{8,24},{10,26},{12,28},{14,30},{16,0},... | collective-permute-start | bytes 442376 | tf_op jit(solution)/shard_map/ppermute | solution.py:530
  385.4 27.1 %collective-permute-start.14 = (bf16[4,2,2,2,24,768]{5,4,3,2,1,0:T(8,128)(2,1)S(1)}, bf16[4,2,2,2,24,768]{5,4,3,2,1,0:T(8,128)(2,1)S(1)}, u32[]{:S(2)}, u32[]{:S(2)}) collective-permute-start(bf16[4,2,2,2,24,768]{5,4,3,2,1,0:T(8,128)(2,1)S(1)} %fusion.8), channel_id=1, source_target_pairs={{0,2},{2,0},{4,6},{6,4},{8,10},{10,8},{12,14},{14,12},{16,18},{18,... | collective-permute-start | bytes 3538952 | tf_op jit(solution)/shard_map/ppermute | solution.py:530
  412.9 20.9 %collective-permute-start.17 = (bf16[4,2,2,24,768]{4,3,2,1,0:T(8,128)(2,1)S(1)}, bf16[4,2,2,24,768]{4,3,2,1,0:T(8,128)(2,1)S(1)}, u32[]{:S(2)}, u32[]{:S(2)}) collective-permute-start(bf16[4,2,2,24,768]{4,3,2,1,0:T(8,128)(2,1)S(1)} %fusion.38), channel_id=1, source_target_pairs={{0,4},{2,6},{4,0},{6,2},{8,12},{10,14},{12,8},{14,10},{16,20},{18,... | collective-permute-start | bytes 1769480 | tf_op jit(solution)/shard_map/ppermute | solution.py:530
  434.0 19.1 %collective-permute-start.18 = (bf16[4,2,24,768]{3,2,1,0:T(8,128)(2,1)S(1)}, bf16[4,2,24,768]{3,2,1,0:T(8,128)(2,1)S(1)}, u32[]{:S(2)}, u32[]{:S(2)}) collective-permute-start(bf16[4,2,24,768]{3,2,1,0:T(8,128)(2,1)S(1)} %fusion.48), channel_id=1, source_target_pairs={{0,8},{2,10},{4,12},{6,14},{8,0},{10,2},{12,4},{14,6},{16,24},{18,... | collective-permute-start | bytes 884744 | tf_op jit(solution)/shard_map/ppermute | solution.py:530
  453.2 20.4 %collective-permute-start.19 = (bf16[4,24,768]{2,1,0:T(8,128)(2,1)S(1)}, bf16[4,24,768]{2,1,0:T(8,128)(2,1)S(1)}, u32[]{:S(2)}, u32[]{:S(2)}) collective-permute-start(bf16[4,24,768]{2,1,0:T(8,128)(2,1)S(1)} %fusion.62), channel_id=1, source_target_pairs={{0,16},{2,18},{4,20},{6,22},{8,24},{10,26},{12,28},{14,30},{16,0},... | collective-permute-start | bytes 442376 | tf_op jit(solution)/shard_map/ppermute | solution.py:530
  (73 other events, 434.3 us)
Sparse Core Ops, SparseCore 0:
  11.6 68.2 all-gather.3
  83.3 80.4 all-gather.5

commit v2 on v1

v2 whole, which is shorter than its diff:
```python
import functools
import math

import jax
import jax.numpy as jnp
import numpy as np
from jax import lax
from jax.experimental import pallas as pl
from jax.experimental.pallas import tpu as pltpu
from jax.sharding import PartitionSpec as P

HEADS = 32
KERN = 128
HEAD = 24
GH = 8
NG = HEADS // GH
GW = GH * HEAD
MIB = 2**20
CENTRE = 6.0
STORED = 1
AXES = ("rows", "mp")
f32 = jnp.float32
bf16 = jnp.bfloat16


def dot(left, right):
    return jnp.dot(left, right, preferred_element_type=f32)


def turned_dot(left, right):
    return lax.dot_general(left, right, (((1,), (1,)), ((), ())), preferred_element_type=f32)


def sum_dot(left, right):
    return lax.dot_general(left, right, (((0,), (0,)), ((), ())), preferred_element_type=f32)


def whole(shape):
    return pl.BlockSpec(shape, lambda i: (0,) * len(shape))


def after(kernel, inputs, tokens):
    def run(*refs):
        kernel(*refs[:inputs], *refs[inputs + len(tokens) :])

    return run, [pl.BlockSpec(memory_space=pl.ANY)] * len(tokens)


def high_low(value):
    high = value.astype(bf16)
    return high, (value - high.astype(f32)).astype(bf16)


def distances(near_ref, all_ref):
    total = None
    for c in range(3):
        diff = near_ref[:, c : c + 1] - all_ref[c : c + 1, :]
        total = diff * diff if total is None else total + diff * diff
    return jnp.sqrt(total) * 0.25


def bias_kernel(
    pairs_step, near_ref, all_ref, code_near_ref, code_all_ref, means_ref, curve_ref, mix_ref,
    bias_ref, phi_ref, dist_ref, mask_ref,
):
    dist_ref[...] = distances(near_ref, all_ref)
    mask_ref[...] = jnp.where(code_near_ref[:, 0:1] == code_all_ref[0:1, :], 0.0, -1e30)
    rows, span = dist_ref.shape

    def body(step, carry):
        for q in range(pairs_step):
            pair = step * pairs_step + q
            drow = [dist_ref[pl.ds(pair * 2 + e, 1), :] for e in range(2)]
            mrow = [mask_ref[pl.ds(pair * 2 + e, 1), :] for e in range(2)]
            for lane in range(0, span, 256):
                tall = []
                for e in range(2):
                    wide = []
                    for low in (lane, lane + 128):
                        u = drow[e][:, low : low + 128] - means_ref[...]
                        wide.append(jnp.exp2((u * curve_ref[...]) * u).astype(bf16))
                    wide = jnp.concatenate(wide, axis=1)
                    if e < STORED:
                        phi_ref[pair * STORED + e, :, lane : lane + 256] = wide
                    tall.append(wide)
                out = dot(mix_ref[...], jnp.concatenate(tall, axis=0)).reshape(NG, 2, GH, 256)
                out = jnp.concatenate(
                    [out[:, e : e + 1] + mrow[e][:, lane : lane + 256].reshape(1, 1, 1, 256) for e in range(2)],
                    axis=1,
                )
                bias_ref[:, pl.ds(pl.multiple_of(pair * 16, 16), 16), lane : lane + 256] = out.reshape(
                    NG, 16, 256
                ).astype(bf16)
        return carry

    lax.fori_loop(0, rows // 2 // pairs_step, body, 0)


def lane_wide(values):
    return jnp.broadcast_to(values[:, None], (KERN, 128))


def pair_bias(near, coord_all, code_near, code_all, means, curve, mix_low, tile=32, pairs_step=8):
    rows, span = near.shape[0], coord_all.shape[1]
    m4 = mix_low.T.reshape(NG, GH, KERN)
    zero = jnp.zeros_like(m4)
    left = jnp.stack([jnp.concatenate([m4, zero], -1), jnp.concatenate([zero, m4], -1)], axis=1)
    left = left.reshape(2 * HEADS, 2 * KERN)
    return pl.pallas_call(
        functools.partial(bias_kernel, pairs_step),
        grid=(rows // tile,),
        in_specs=[
            pl.BlockSpec((tile, 3), lambda i: (i, 0)),
            whole((3, span)),
            pl.BlockSpec((tile, 1), lambda i: (i, 0)),
            whole((1, span)),
            whole((KERN, 128)),
            whole((KERN, 128)),
            whole((2 * HEADS, 2 * KERN)),
        ],
        out_specs=[
            pl.BlockSpec((NG, tile * GH, span), lambda i: (0, i, 0)),
            pl.BlockSpec((tile * STORED // 2, KERN, span), lambda i: (i, 0, 0)),
        ],
        out_shape=[
            jax.ShapeDtypeStruct((NG, rows * GH, span), bf16),
            jax.ShapeDtypeStruct((rows * STORED // 2, KERN, span), bf16),
        ],
        scratch_shapes=[pltpu.VMEM((tile, span), f32), pltpu.VMEM((tile, span), f32)],
        compiler_params=pltpu.CompilerParams(vmem_limit_bytes=50 * MIB),
        cost_estimate=pl.CostEstimate(flops=rows * 140 * 10**6, bytes_accessed=MIB, transcendentals=0),
        name="bias",
    )(near, coord_all, code_near, code_all, lane_wide(means), lane_wide(curve), left)


def repeat_tables(tile):
    row = np.arange(tile * GH)
    repeat = row[:, None] // GH == np.arange(tile)[None, :]
    own = row[:, None] % GH == np.arange(GW)[None, :] // HEAD
    return repeat, own


def project_kernel(
    atoms_ref, code_ref, time_ref, gain_ref, shift_ref, bias_ref, wide_ref,
    h_ref, q_ref, k_ref, v_ref,
):
    width = atoms_ref.shape[1]
    items = lax.broadcasted_iota(jnp.int32, (1, time_ref.shape[0]), 1)
    picks = (code_ref[...] == items).astype(f32).astype(bf16)
    h_zero = atoms_ref[...].astype(f32) + dot(picks, time_ref[...])
    h_ref[...] = h_zero
    centre = h_zero - jnp.mean(h_zero, axis=1, keepdims=True)
    rate = lax.rsqrt(jnp.mean(centre * centre, axis=1, keepdims=True) + 1e-05)
    normed = (centre * rate * gain_ref[...] + shift_ref[...]).astype(bf16)
    tile = h_zero.shape[0]
    lane = lax.broadcasted_iota(jnp.int32, (tile, 256 - GW), 1)
    ones = jnp.where(lane == 0, 1.0, 0.0)
    for n, out_ref in ((1, k_ref), (2, v_ref), (0, q_ref)):
        out = dot(normed, wide_ref[:, n * width : (n + 1) * width])
        if n == 2:
            out = out + bias_ref[...]
        for g in range(NG):
            part = out[:, g * GW : (g + 1) * GW]
            if n == 2:
                part = jnp.concatenate([part, ones], axis=1)
            out_ref[g] = part.astype(bf16)


def project(atoms, code, time_embedding, gain, shift, value_bias, wide, tile=256):
    rows, width = atoms.shape
    return pl.pallas_call(
        project_kernel,
        grid=(rows // tile,),
        in_specs=[
            pl.BlockSpec((tile, width), lambda i: (i, 0)),
            pl.BlockSpec((tile, 1), lambda i: (i, 0)),
            whole(time_embedding.shape),
            *[whole((1, width))] * 3,
            whole((width, 3 * width)),
        ],
        out_specs=[
            pl.BlockSpec((tile, width), lambda i: (i, 0)),
            *[pl.BlockSpec((NG, tile, GW), lambda i: (0, i, 0))] * 2,
            pl.BlockSpec((NG, tile, 256), lambda i: (0, i, 0)),
        ],
        out_shape=[
            jax.ShapeDtypeStruct((rows, width), f32),
            *[jax.ShapeDtypeStruct((NG, rows, GW), bf16)] * 2,
            jax.ShapeDtypeStruct((NG, rows, 256), bf16),
        ],
        compiler_params=pltpu.CompilerParams(vmem_limit_bytes=40 * MIB),
        cost_estimate=pl.CostEstimate(flops=rows * 16 * 10**6, bytes_accessed=MIB, transcendentals=0),
        name="project",
    )(atoms, code, time_embedding, gain[None], shift[None], value_bias[None], wide)


def project_back_kernel(
    h_ref, grad_one_ref, q0_ref, q1_ref, k0_ref, k1_ref, v0_ref, v1_ref, kc0_ref, kc1_ref, vc0_ref, vc1_ref,
    gain_ref, shift_ref, wide_ref, out_grad_ref,
    atoms_grad_ref, grads_ref, sums_ref, normed_s, grad_s,
):
    rows, width = h_ref.shape
    for g in range(NG):
        q_ref, k_ref, v_ref, kc_ref, vc_ref = (
            (q0_ref, k0_ref, v0_ref, kc0_ref, vc0_ref) if g < NG // 2 else (q1_ref, k1_ref, v1_ref, kc1_ref, vc1_ref)
        )
        m = g % (NG // 2)
        cols = slice(g * GW, (g + 1) * GW)
        grad_s[0, :, cols] = q_ref[m]
        grad_s[1, :, cols] = (k_ref[m] + kc_ref[m].astype(f32)).T.astype(bf16)
        grad_s[2, :, cols] = (v_ref[m] + vc_ref[m].astype(f32)).T.astype(bf16)
    h_zero = h_ref[...]
    centre = h_zero - jnp.mean(h_zero, axis=1, keepdims=True)
    rate = lax.rsqrt(jnp.mean(centre * centre, axis=1, keepdims=True) + 1e-05)
    hat = centre * rate
    normed_s[...] = (hat * gain_ref[...] + shift_ref[...]).astype(bf16)
    grads_ref[3] = out_grad_ref[...]
    grad = None
    for n in range(3):
        grads_ref[n] = sum_dot(normed_s[...], grad_s[n]).astype(bf16)
        part = turned_dot(grad_s[n], wide_ref[:, n * width : (n + 1) * width])
        grad = part if grad is None else grad + part
    g = grad * gain_ref[...]
    atoms_grad_ref[...] = grad_one_ref[...] + rate * (
        g - jnp.mean(g, axis=1, keepdims=True) - hat * jnp.mean(g * hat, axis=1, keepdims=True)
    )
    sums_ref[...] = jnp.zeros_like(sums_ref)
    sums_ref[0:1, :] = jnp.sum(grad * hat, axis=0, keepdims=True)
    sums_ref[1:2, :] = jnp.sum(grad, axis=0, keepdims=True)
    sums_ref[2:3, :] = dot(jnp.ones((8, rows), bf16), grad_s[2])[0:1]


def project_back(h_zero, grad_one, pairs, gain, shift, wide, out_grad, tokens=()):
    rows, width = h_zero.shape
    once = pl.Buffered(1)
    kernel, token_specs = after(project_back_kernel, 16, tokens)
    return pl.pallas_call(
        kernel,
        grid=(1,),
        in_specs=[
            whole((rows, width)),
            whole((rows, width)),
            *[whole(p.shape) for p in pairs],
            *[whole((1, width))] * 2,
            pl.BlockSpec((width, 3 * width), lambda i: (0, 0), pipeline_mode=once),
            whole((width, width)),
            *token_specs,
        ],
        out_specs=[whole((rows, width)), whole((NG, width, width)), whole((8, width))],
        out_shape=[
            jax.ShapeDtypeStruct((rows, width), f32),
            jax.ShapeDtypeStruct((4, width, width), bf16),
            jax.ShapeDtypeStruct((8, width), f32),
        ],
        scratch_shapes=[pltpu.VMEM((rows, width), bf16), pltpu.VMEM((3, rows, width), bf16)],
        compiler_params=pltpu.CompilerParams(vmem_limit_bytes=56 * MIB),
        cost_estimate=pl.CostEstimate(flops=rows * 30 * 10**6, bytes_accessed=MIB, transcendentals=0),
        name="project_back",
    )(h_zero, grad_one, *pairs, gain[None], shift[None], wide, out_grad, *tokens)


def attend_kernel(
    tiles, q_ref, k0_ref, k1_ref, v0_ref, v1_ref, b_ref, rep_ref, rept_ref, own_ref, scaled_ref,
    e_ref, mixed_ref, inv_ref, qa, qb, sa, sb, ea, oa, ob, wa, wb,
):
    keys, values = (k0_ref, k1_ref), (v0_ref, v1_ref)
    query, scores, outs, wides = (qa, qb), (sa, sb), (oa, ob), (wa, wb)
    rows, span = sa.shape
    held = rows // GH
    units = NG * tiles
    parts, chunk, ahead = 4, 8, 3
    step, some = span // parts, rows // parts
    pid = pl.program_id(0)

    def place(unit):
        unit = jnp.clip(unit, 0, units - 1)
        group = unit // tiles
        return group, pl.ds(pl.multiple_of((unit - group * tiles) * held, held), held)

    def spread(unit, par):
        g, i = place(unit)
        query[par][...] = (dot(rep_ref[...], q_ref[g, i, :]) * scaled_ref[...]).astype(bf16)

    def score(unit, par, part):
        g, _ = place(unit)
        cols = slice(part * step, (part + 1) * step)
        there = slice(part % 2 * step, (part % 2 + 1) * step)
        scores[par][:, cols] = turned_dot(query[par][...], keys[part // 2][g, there, :])

    def soften(par, part):
        chunks = range(part * some, (part + 1) * some, chunk)
        held_x = {}
        for n in range(len(chunks) + ahead):
            if n < len(chunks):
                here = slice(chunks[n], chunks[n] + chunk)
                x = scores[par][here, :] + b_ref[par, here, :].astype(f32)
                held_x[n] = x, jnp.max(x, axis=1, keepdims=True)
            if n >= ahead:
                here = slice(chunks[n - ahead], chunks[n - ahead] + chunk)
                x, top = held_x.pop(n - ahead)
                e = jnp.exp2(x - top).astype(bf16)
                e_ref[par, here, :] = e
                if par == 1:
                    ea[here, :] = e

    def mix(unit, par, part):
        g, _ = place(unit)
        here = slice(part * some, (part + 1) * some)
        source = e_ref.at[0] if par == 0 else ea
        half = span // 2
        outs[par][here, :] = dot(source[here, :half], v0_ref[g]) + dot(source[here, half:], v1_ref[g])

    def scale(par, part):
        here = slice(part * some, (part + 1) * some)
        out = outs[par][here, :]
        inv = 1.0 / out[:, GW : GW + 1]
        own = own_ref[here, :]
        wides[par][here, :] = jnp.concatenate(
            [*high_low(out[:, :GW] * inv * own), *high_low(inv * own)], axis=1
        )

    def gather(unit, par):
        g, i = place(unit)
        out = dot(rept_ref[...], wides[par][...])
        mixed_ref[g, i, :] = out[:, :GW] + out[:, GW : 2 * GW]
        inv_ref[g, i, :] = out[:, 2 * GW : 3 * GW] + out[:, 3 * GW :]

    @pl.when(pid == 0)
    def _():
        spread(0, 0)
        for part in range(parts):
            score(0, 0, part)
        spread(1, 1)
        ea[...] = jnp.ones_like(ea)
        for ref in (oa, ob):
            ref[...] = jnp.ones_like(ref)
        for ref in (wa, wb):
            ref[...] = jnp.zeros_like(ref)

    for par in range(2):
        unit = pid * 2 + par
        gather(unit - 3, 1 - par)
        for part in range(parts):
            score(unit + 1, 1 - par, part)
            scale(par, part)
            mix(unit - 1, 1 - par, part)
            soften(par, part)
        spread(unit + 2, par)

    @pl.when(pid == units // 2 - 1)
    def _():
        for part in range(parts):
            scale(0, part)
            mix(units - 1, 1, part)
        gather(units - 3, 1)
        gather(units - 2, 0)
        for part in range(parts):
            scale(1, part)
        gather(units - 1, 1)


def attend(q4, keys, values, bias, tile=64):
    rows = q4.shape[1]
    span = 2 * rows
    tiles = rows // tile
    repeat, own = repeat_tables(tile)
    deep = tile * GH
    bias = bias.reshape(NG * tiles, deep, span)
    big = pl.BlockSpec((2, deep, span), lambda i: (i, 0, 0))
    scale = HEAD**-0.5 * math.log2(math.e)
    e, mixed, inv = pl.pallas_call(
        functools.partial(attend_kernel, tiles),
        grid=(NG * tiles // 2,),
        in_specs=[
            whole((NG, rows, GW)),
            *[whole((NG, rows, GW))] * 2,
            *[whole((NG, rows, 256))] * 2,
            big,
            whole((deep, tile)),
            whole((tile, deep)),
            whole((deep, GW)),
            whole((deep, GW)),
        ],
        out_specs=[big, whole((NG, rows, GW)), whole((NG, rows, GW))],
        out_shape=[
            jax.ShapeDtypeStruct((NG * tiles, deep, span), bf16),
            jax.ShapeDtypeStruct((NG, rows, GW), f32),
            jax.ShapeDtypeStruct((NG, rows, GW), f32),
        ],
        scratch_shapes=[pltpu.VMEM((deep, GW), bf16)] * 2
        + [pltpu.VMEM((deep, span), f32)] * 2
        + [pltpu.VMEM((deep, span), bf16)]
        + [pltpu.VMEM((deep, 256), f32)] * 2
        + [pltpu.VMEM((deep, 4 * GW), bf16)] * 2,
        compiler_params=pltpu.CompilerParams(vmem_limit_bytes=50 * MIB),
        cost_estimate=pl.CostEstimate(flops=rows * 100 * 10**6, bytes_accessed=MIB, transcendentals=0),
        name="attend",
    )(
        q4, *keys, *values, bias, jnp.asarray(repeat, bf16), jnp.asarray(repeat.T, bf16),
        jnp.asarray(own, f32), jnp.asarray(own * scale, f32),
    )
    return e.reshape(NG, rows * GH, span), mixed, inv


def attend_back_kernel(
    tiles, q_ref, gs_ref, mx_ref, k0_ref, k1_ref, v0_ref, v1_ref, e_ref, rep_ref, rept_ref, own_ref, ownt_ref,
    ds_ref, dq_ref, dk_near_ref, dk_far_ref, dv_near_ref, dv_far_ref,
    ga, gb, da, db, qta, qtb, gta, gtb, sa, sb, kept, oa, ob, wa, wb, dk, dv,
):
    keys, values = (k0_ref, k1_ref), (v0_ref, v1_ref)
    grads, deltas, queries_t, grads_t = (ga, gb), (da, db), (qta, qtb), (gta, gtb)
    scores, outs, wides = (sa, sb), (oa, ob), (wa, wb)
    deep, span = sa.shape
    held = deep // GH
    units = q_ref.shape[0] * tiles
    parts, chunk = 4, 8
    step, some = span // parts, deep // parts
    scale = HEAD**-0.5
    pid = pl.program_id(0)

    def place(unit):
        unit = jnp.clip(unit, 0, units - 1)
        group = unit // tiles
        return group, pl.ds(pl.multiple_of((unit - group * tiles) * held, held), held)

    def begin(unit, par):
        g, i = place(unit)
        gs = gs_ref[g, i, :]
        high, low = high_low(gs.astype(f32) * mx_ref[g, i, :])
        wide = dot(rep_ref[...], jnp.concatenate([gs, high, low], axis=1))
        own = own_ref[...]
        grads[par][...] = (wide[:, :GW] * own).astype(bf16)
        deltas[par][...] = jnp.sum((wide[:, GW : 2 * GW] + wide[:, 2 * GW :]) * own, axis=1, keepdims=True)
        grads_t[par][...] = (sum_dot(gs, rept_ref[...]) * ownt_ref[...]).astype(bf16)

    def turn_query(unit, par):
        g, i = place(unit)
        queries_t[par][...] = (sum_dot(q_ref[g, i, :], rept_ref[...]) * ownt_ref[...]).astype(bf16)

    def grad_probs(unit, par, part):
        g, _ = place(unit)
        cols = slice(part * step, (part + 1) * step)
        there = slice(part % 2 * step, (part % 2 + 1) * step)
        scores[par][:, cols] = turned_dot(grads[par][...], values[part // 2][g, there, :GW])

    def soften(par, part):
        for c in range(part * some, (part + 1) * some, chunk):
            here = slice(c, c + chunk)
            ds = (e_ref[par, here, :].astype(f32) * (scores[par][here, :] - deltas[par][here, :])).astype(bf16)
            ds_ref[par, here, :] = ds
            if par == 1:
                kept[here, :] = ds

    def value_grad(unit, par, part):
        g, _ = place(unit)
        cols = slice(part * step, (part + 1) * step)
        dv[g, :, cols] += dot(grads_t[par][...], e_ref[par, :, cols])

    def key_grad(unit, par, part):
        g, _ = place(unit)
        cols = slice(part * step, (part + 1) * step)
        source = ds_ref.at[0] if par == 0 else kept
        dk[g, :, cols] += dot(queries_t[par][...], source[:, cols])

    def query_grad(unit, par, part):
        g, _ = place(unit)
        here = slice(part * some, (part + 1) * some)
        source = ds_ref.at[0] if par == 0 else kept
        half = span // 2
        outs[par][here, :] = dot(source[here, :half], k0_ref[g]) + dot(source[here, half:], k1_ref[g])

    def mask(par):
        wides[par][...] = (outs[par][...] * own_ref[...]).astype(bf16)

    def gather(unit, par):
        g, i = place(unit)
        dq_ref[g, i, :] = (dot(rept_ref[...], wides[par][...]) * scale).astype(bf16)

    @pl.when(pid == 0)
    def _():
        dk[...] = jnp.zeros_like(dk)
        dv[...] = jnp.zeros_like(dv)
        begin(0, 0)
        for part in range(parts):
            grad_probs(0, 0, part)
        begin(1, 1)
        queries_t[1][...] = jnp.zeros_like(queries_t[1])
        kept[...] = jnp.zeros_like(kept)
        for ref in (oa, ob, wa, wb):
            ref[...] = jnp.zeros_like(ref)

    for par in range(2):
        unit = pid * 2 + par
        gather(unit - 3, 1 - par)
        mask(par)
        for part in range(parts):
            grad_probs(unit + 1, 1 - par, part)
            value_grad(unit, par, part)
            key_grad(unit - 1, 1 - par, part)
            query_grad(unit - 1, 1 - par, part)
            soften(par, part)
        turn_query(unit, par)
        begin(unit + 2, par)

    @pl.when(pid == units // 2 - 1)
    def _():
        last = units - 1
        gather(last - 2, 1)
        mask(0)
        for part in range(parts):
            key_grad(last, 1, part)
            query_grad(last, 1, part)
        gather(last - 1, 0)
        mask(1)
        gather(last, 1)
        half = span // 2
        dk_near_ref[...] = dk[:, :, :half] * scale
        dk_far_ref[...] = (dk[:, :, half:] * scale).astype(bf16)
        dv_near_ref[...] = dv[:, :, :half]
        dv_far_ref[...] = dv[:, :, half:].astype(bf16)


def attend_back(q4, gs4, mx4, keys, values, e, first, groups, tokens=(), tile=64):
    rows = q4.shape[1]
    span = 2 * rows
    tiles = rows // tile
    deep = tile * GH
    repeat, own = repeat_tables(tile)
    e = e.reshape(NG * tiles, deep, span)
    block = first // groups
    ahead = first * tiles // 2
    held = lambda wide: pl.BlockSpec((groups, rows, wide), lambda i: (block, 0, 0))
    near = jax.ShapeDtypeStruct((groups, GW, rows), f32)
    far = jax.ShapeDtypeStruct((groups, GW, rows), bf16)
    kernel, token_specs = after(functools.partial(attend_back_kernel, tiles), 12, tokens)
    ds, *rest = pl.pallas_call(
        kernel,
        grid=(groups * tiles // 2,),
        in_specs=[
            *[held(GW)] * 5,
            *[held(256)] * 2,
            pl.BlockSpec((2, deep, span), lambda i: (i + ahead, 0, 0)),
            whole((deep, tile)),
            whole((tile, deep)),
            whole((deep, GW)),
            whole((GW, deep)),
            *token_specs,
        ],
        out_specs=[
            pl.BlockSpec((2, deep, span), lambda i: (i, 0, 0)),
            whole((groups, rows, GW)),
            *[whole((groups, GW, rows))] * 4,
        ],
        out_shape=[
            jax.ShapeDtypeStruct((groups * tiles, deep, span), bf16),
            jax.ShapeDtypeStruct((groups, rows, GW), bf16),
            near,
            far,
            near,
            far,
        ],
        scratch_shapes=[pltpu.VMEM((deep, GW), bf16)] * 2
        + [pltpu.VMEM((deep, 1), f32)] * 2
        + [pltpu.VMEM((GW, deep), bf16)] * 4
        + [pltpu.VMEM((deep, span), f32)] * 2
        + [pltpu.VMEM((deep, span), bf16)]
        + [pltpu.VMEM((deep, GW), f32)] * 2
        + [pltpu.VMEM((deep, GW), bf16)] * 2
        + [pltpu.VMEM((groups, GW, span), f32)] * 2,
        compiler_params=pltpu.CompilerParams(vmem_limit_bytes=50 * MIB),
        cost_estimate=pl.CostEstimate(flops=rows * groups * 40 * 10**6, bytes_accessed=MIB, transcendentals=0),
        name="attend_back",
    )(
        q4, gs4, mx4, *keys, *values, e, jnp.asarray(repeat, bf16), jnp.asarray(repeat.T, bf16),
        jnp.asarray(own, f32), jnp.asarray(own.T, f32), *tokens,
    )
    return (ds.reshape(groups, rows * GH, span), *rest)


def feed_kernel(
    row_steps, h_ref, mixed_ref, inv_ref, valid_ref, cot_ref, out_w_ref, up_w_ref, down_w_ref,
    out_b_ref, up_b_ref, down_b_ref, gain_ref, shift_ref,
    layer_ref, grad_one_ref, gs_ref, down_grad_ref, up_grad_ref, out_grad_ref, sums_ref, up_sums_ref,
    act_s, gup_s, second_s, gatt_s, gffn_s, mixed_s, up_s, gact_s,
):
    step = pl.program_id(0)
    tile, width = h_ref.shape
    hidden = up_w_ref.shape[1]
    some = 32

    @pl.when(step == 0)
    def _():
        sums_ref[...] = jnp.zeros_like(sums_ref)

    @pl.when(step < row_steps)
    def _():
        here = pl.ds(pl.multiple_of(step * tile, tile), tile)
        h_one = h_ref[...] + out_b_ref[...]
        for g in range(NG):
            mixed = mixed_ref[g].astype(bf16)
            mixed_s[g, here, :] = mixed
            h_one = h_one + dot(mixed, out_w_ref[g * GW : (g + 1) * GW, :])
        centre = h_one - jnp.mean(h_one, axis=1, keepdims=True)
        rate = lax.rsqrt(jnp.mean(centre * centre, axis=1, keepdims=True) + 1e-05)
        second = (centre * rate * gain_ref[...] + shift_ref[...]).astype(bf16)
        second_s[here, :] = second
        grad_two = cot_ref[...].astype(f32) * valid_ref[...]
        grad_ffn = grad_two.astype(bf16)
        gffn_s[here, :] = grad_ffn
        h_two = h_one + down_b_ref[...]
        grad_second = None
        for low in range(0, hidden, width):
            cols = slice(low, low + width)
            up_s[...] = dot(second, up_w_ref[:, cols]) + up_b_ref[:, cols]
            gact_s[...] = turned_dot(grad_ffn, down_w_ref[cols, :])

            def bend(n, carry):
                rows = pl.ds(pl.multiple_of(n * some, some), some)
                at = pl.ds(pl.multiple_of(step * tile + n * some, some), some)
                up = up_s[rows, :]
                below = 0.5 + 0.5 * lax.erf(up * (2.0**-0.5))
                slope = below + up * (jnp.exp(-0.5 * up * up) * (2.0 * math.pi) ** -0.5)
                act_s[at, cols] = (up * below).astype(bf16)
                gup_s[at, cols] = (gact_s[rows, :] * slope).astype(bf16)
                return carry

            lax.fori_loop(0, tile // some, bend, 0)
            h_two = h_two + dot(act_s[here, cols], down_w_ref[cols, :])
            part = turned_dot(gup_s[here, cols], up_w_ref[:, cols])
            grad_second = part if grad_second is None else grad_second + part
        layer_ref[...] = (h_two * valid_ref[...]).astype(bf16)
        hat = centre * rate
        sums_ref[0:1, :] += jnp.sum(grad_second * hat, axis=0, keepdims=True)
        sums_ref[1:2, :] += jnp.sum(grad_second, axis=0, keepdims=True)
        g = grad_second * gain_ref[...]
        grad_one = grad_two + rate * (
            g - jnp.mean(g, axis=1, keepdims=True) - hat * jnp.mean(g * hat, axis=1, keepdims=True)
        )
        grad_one_ref[...] = grad_one
        grad_att = grad_one.astype(bf16)
        gatt_s[here, :] = grad_att
        for g in range(NG):
            grad_mixed = turned_dot(grad_att, out_w_ref[g * GW : (g + 1) * GW, :]).astype(bf16)
            gs_ref[g] = (grad_mixed.astype(f32) * inv_ref[g]).astype(bf16)

    for n in range(WEIGHT_STEPS):

        @pl.when(step == row_steps + n)
        def _():
            size = hidden // WEIGHT_STEPS
            cols = slice(n * size, (n + 1) * size)
            down_grad_ref[...] = sum_dot(act_s[:, cols], gffn_s[...]).astype(bf16)
            up_grad_ref[...] = sum_dot(second_s[...], gup_s[:, cols]).astype(bf16)
            ones = jnp.ones((8, act_s.shape[0]), bf16)
            up_sums_ref[...] = dot(ones, gup_s[:, cols])
            if n < NG:
                out_grad_ref[n * GW : (n + 1) * GW, :] = sum_dot(mixed_s[n], gatt_s[...]).astype(bf16)
            if n == WEIGHT_STEPS - 1:
                sums_ref[2:3, :] = dot(ones, gatt_s[...])[0:1]
                sums_ref[3:4, :] = dot(ones, gffn_s[...])[0:1]


WEIGHT_STEPS = 8


def feed_forward(h_zero, mixed4, inverse4, valid, cotangent, wide, down_w, vectors, tile=256):
    rows, width = h_zero.shape
    hidden = down_w.shape[0]
    row_steps = rows // tile
    last = row_steps - 1
    size = hidden // WEIGHT_STEPS
    row = lambda i: (jnp.minimum(i, last), 0)
    row4 = lambda i: (0, jnp.minimum(i, last), 0)
    after = lambda i: jnp.maximum(i - row_steps, 0)
    once = pl.Buffered(1)
    return pl.pallas_call(
        functools.partial(feed_kernel, row_steps),
        grid=(row_steps + WEIGHT_STEPS,),
        in_specs=[
            pl.BlockSpec((tile, width), row),
            pl.BlockSpec((NG, tile, GW), row4),
            pl.BlockSpec((NG, tile, GW), row4),
            pl.BlockSpec((tile, 1), row),
            pl.BlockSpec((tile, width), row),
            pl.BlockSpec((width, width), lambda i: (0, 3), pipeline_mode=once),
            pl.BlockSpec((width, hidden), lambda i: (0, 1), pipeline_mode=once),
            pl.BlockSpec((hidden, width), lambda i: (0, 0), pipeline_mode=once),
            *[whole((1, v.shape[0])) for v in vectors],
        ],
        out_specs=[
            pl.BlockSpec((tile, width), row),
            pl.BlockSpec((tile, width), row),
            pl.BlockSpec((NG, tile, GW), row4),
            pl.BlockSpec((size, width), lambda i: (after(i), 0)),
            pl.BlockSpec((width, size), lambda i: (0, after(i))),
            whole((width, width)),
            whole((8, width)),
            pl.BlockSpec((8, size), lambda i: (0, after(i))),
        ],
        out_shape=[
            jax.ShapeDtypeStruct((rows, width), bf16),
            jax.ShapeDtypeStruct((rows, width), f32),
            jax.ShapeDtypeStruct((NG, rows, GW), bf16),
            jax.ShapeDtypeStruct((hidden, width), bf16),
            jax.ShapeDtypeStruct((width, hidden), bf16),
            jax.ShapeDtypeStruct((width, width), bf16),
            jax.ShapeDtypeStruct((8, width), f32),
            jax.ShapeDtypeStruct((8, hidden), f32),
        ],
        scratch_shapes=[
            pltpu.VMEM((rows, hidden), bf16),
            pltpu.VMEM((rows, hidden), bf16),
            pltpu.VMEM((rows, width), bf16),
            pltpu.VMEM((rows, width), bf16),
            pltpu.VMEM((rows, width), bf16),
            pltpu.VMEM((NG, rows, GW), bf16),
            pltpu.VMEM((tile, width), f32),
            pltpu.VMEM((tile, width), f32),
        ],
        compiler_params=pltpu.CompilerParams(vmem_limit_bytes=56 * MIB),
        cost_estimate=pl.CostEstimate(flops=rows * 110 * 10**6, bytes_accessed=MIB, transcendentals=0),
        name="feed_forward",
    )(h_zero, mixed4, inverse4, valid, cotangent, wide, wide, down_w, *[v[None] for v in vectors])


def bias_back_kernel(
    pairs_step, near_ref, all_ref, means_ref, curve_ref, ds0_ref, ds1_ref, phi_ref, out_ref, dist_ref
):
    dist_ref[...] = distances(near_ref, all_ref)
    rows, span = dist_ref.shape

    @pl.when(pl.program_id(0) == 0)
    def _():
        out_ref[...] = jnp.zeros_like(out_ref)

    def body(step, acc):
        for q in range(pairs_step):
            pair = step * pairs_step + q
            here = pl.ds(pl.multiple_of(pair * 16, 16), 16)
            both = jnp.concatenate([ds0_ref[:, here, :].astype(f32), ds1_ref[:, here, :].astype(f32)], axis=0)
            for e in range(2):
                d = dist_ref[pl.ds(pair * 2 + e, 1), :]
                if e < STORED:
                    phi = phi_ref[pair * STORED + e]
                else:
                    wide = []
                    for lane in range(0, span, 128):
                        u = d[:, lane : lane + 128] - means_ref[...]
                        wide.append(jnp.exp2((u * curve_ref[...]) * u).astype(bf16))
                    phi = jnp.concatenate(wide, axis=1)
                d = d - CENTRE
                s = both[:, e * GH : (e + 1) * GH, :].reshape(HEADS, span)
                one = s * d
                x = jnp.concatenate([s.astype(bf16), *high_low(one), *high_low(one * d)], axis=0)
                acc = acc + lax.dot_general(
                    x, phi, (((1,), (1,)), ((), ())), preferred_element_type=f32
                )
        return acc

    out_ref[...] += lax.fori_loop(0, rows // 2 // pairs_step, body, jnp.zeros(out_ref.shape, f32))


def bias_back(near, coord_all, means, curve, ds, phi, first, count, tokens=(), tile=32, pairs_step=4):
    span = coord_all.shape[1]
    rows = count * tile
    kernel, token_specs = after(functools.partial(bias_back_kernel, pairs_step), 7, tokens)
    return pl.pallas_call(
        kernel,
        grid=(count,),
        in_specs=[
            pl.BlockSpec((tile, 3), lambda i: (i + first, 0)),
            whole((3, span)),
            whole((KERN, 128)),
            whole((KERN, 128)),
            pl.BlockSpec((NG // 2, tile * GH, span), lambda i: (0, i + first, 0)),
            pl.BlockSpec((NG // 2, tile * GH, span), lambda i: (0, i + first, 0)),
            pl.BlockSpec((tile * STORED // 2, KERN, span), lambda i: (i + first, 0, 0)),
            *token_specs,
        ],
        out_specs=whole((5 * HEADS, KERN)),
        out_shape=jax.ShapeDtypeStruct((5 * HEADS, KERN), f32),
        scratch_shapes=[pltpu.VMEM((tile, span), f32)],
        compiler_params=pltpu.CompilerParams(vmem_limit_bytes=50 * MIB),
        cost_estimate=pl.CostEstimate(flops=rows * 190 * 10**6, bytes_accessed=MIB, transcendentals=0),
        name="bias_back",
    )(near, coord_all, lane_wide(means), lane_wide(curve), *ds, phi, *tokens)


def row_items(global_rows, group_rows, lengths, groups):
    count = lengths.shape[0]
    order = jnp.arange(count, dtype=jnp.int32)
    earlier = (groups[:, None] == groups[None, :]) & (order[None, :] < order[:, None])
    starts = jnp.sum(jnp.where(earlier, lengths[None, :], 0), axis=1)
    group_of = global_rows // group_rows
    place = global_rows - group_of * group_rows
    hits = (
        (groups[None, :] == group_of[:, None])
        & (place[:, None] >= starts[None, :])
        & (place[:, None] < starts[None, :] + lengths[None, :])
    )
    item = jnp.sum(jnp.where(hits, order[None, :], 0), axis=1)
    return (item, jnp.any(hits, axis=1))


PIECES = (2, 6, 4, 2, 2)


def swap_sides(block):
    return lax.ppermute(block, "mp", [(0, 1), (1, 0)])


class Shards:
    def __init__(self, partial, first_bits):
        chips = lax.axis_size("rows")
        bits = chips.bit_length() - 1
        stack, rows, columns = partial.shape
        self.kept = partial.reshape(stack, *[2] * bits, 2, rows // (2 * chips), columns)
        self.come = None
        self.left = list(range(bits))[::-1]
        self.order = [None] + [b for b in first_bits if b < bits] + [b for b in range(bits) if b not in first_bits]

    def half(self, axis, index):
        part = lax.dynamic_index_in_dim(self.kept, index, axis, keepdims=False)
        if self.come is None:
            return part
        come = lax.dynamic_index_in_dim(self.come, index, axis, keepdims=False)
        return part.astype(f32) + come.astype(f32)

    def prepare(self):
        self.bit = self.order.pop(0)
        if self.bit is None:
            axis, mine = 1 + len(self.left), lax.axis_index("mp")
        else:
            axis, mine = 1 + self.left.index(self.bit), (lax.axis_index("rows") >> self.bit) & 1
            self.left.remove(self.bit)
        self.send = self.half(axis, 1 - mine).astype(bf16)
        self.kept = self.half(axis, mine)

    def launch(self):
        chips = lax.axis_size("rows")
        if self.bit is None:
            self.come = swap_sides(self.send)
        else:
            self.come = lax.ppermute(self.send, "rows", [(n, n ^ (1 << self.bit)) for n in range(chips)])

    def total(self):
        while self.order:
            self.prepare()
            self.launch()
        return self.kept.astype(f32) + self.come.astype(f32)


def beside(shards, run, inputs):
    shards = [s for s in shards if s.order]
    for s in shards:
        s.prepare()
    held = [(s.send, s.kept) for s in shards]
    held, inputs = lax.optimization_barrier((held, inputs))
    for s, (send, kept) in zip(shards, held):
        s.send, s.kept = send, kept
        s.launch()
    out = run(*inputs)
    came, out = lax.optimization_barrier(([s.come for s in shards], out))
    for s, come in zip(shards, came):
        s.come = come
    return out


def everyone(visit):
    side_count = lax.axis_size("mp")
    count = lax.axis_size("rows") * side_count
    me = lax.axis_index("rows") * side_count + lax.axis_index("mp")

    def body(step, carry):
        visit(step, lax.rem(me + step, count), lax.rem(me + count - step, count))
        return carry

    lax.fori_loop(1, count, body, 0)
    return me


def address(device):
    side_count = lax.axis_size("mp")
    return (device // side_count, lax.rem(device, side_count))


def meet_everyone():
    barrier = pltpu.get_barrier_semaphore()

    def greet(step, target, source):
        pl.semaphore_signal(
            barrier, inc=1, device_id=address(target), device_id_type=pl.DeviceIdType.MESH
        )

    everyone(greet)
    pl.semaphore_wait(barrier, lax.axis_size("rows") * lax.axis_size("mp") - 1)


def remote(source_ref, target_ref, send_sem, recv_sem, device):
    return pltpu.make_async_remote_copy(
        src_ref=source_ref,
        dst_ref=target_ref,
        send_sem=send_sem,
        recv_sem=recv_sem,
        device_id=address(device),
        device_id_type=pl.DeviceIdType.MESH,
    )


def gather_kernel(*refs):
    *x_refs, out_ref, block_ref, send_sem, recv_sem = refs
    count, rows, lanes = out_ref.shape
    side_count = lax.axis_size("mp")
    me = lax.axis_index("rows") * side_count + lax.axis_index("mp")
    block = [
        jnp.concatenate([r[...].astype(f32), jnp.zeros((1, lanes - r.shape[1]), f32)], axis=1) for r in x_refs
    ]
    block.append(jnp.zeros((rows - len(block), lanes), f32))
    block = jnp.concatenate(block, axis=0).astype(bf16)
    block_ref[...] = block
    meet_everyone()
    out_ref[me] = block

    def send(step, target, source):
        remote(block_ref, out_ref.at[me], send_sem.at[step], recv_sem.at[step], target).start()

    def wait(step, target, source):
        remote(block_ref, out_ref.at[source], send_sem.at[step], recv_sem.at[step], target).wait()

    everyone(send)
    everyone(wait)


def gather_small(vectors, count):
    return pl.pallas_call(
        gather_kernel,
        out_shape=jax.ShapeDtypeStruct((count, 16, 256), bf16),
        in_specs=[pl.BlockSpec(memory_space=pltpu.VMEM)] * len(vectors),
        out_specs=pl.BlockSpec(memory_space=pltpu.VMEM),
        scratch_shapes=[
            pltpu.VMEM((16, 256), bf16),
            pltpu.SemaphoreType.DMA((count,)),
            pltpu.SemaphoreType.DMA((count,)),
        ],
        compiler_params=pltpu.CompilerParams(
            collective_id=1, has_side_effects=True, vmem_limit_bytes=16 * MIB
        ),
        name="gather_small",
    )(*[v[None] for v in vectors])


def sum_kernel(x_ref, out_ref, come_ref, send_sem, recv_sem):
    side_count = lax.axis_size("mp")
    me = lax.axis_index("rows") * side_count + lax.axis_index("mp")
    meet_everyone()

    def send(step, target, source):
        remote(x_ref.at[target], come_ref.at[step], send_sem.at[step], recv_sem.at[step], target).start()

    def wait(step, target, source):
        remote(x_ref.at[target], come_ref.at[step], send_sem.at[step], recv_sem.at[step], target).wait()

    everyone(send)
    come_ref[0] = x_ref[me]
    everyone(wait)
    out_ref[...] = jnp.sum(come_ref[...].astype(f32), axis=0)


def sum_small(blocks):
    count = blocks.shape[0]
    return pl.pallas_call(
        sum_kernel,
        out_shape=jax.ShapeDtypeStruct(blocks.shape[1:], f32),
        in_specs=[pl.BlockSpec(memory_space=pltpu.VMEM)],
        out_specs=pl.BlockSpec(memory_space=pltpu.VMEM),
        scratch_shapes=[
            pltpu.VMEM(blocks.shape, blocks.dtype),
            pltpu.SemaphoreType.DMA((count,)),
            pltpu.SemaphoreType.DMA((count,)),
        ],
        compiler_params=pltpu.CompilerParams(
            collective_id=2, has_side_effects=True, vmem_limit_bytes=16 * MIB
        ),
        name="sum_small",
    )(blocks)


def lay_tables(share, count):
    lane = np.arange(share * count)
    place = lane[None, :] % share == np.arange(share)[:, None]
    mark = lane[None, :] // share == np.arange(count)[:, None]
    return jnp.asarray(place, bf16), jnp.asarray(mark, f32)


def joined(shares):
    count, vectors, share = shares.shape
    place, mark = lay_tables(share, count)
    wide = dot(shares.reshape(count * vectors, share), place).reshape(count, vectors, count * share)
    return jnp.sum(wide * mark[:, None, :], axis=0)


def cut(vectors, share):
    number, size = vectors.shape
    place, mark = lay_tables(share, size // share)
    wide = (vectors[None] * mark[:, None, :]).astype(bf16)
    out = lax.dot_general(wide, place, (((2,), (1,)), ((), ())), preferred_element_type=f32)
    return out.astype(bf16)


def on_device(
    atoms,
    time_embedding,
    coordinates,
    item_lengths,
    item_group,
    query_weight,
    key_weight,
    value_weight,
    out_weight,
    up_weight,
    down_weight,
    value_bias,
    out_bias,
    up_bias,
    down_bias,
    first_gain,
    first_shift,
    second_gain,
    second_shift,
    kernel_params,
    cotangent,
):
    rows_here = atoms.shape[0]
    pair_size = lax.axis_size("mp")
    side = lax.axis_index("mp")
    pair_index = lax.axis_index("rows")
    group_rows = rows_here * pair_size
    counter = jnp.arange(rows_here, dtype=jnp.int32)
    near_rows = (pair_index * pair_size + side) * rows_here + counter
    far_rows = (pair_index * pair_size + 1 - side) * rows_here + counter
    items = item_lengths.shape[0]
    near_item, near_valid = row_items(near_rows, group_rows, item_lengths, item_group)
    far_item, far_valid = row_items(far_rows, group_rows, item_lengths, item_group)
    near_code = jnp.where(near_valid, near_item, items + near_rows)
    far_code = jnp.where(far_valid, far_item, items + far_rows)
    all_code = jnp.concatenate([near_code, far_code])
    item = jnp.where(near_valid, near_item, -1)[:, None]
    valid = near_valid.astype(f32)[:, None]

    count = lax.axis_size("rows") * pair_size
    share, hidden = up_weight.shape
    width = query_weight.shape[1]
    blocks = hidden // width
    small = (value_bias, out_bias, down_bias, first_gain, first_shift, second_gain, second_shift)
    table_share = kernel_params.shape[0]
    gathered = gather_small((*small, up_bias, kernel_params), count)
    value_b, out_b, down_b, gain_one, shift_one, gain_two, shift_two = joined(gathered[:, :7, :share])
    up_b = joined(gathered[:, 7:8, : blocks * share])[0]
    table = joined(gathered[:, 8:9, :table_share])[0]
    wide = lax.all_gather(
        jnp.concatenate([query_weight, key_weight, value_weight, out_weight, up_weight], axis=1),
        AXES,
        axis=0,
        tiled=True,
    )
    down_w = lax.all_gather(down_weight, AXES, axis=0, tiled=True)

    means, widths, mix = table[:KERN], table[KERN : 2 * KERN], table[2 * KERN :].reshape(KERN, HEADS)
    norm = 1.0 / (widths * math.sqrt(2.0 * math.pi))
    curve = (-0.5 * math.log2(math.e)) / (widths * widths)
    mix_low = (mix * norm[:, None] * math.log2(math.e)).astype(bf16)
    coord_low = coordinates.astype(bf16)
    coord_all = jnp.concatenate([coord_low, swap_sides(coord_low)], axis=1).astype(f32)
    near = coordinates.astype(f32).T
    bias, phi = pair_bias(near, coord_all, near_code[:, None], all_code[None], means, curve, mix_low)

    bias, wide = lax.optimization_barrier((bias, wide))
    h_zero, q4, k4, v4 = project(atoms, item, time_embedding, gain_one, shift_one, value_b, wide)
    keys, values = (k4, swap_sides(k4)), (v4, swap_sides(v4))
    expo, mixed4, inverse4 = attend(q4, keys, values, bias)
    layer_out, grad_one, scaled4, down_grad, up_grad, out_grad, sums_two, up_sums = feed_forward(
        h_zero, mixed4, inverse4, valid, cotangent, wide, down_w, (out_b, up_b, down_b, gain_two, shift_two)
    )

    down_shards = Shards(down_grad[None], (0, 1))
    up_shards = Shards(up_grad[None], (1, 0))
    feed_shards = (down_shards, up_shards)
    half = NG // 2
    done = []
    for n in range(2):

        def run(scaled4):
            return attend_back(q4, scaled4, mixed4, keys, values, expo, n * half, half), scaled4

        out, scaled4 = beside(feed_shards, run, (scaled4,))
        done.append(out)
    scores_grad = [d[0] for d in done]
    turned = [(d[2], swap_sides(d[3]), d[4], swap_sides(d[5])) for d in done]
    pairs = [done[0][1], done[1][1]]
    for m in (0, 2, 1, 3):
        pairs += [turned[0][m], turned[1][m]]
    atoms_grad, square_grads, sums_one = beside(
        feed_shards,
        lambda h_zero, *pairs: project_back(h_zero, grad_one, pairs, gain_one, shift_one, wide, out_grad),
        (h_zero, *pairs),
    )
    square_shards = Shards(square_grads, (0, 1))

    tiles = rows_here // 32
    moments = 0.0
    first = 0
    for sixteenths in PIECES:
        size = sixteenths * tiles // 16
        piece, near = beside(
            (square_shards, *feed_shards),
            lambda near: (bias_back(near, coord_all, means, curve, scores_grad, phi, first, size), near),
            (near,),
        )
        moments = moments + piece
        first += size
    zeroth = moments[:HEADS].T * norm[:, None]
    first = (moments[HEADS : 2 * HEADS] + moments[2 * HEADS : 3 * HEADS]).T * norm[:, None]
    twice = (moments[3 * HEADS : 4 * HEADS] + moments[4 * HEADS :]).T * norm[:, None]
    m_zero, m_one, m_two = [jnp.sum(mix * r, axis=1) for r in (zeroth, first, twice)]
    offset = means - CENTRE
    mean_grad = (m_one - offset * m_zero) / widths**2
    width_grad = (m_two - 2.0 * offset * m_one + offset * offset * m_zero) / widths**3 - m_zero / widths
    table_grad = jnp.concatenate([mean_grad, width_grad, zeroth.reshape(-1)])

    cuts = jnp.concatenate(
        [
            jnp.pad(
                cut(
                    jnp.stack(
                        [sums_one[2], sums_two[2], sums_two[3], sums_one[0], sums_one[1], sums_two[0], sums_two[1]]
                    ),
                    share,
                ),
                ((0, 0), (0, 0), (0, 256 - share)),
            ),
            jnp.pad(cut(up_sums[0:1], blocks * share), ((0, 0), (0, 0), (0, 256 - blocks * share))),
            jnp.pad(cut(table_grad[None], table_share), ((0, 0), (0, 7), (0, 256 - table_share))),
        ],
        axis=1,
    )
    sums = sum_small(cuts)
    square_sum = square_shards.total()
    return (
        layer_out,
        atoms_grad,
        square_sum[0],
        square_sum[1],
        square_sum[2],
        square_sum[3],
        up_shards.total()[0],
        down_shards.total()[0],
        sums[0, :share],
        sums[1, :share],
        sums[7, : blocks * share],
        sums[2, :share],
        sums[3, :share],
        sums[4, :share],
        sums[5, :share],
        sums[6, :share],
        sums[8, :table_share],
    )


def solution(mesh):
    row = P(AXES, None)
    vec = P(AXES)
    in_specs = (row, P(), P(None, AXES), P(), P(), *[row] * 6, *[vec] * 9, row)
    out_specs = (*[row] * 8, *[vec] * 9)
    return jax.shard_map(on_device, mesh=mesh, in_specs=in_specs, out_specs=out_specs, check_vma=False)
```

time: 511 us -> 472 us (0.924)
  Pallas kernels: 288 us -> 349 us
  matrix products: 55.7 us -> 6.09 us
  other arithmetic: 60.4 us -> 18.4 us
  local copies, waits for them, and re-layouts: 61.9 us -> 43.8 us
  waiting for transfers between devices: 5.15 us -> 13.2 us
    pallas_call x7 -> x11, Pallas kernels: 165 us -> 229 us  [the longest x5 76.7 us: bias_back(): pl.pallas_call(kernel, grid=(count,), in_specs=[pl.BlockSpec((tile, 3), l...]
    dot_general x19 -> x0, matrix products: 52.6 us -> none  [the longest x6 20.9 us: right_dot(): lax.dot_general(left, right, (((1,), (1,)), ((), ())), preferred_element_...]
    concatenate x8 -> x1, other arithmetic: 16.2 us -> 0.1 us  [on_device(): jnp.concatenate([jnp.pad(cut(jnp.stack([sums_one[2], sums_two[2], sums_tw...]
    convert_element_type x12 -> x1, other arithmetic: 15.9 us -> 0.01 us  [on_device(): valid = near_valid.astype(f32)[:, None]]
    convert_element_type x6 -> x1, local copies, waits for them, and re-layouts: 11.8 us -> 0.86 us  [on_device(): valid = near_valid.astype(f32)[:, None]]
    ppermute x12, waiting for transfers between devices: 5.08 us -> 13.2 us  [launch(): lax.ppermute(self.send, 'rows', [(n, n ^ 1 << self.bit) for n in range(ch...]
    transpose x4 -> x0, local copies, waits for them, and re-layouts: 6.84 us -> none  [the longest x2 3.45 us: from_group(): return value.transpose(1, 0, 2).reshape(-1, NG * GW)]
    reshape x7 -> x0, local copies, waits for them, and re-layouts: 6.83 us -> none  [the longest x3 6.82 us: by_group(): return value.reshape(-1, NG, GW).transpose(1, 0, 2)]
  transfers between devices with their start and end apart: 22 -> 24, of which waited for: 1 -> 4; matrix products, arithmetic and copies ran while one was open for 24% -> 6% of each run, Pallas kernels for 55% -> 58%
where the time goes in v2:
time: 472 us; the launch traced here: 462 us
  Pallas kernels  349 us (74%)
  local copies, waits for them, and re-layouts  43.8 us (9%)
  other arithmetic  18.4 us (4%)
  starting transfers between devices  16.5 us (3%)
  between operations  15.5 us (3%)
  waiting for transfers between devices  13.2 us (3%)
  matrix products  6.09 us (1%)
    pallas_call x5, Pallas kernels, bias_back(): pl.pallas_call(kernel, grid=(count,), in_specs=[pl.BlockSpec((tile, 3), l...  76.7 us
    pallas_call x2, Pallas kernels, attend_back(): pl.pallas_call(kernel, grid=(groups * tiles // 2,), in_specs=[*[held(GW)]...  71.2 us
    pallas_call x1, Pallas kernels, pair_bias(): pl.pallas_call(functools.partial(bias_kernel, pairs_step), grid=(rows //...  61.4 us
    pallas_call x1, Pallas kernels, feed_forward(): pl.pallas_call(functools.partial(feed_kernel, row_steps), grid=(row_steps...  47.4 us
    pallas_call x1, Pallas kernels, attend(): pl.pallas_call(functools.partial(attend_kernel, tiles), grid=(NG * tiles...  43.6 us
    unnamed x124, local copies, waits for them, and re-layouts  18.2 us
    pallas_call x1, Pallas kernels, gather_small(): pl.pallas_call(gather_kernel, out_shape=jax.ShapeDtypeStruct((count, 16,...  15.7 us
    pallas_call x1, Pallas kernels, sum_small(): pl.pallas_call(sum_kernel, out_shape=jax.ShapeDtypeStruct(blocks.shape[1:...  14.6 us
  transfers between devices with their start and end apart: 24, of which 4 were waited for; matrix products, arithmetic and copies ran while one was open for 6% of the time, Pallas kernels for 58%

profile of v2, /device:TPU:11, one launch (start us, length us, event | category | flops | bytes accessed | tf_op | source)
XLA Modules:
  0.0 462.4 jit_solution(12768284211825257624)
XLA Ops:
  22.7 15.7 %gather_small.1 = bf16[32,16,256]{2,1,0:T(8,128)(2,1)S(1)} custom-call(bf16[1,24]{1,0:T(2,128)(2,1)S(1)} %bitcast.178, bf16[1,24]{1,0:T(2,128)(2,1)S(1)} %bitcast.179, bf16[1,24]{1,0:T(2,128)(2,1)S(1)} %bitcast.180, bf16[1,24]{1,0:T(2,128)(2,1)S(1)} %bitcast.181, bf16[1,24]{1,0:T(2,128)(2,1)S(1)} %bitcast.182, bf16[1,24]{1,0:T(2,128)(2,1)S(1)} %bitcast.183, ...), custom_call_target="tpu_custom_call" | custom-call | tf_op jit(solution)/shard_map/gather_small/pallas_call | solution.py:935
  38.4 1.7 fusion.4
  43.4 61.4 %bias.1 = (bf16[4,4096,1024]{2,1,0:T(8,128)(2,1)}, bf16[256,128,1024]{2,1,0:T(8,128)(2,1)}) custom-call(f32[512,3]{1,0:T(8,128)S(1)} %bitcast.170, f32[3,1024]{1,0:T(4,128)S(1)} %maximum_convert_fusion.all_ref.refs_1_, s32[512,1]{1,0:T(8,128)S(1)} %get-tuple-element.299.code_near_ref, s32[1,1024]{1,0:T(1,128)S(1)} %bitcast.177, ...), custom_call_target="tpu_custom_call" | custom-call | flops 71680000000 | bytes 1048576 | tf_op jit(solution)/shard_map/bias/pallas_call | solution.py:109
  106.5 5.5 %project.1 = (f32[512,768]{1,0:T(8,128)S(1)}, bf16[4,512,192]{2,1,0:T(8,128)(2,1)S(1)}, bf16[4,512,192]{2,1,0:T(8,128)(2,1)S(1)}, bf16[4,512,256]{2,1,0:T(8,128)(2,1)S(1)}) custom-call(bf16[512,768]{1,0:T(8,128)(2,1)S(1)} %copy-done.18, s32[512,1]{1,0:T(8,128)S(1)} %get-tuple-element.300.code_ref, bf16[48,768]{1,0:T(8,128)(2,1)S(1)} %copy-done.19, ...), custom_call_target="tpu_custom_call" | custom-call | flops 8192000000 | bytes 1048576 | tf_op jit(solution)/shard_map/project/pallas_call | solution.py:171
  117.4 2.0 fusion.5
  119.5 2.2 copy.177.k1_ref.refs_4_
  123.8 43.6 %attend.1 = (bf16[32,512,1024]{2,1,0:T(8,128)(2,1)}, f32[4,512,192]{2,1,0:T(8,128)}, f32[4,512,192]{2,1,0:T(8,128)}) custom-call(bf16[4,512,192]{2,1,0:T(8,128)(2,1)S(1)} %copy-done.27, bf16[4,512,192]{2,1,0:T(8,128)(2,1)S(1)} %get-tuple-element.143.k0_ref.refs_3_, bf16[4,512,192]{2,1,0:T(8,128)(2,1)} %copy.177.k1_ref.refs_4_, ...), custom_call_target="tpu_custom_call" | custom-call | flops 51200000000 | bytes 1048576 | tf_op jit(solution)/shard_map/attend/pallas_call | solution.py:371
  167.4 47.4 %feed_forward.1 = (bf16[512,768]{1,0:T(8,128)(2,1)}, f32[512,768]{1,0:T(8,128)}, bf16[4,512,192]{2,1,0:T(8,128)(2,1)}, bf16[3072,768]{1,0:T(8,128)(2,1)}, bf16[7...) custom-call(f32[512,768]{1,0:T(8,128)} %copy-done.25, ...), custom_call_target="tpu_custom_call" | custom-call | flops 56320000000 | bytes 1048576 | tf_op jit(solution)/shard_map/feed_forward/pallas_call | solution.py:676
  214.8 2.8 constant_dynamic-slice_fusion.4
  217.9 1.6 copy.215
  219.8 1.6 copy.212
  222.4 35.5 %attend_back.2 = (bf16[16,512,1024]{2,1,0:T(8,128)(2,1)}, bf16[2,512,192]{2,1,0:T(8,128)(2,1)S(1)}, f32[2,192,512]{2,1,0:T(8,128)S(1)}, bf16[2,192,512]{2,1,0:T(...) custom-call(bf16[4,512,192]{2,1,0:T(8,128)(2,1)} %copy-done.26, ...), custom_call_target="tpu_custom_call" | custom-call | flops 40960000000 | bytes 1048576 | tf_op jit(solution)/shard_map/attend_back/pallas_call | solution.py:536
  257.9 1.5 copy-done.40
  259.9 2.4 add_bitcast_fusion.2
  262.4 1.8 add_bitcast_fusion.1
  264.3 1.8 collective-permute-start.6
  266.1 35.7 %attend_back.3 = (bf16[16,512,1024]{2,1,0:T(8,128)(2,1)}, bf16[2,512,192]{2,1,0:T(8,128)(2,1)S(1)}, f32[2,192,512]{2,1,0:T(8,128)S(1)}, bf16[2,192,512]{2,1,0:T(...) custom-call(bf16[4,512,192]{2,1,0:T(8,128)(2,1)} %copy-done.26, ...), custom_call_target="tpu_custom_call" | custom-call | flops 40960000000 | bytes 1048576 | tf_op jit(solution)/shard_map/attend_back/pallas_call | solution.py:536
  302.9 1.5 add_bitcast_fusion.5
  307.1 12.8 %project_back.1 = (f32[512,768]{1,0:T(8,128)}, bf16[4,768,768]{2,1,0:T(8,128)(2,1)}, f32[8,768]{1,0:T(8,128)}) custom-call(f32[512,768]{1,0:T(8,128)} %copy-done.25, f32[512,768]{1,0:T(8,128)} %get-tuple-element.193.refs_1_, bf16[2,512,192]{2,1,0:T(8,128)(2,1)} %copy-done.32, bf16[2,512,192]{2,1,0:T(8,128)(2,1)} %copy-done.33, f32[2,192,512]{2,1,0:T(8,128)} %copy-done.28, ...), custom_call_target="tpu_custom_call" | custom-call | flops 15360000000 | bytes 1048576 | tf_op jit(solution)/shard_map/project_back/pallas_call | solution.py:237
  320.3 2.8 constant_dynamic-slice_fusion
  323.4 1.7 copy.211
  333.5 1.5 collective-permute-start.15
  335.0 10.6 %bias_back.5 = f32[160,128]{1,0:T(8,128)S(1)} custom-call(f32[512,3]{1,0:T(8,128)S(1)} %bitcast.171, f32[3,1024]{1,0:T(4,128)S(1)} %copy-done.6, f32[128,128]{1,0:T(8,128)S(1)} %copy-done.3, f32[128,128]{1,0:T(8,128)S(1)} %copy-done.1, bf16[2,4096,1024]{2,1,0:T(8,128)(2,1)} %bitcast.186, bf16[2,4096,1024]{2,1,0:T(8,128)(2,1)} %bitcast.191, ...), custom_call_target="tpu_custom_call" | custom-call | flops 12160000000 | bytes 1048576 | tf_op jit(solution)/shard_map/bias_back/pallas_call | solution.py:767
  346.2 2.5 collective-permute-done.15
  348.7 2.2 add_bitcast_fusion
  351.0 1.6 collective-permute-start.17
  354.7 26.1 %bias_back.6 = f32[160,128]{1,0:T(8,128)S(1)} custom-call(f32[512,3]{1,0:T(8,128)S(1)} %bitcast.172, f32[3,1024]{1,0:T(4,128)S(1)} %copy-done.6, f32[128,128]{1,0:T(8,128)S(1)} %copy-done.3, f32[128,128]{1,0:T(8,128)S(1)} %copy-done.1, bf16[2,4096,1024]{2,1,0:T(8,128)(2,1)} %bitcast.187, bf16[2,4096,1024]{2,1,0:T(8,128)(2,1)} %bitcast.192, ...), custom_call_target="tpu_custom_call" | custom-call | flops 36480000000 | bytes 1048576 | tf_op jit(solution)/shard_map/bias_back/pallas_call | solution.py:767
  381.1 18.6 %bias_back.7 = f32[160,128]{1,0:T(8,128)S(1)} custom-call(f32[512,3]{1,0:T(8,128)S(1)} %bitcast.173, f32[3,1024]{1,0:T(4,128)S(1)} %copy-done.6, f32[128,128]{1,0:T(8,128)S(1)} %copy-done.3, f32[128,128]{1,0:T(8,128)S(1)} %copy-done.1, bf16[2,4096,1024]{2,1,0:T(8,128)(2,1)} %bitcast.188, bf16[2,4096,1024]{2,1,0:T(8,128)(2,1)} %bitcast.193, ...), custom_call_target="tpu_custom_call" | custom-call | flops 24320000000 | bytes 1048576 | tf_op jit(solution)/shard_map/bias_back/pallas_call | solution.py:767
  402.7 10.3 %collective-permute-done.19 = bf16[4,2,2,24,768]{4,3,0,1,2:T(8,128)(2,1)S(1)} collective-permute-done((bf16[4,2,2,24,768]{4,3,0,1,2:T(8,128)(2,1)S(1)}, bf16[4,2,2,24,768]{4,3,0,1,2:T(8,128)(2,1)S(1)}, u32[]{:S(2)}, u32[]{:S(2)}) %collective-permute-start.19) | collective-permute-done | bytes 589856 | tf_op jit(solution)/shard_map/ppermute | solution.py:844
  413.6 10.7 %bias_back.8 = f32[160,128]{1,0:T(8,128)S(1)} custom-call(f32[512,3]{1,0:T(8,128)S(1)} %bitcast.174, f32[3,1024]{1,0:T(4,128)S(1)} %copy-done.6, f32[128,128]{1,0:T(8,128)S(1)} %copy-done.3, f32[128,128]{1,0:T(8,128)S(1)} %copy-done.1, bf16[2,4096,1024]{2,1,0:T(8,128)(2,1)} %bitcast.189, bf16[2,4096,1024]{2,1,0:T(8,128)(2,1)} %bitcast.194, ...), custom_call_target="tpu_custom_call" | custom-call | flops 12160000000 | bytes 1048576 | tf_op jit(solution)/shard_map/bias_back/pallas_call | solution.py:767
  425.9 10.6 %bias_back.9 = f32[160,128]{1,0:T(8,128)S(1)} custom-call(f32[512,3]{1,0:T(8,128)S(1)} %bitcast.175, f32[3,1024]{1,0:T(4,128)S(1)} %copy-done.6, f32[128,128]{1,0:T(8,128)S(1)} %copy-done.3, f32[128,128]{1,0:T(8,128)S(1)} %copy-done.1, bf16[2,4096,1024]{2,1,0:T(8,128)(2,1)} %bitcast.190, bf16[2,4096,1024]{2,1,0:T(8,128)(2,1)} %bitcast.195, ...), custom_call_target="tpu_custom_call" | custom-call | flops 12160000000 | bytes 1048576 | tf_op jit(solution)/shard_map/bias_back/pallas_call | solution.py:767
  438.1 14.6 %sum_small.1 = f32[16,256]{1,0:T(8,128)S(1)} custom-call(bf16[32,16,256]{2,1,0:T(8,128)(2,1)S(1)} %fusion.22.x_ref), custom_call_target="tpu_custom_call" | custom-call | tf_op jit(solution)/shard_map/sum_small/pallas_call | solution.py:971
  (243 shorter events, 54.4 us)
Async XLA Ops:
  7.2 33.1 %copy-start.56 = (bf16[24,768,1]{1,0,2:T(8,128)(2,1)S(1)}, bf16[24,768,1]{1,0,2:T(8,128)(2,1)}, u32[]{:S(2)}) copy-start(bf16[24,768,1]{1,0,2:T(8,128)(2,1)} %constant.281) | copy-start | bytes 110596
  7.2 33.1 %copy-start.54 = (f32[32,768]{1,0:T(8,128)S(1)}, f32[32,768]{1,0:T(8,128)}, u32[]{:S(2)}) copy-start(f32[32,768]{1,0:T(8,128)} %constant.248.clone) | copy-start | bytes 294916
  7.2 98.2 %all-gather.3.cloned.1.call-start = ((), (), s32[]{:S(2)}) async-start(), calls=%async_computation | async-start | bytes 9732096 | tf_op jit(solution)/shard_map/all_gather | solution.py:1060
  12.0 155.4 %all-gather.5.cloned.1.call-start = ((), (), s32[]{:S(2)}) async-start(), calls=%async_computation.1 | async-start | bytes 4866048 | tf_op jit(solution)/shard_map/all_gather | solution.py:1066
  12.8 29.8 %collective-permute-start = (bf16[3,512]{1,0:T(4,128)(2,1)S(1)}, bf16[3,512]{1,0:T(4,128)(2,1)S(1)}, u32[]{:S(2)}, u32[]{:S(2)}) collective-permute-start(bf16[3,512]{1,0:T(4,128)(2,1)S(1)} %get-tuple-element.327), channel_id=1, source_target_pairs={{0,1},{1,0},{2,3},{3,2},{4,5},{5,4},{6,7},{7,6},{8,9},{9,8},{10,11... | collective-permute-start | bytes 9224 | tf_op jit(solution)/shard_map/ppermute | solution.py:809
  41.4 64.0 %copy-start.7 = (f32[1,768]{1,0:T(1,128)}, f32[1,768]{1,0:T(1,128)S(1)}, u32[]{:S(2)}) copy-start(f32[1,768]{1,0:T(1,128)S(1)} %get-tuple-element.312.shift_ref.refs_13_) | copy-start | bytes 9220
  41.4 64.0 %copy-start.8 = (f32[1,768]{1,0:T(1,128)}, f32[1,768]{1,0:T(1,128)S(1)}, u32[]{:S(2)}) copy-start(f32[1,768]{1,0:T(1,128)S(1)} %get-tuple-element.313.gain_ref.refs_12_) | copy-start | bytes 9220
  43.4 62.0 %copy-start.19 = (bf16[48,768]{1,0:T(8,128)(2,1)S(1)}, bf16[48,768]{1,0:T(8,128)(2,1)}, u32[]{:S(2)}) copy-start(bf16[48,768]{1,0:T(8,128)(2,1)} %time_ref.1) | copy-start | bytes 221188
  114.2 7.5 %collective-permute-start.2 = (bf16[4,512,256]{2,1,0:T(8,128)(2,1)S(1)}, bf16[4,512,256]{2,1,0:T(8,128)(2,1)}, u32[]{:S(2)}, u32[]{:S(2)}) collective-permute-start(bf16[4,512,256]{2,1,0:T(8,128)(2,1)S(1)} %get-tuple-element.144.v0_ref.refs_5_), channel_id=1, source_target_pairs={{0,1},{1,0},{2,3},{3,2},{4,5},{5,4},{6,7},{7,6},{8,9},{9,8},{10,11... | collective-permute-start | bytes 3145736 | tf_op jit(solution)/shard_map/ppermute | solution.py:809
  115.8 3.7 collective-permute-start.1
  221.6 36.3 %collective-permute-start.3 = (bf16[1,2,2,2,2,96,768]{6,5,1,2,3,4,0:T(8,128)(2,1)}, bf16[1,2,2,2,2,96,768]{6,5,1,2,3,4,0:T(8,128)(2,1)}, u32[]{:S(2)}, u32[]{:S(2)}) collective-permute-start(bf16[1,2,2,2,2,96,768]{6,5,1,2,3,4,0:T(8,128)(2,1)} %bitcast.169), channel_id=1, source_target_pairs={{0,1},{1,0},{2,3},{3,2},{4,5},{5,4},{6,7},{7,6},{8,9},{9,8},{10,11... | collective-permute-start | bytes 7077896 | tf_op jit(solution)/shard_map/ppermute | solution.py:809
  221.9 35.9 %collective-permute-start.4 = (bf16[1,2,2,2,2,24,3072]{6,5,1,2,4,3,0:T(8,128)(2,1)S(1)}, bf16[1,2,2,2,2,24,3072]{6,5,1,2,4,3,0:T(8,128)(2,1)S(1)}, u32[]{:S(2)}, u32[]{:S(2)}) collective-permute-start(bf16[1,2,2,2,2,24,3072]{6,5,1,2,4,3,0:T(8,128)(2,1)S(1)} %bitcast.204), channel_id=1, source_target_pairs={{0,1},{1,0},{2,3},{3,2},{4,5},{5,4},{6,7},{7,6},{8,9},{9,8},{10,11... | collective-permute-start | bytes 7077896 | tf_op jit(solution)/shard_map/ppermute | solution.py:809
  259.4 46.4 %collective-permute-start.7 = (bf16[2,192,512]{2,1,0:T(8,128)(2,1)S(1)}, bf16[2,192,512]{2,1,0:T(8,128)(2,1)}, u32[]{:S(2)}, u32[]{:S(2)}) collective-permute-start(bf16[2,192,512]{2,1,0:T(8,128)(2,1)S(1)} %get-tuple-element.186), channel_id=1, source_target_pairs={{0,1},{1,0},{2,3},{3,2},{4,5},{5,4},{6,7},{7,6},{8,9},{9,8},{10,11... | collective-permute-start | bytes 1179656 | tf_op jit(solution)/shard_map/ppermute | solution.py:809
  259.6 46.1 %collective-permute-start.9 = (bf16[2,192,512]{2,1,0:T(8,128)(2,1)S(1)}, bf16[2,192,512]{2,1,0:T(8,128)(2,1)}, u32[]{:S(2)}, u32[]{:S(2)}) collective-permute-start(bf16[2,192,512]{2,1,0:T(8,128)(2,1)S(1)} %get-tuple-element.188), channel_id=1, source_target_pairs={{0,1},{1,0},{2,3},{3,2},{4,5},{5,4},{6,7},{7,6},{8,9},{9,8},{10,11... | collective-permute-start | bytes 1179656 | tf_op jit(solution)/shard_map/ppermute | solution.py:809
  264.2 37.6 %collective-permute-start.5 = (bf16[1,2,2,2,96,768]{5,4,1,2,3,0:T(8,128)(2,1)S(1)}, bf16[1,2,2,2,96,768]{5,4,1,2,3,0:T(8,128)(2,1)}, u32[]{:S(2)}, u32[]{:S(2)}) collective-permute-start(bf16[1,2,2,2,96,768]{5,4,1,2,3,0:T(8,128)(2,1)S(1)} %get-tuple-element.168), channel_id=1, source_target_pairs={{0,2},{2,0},{4,6},{6,4},{8,10},{10,8},{12,14},{14,12},{16,18},{18,... | collective-permute-start | bytes 3538952 | tf_op jit(solution)/shard_map/ppermute | solution.py:844
  264.3 37.6 %collective-permute-start.6 = (bf16[1,2,2,2,24,3072]{5,4,1,2,3,0:T(8,128)(2,1)}, bf16[1,2,2,2,24,3072]{5,4,1,2,3,0:T(8,128)(2,1)S(1)}, u32[]{:S(2)}, u32[]{:S(2)}) collective-permute-start(bf16[1,2,2,2,24,3072]{5,4,1,2,3,0:T(8,128)(2,1)} %get-tuple-element.169), channel_id=1, source_target_pairs={{0,4},{2,6},{4,0},{6,2},{8,12},{10,14},{12,8},{14,10},{16,20},{18,... | collective-permute-start | bytes 3538952 | tf_op jit(solution)/shard_map/ppermute | solution.py:844
  301.9 3.9 collective-permute-start.8
  302.8 2.9 collective-permute-start.10
  305.8 14.4 %collective-permute-start.11 = (bf16[1,2,2,96,768]{4,3,1,2,0:T(8,128)(2,1)S(1)}, bf16[1,2,2,96,768]{4,3,1,2,0:T(8,128)(2,1)S(1)}, u32[]{:S(2)}, u32[]{:S(2)}) collective-permute-start(bf16[1,2,2,96,768]{4,3,1,2,0:T(8,128)(2,1)S(1)} %get-tuple-element.190), channel_id=1, source_target_pairs={{0,4},{2,6},{4,0},{6,2},{8,12},{10,14},{12,8},{14,10},{16,20},{18,... | collective-permute-start | bytes 1769480 | tf_op jit(solution)/shard_map/ppermute | solution.py:844
  305.9 14.4 %collective-permute-start.12 = (bf16[1,2,2,24,3072]{4,3,1,2,0:T(8,128)(2,1)S(1)}, bf16[1,2,2,24,3072]{4,3,1,2,0:T(8,128)(2,1)S(1)}, u32[]{:S(2)}, u32[]{:S(2)}) collective-permute-start(bf16[1,2,2,24,3072]{4,3,1,2,0:T(8,128)(2,1)S(1)} %get-tuple-element.191), channel_id=1, source_target_pairs={{0,2},{2,0},{4,6},{6,4},{8,10},{10,8},{12,14},{14,12},{16,18},{18,... | collective-permute-start | bytes 1769480 | tf_op jit(solution)/shard_map/ppermute | solution.py:844
  327.1 21.6 %collective-permute-start.13 = (bf16[4,2,2,2,2,24,768]{6,5,0,1,2,3,4:T(8,128)(2,1)}, bf16[4,2,2,2,2,24,768]{6,5,0,1,2,3,4:T(8,128)(2,1)}, u32[]{:S(2)}, u32[]{:S(2)}) collective-permute-start(bf16[4,2,2,2,2,24,768]{6,5,0,1,2,3,4:T(8,128)(2,1)} %bitcast.165), channel_id=1, source_target_pairs={{0,1},{1,0},{2,3},{3,2},{4,5},{5,4},{6,7},{7,6},{8,9},{9,8},{10,11... | collective-permute-start | bytes 7077896 | tf_op jit(solution)/shard_map/ppermute | solution.py:809
  333.5 12.7 %collective-permute-start.14 = (bf16[1,2,96,768]{3,2,1,0:T(8,128)(2,1)}, bf16[1,2,96,768]{3,2,1,0:T(8,128)(2,1)S(1)}, u32[]{:S(2)}, u32[]{:S(2)}) collective-permute-start(bf16[1,2,96,768]{3,2,1,0:T(8,128)(2,1)} %get-tuple-element.216), channel_id=1, source_target_pairs={{0,8},{2,10},{4,12},{6,14},{8,0},{10,2},{12,4},{14,6},{16,24},{18,... | collective-permute-start | bytes 884744 | tf_op jit(solution)/shard_map/ppermute | solution.py:844
  333.5 15.2 %collective-permute-start.15 = (bf16[1,2,24,3072]{3,2,1,0:T(8,128)(2,1)}, bf16[1,2,24,3072]{3,2,1,0:T(8,128)(2,1)S(1)}, u32[]{:S(2)}, u32[]{:S(2)}) collective-permute-start(bf16[1,2,24,3072]{3,2,1,0:T(8,128)(2,1)} %get-tuple-element.217), channel_id=1, source_target_pairs={{0,8},{2,10},{4,12},{6,14},{8,0},{10,2},{12,4},{14,6},{16,24},{18,... | collective-permute-start | bytes 884744 | tf_op jit(solution)/shard_map/ppermute | solution.py:844
  351.0 29.8 %collective-permute-start.17 = (bf16[1,96,768]{2,1,0:T(8,128)(2,1)S(1)}, bf16[1,96,768]{2,1,0:T(8,128)(2,1)S(1)}, u32[]{:S(2)}, u32[]{:S(2)}) collective-permute-start(bf16[1,96,768]{2,1,0:T(8,128)(2,1)S(1)} %get-tuple-element.230), channel_id=1, source_target_pairs={{0,16},{2,18},{4,20},{6,22},{8,24},{10,26},{12,28},{14,30},{16,0},... | collective-permute-start | bytes 442376 | tf_op jit(solution)/shard_map/ppermute | solution.py:844
  352.7 28.2 %collective-permute-start.18 = (bf16[1,24,3072]{2,1,0:T(8,128)(2,1)S(1)}, bf16[1,24,3072]{2,1,0:T(8,128)(2,1)S(1)}, u32[]{:S(2)}, u32[]{:S(2)}) collective-permute-start(bf16[1,24,3072]{2,1,0:T(8,128)(2,1)S(1)} %get-tuple-element.231), channel_id=1, source_target_pairs={{0,16},{2,18},{4,20},{6,22},{8,24},{10,26},{12,28},{14,30},{16,0},... | collective-permute-start | bytes 442376 | tf_op jit(solution)/shard_map/ppermute | solution.py:844
  353.5 27.4 %collective-permute-start.16 = (bf16[4,2,2,2,24,768]{5,4,0,1,2,3:T(8,128)(2,1)S(1)}, bf16[4,2,2,2,24,768]{5,4,0,1,2,3:T(8,128)(2,1)S(1)}, u32[]{:S(2)}, u32[]{:S(2)}) collective-permute-start(bf16[4,2,2,2,24,768]{5,4,0,1,2,3:T(8,128)(2,1)S(1)} %get-tuple-element.229), channel_id=1, source_target_pairs={{0,2},{2,0},{4,6},{6,4},{8,10},{10,8},{12,14},{14,12},{16,18},{18,... | collective-permute-start | bytes 3538952 | tf_op jit(solution)/shard_map/ppermute | solution.py:844
  399.8 13.3 %collective-permute-start.19 = (bf16[4,2,2,24,768]{4,3,0,1,2:T(8,128)(2,1)S(1)}, bf16[4,2,2,24,768]{4,3,0,1,2:T(8,128)(2,1)S(1)}, u32[]{:S(2)}, u32[]{:S(2)}) collective-permute-start(bf16[4,2,2,24,768]{4,3,0,1,2:T(8,128)(2,1)S(1)} %get-tuple-element.236), channel_id=1, source_target_pairs={{0,4},{2,6},{4,0},{6,2},{8,12},{10,14},{12,8},{14,10},{16,20},{18,... | collective-permute-start | bytes 1769480 | tf_op jit(solution)/shard_map/ppermute | solution.py:844
  413.2 11.2 %collective-permute-start.20 = (bf16[4,2,24,768]{3,2,0,1:T(8,128)(2,1)S(1)}, bf16[4,2,24,768]{3,2,0,1:T(8,128)(2,1)S(1)}, u32[]{:S(2)}, u32[]{:S(2)}) collective-permute-start(bf16[4,2,24,768]{3,2,0,1:T(8,128)(2,1)S(1)} %get-tuple-element.241), channel_id=1, source_target_pairs={{0,8},{2,10},{4,12},{6,14},{8,0},{10,2},{12,4},{14,6},{16,24},{18,... | collective-permute-start | bytes 884744 | tf_op jit(solution)/shard_map/ppermute | solution.py:844
  424.4 12.1 %copy-start.47 = (f32[128,32]{0,1:T(8,128)S(1)}, f32[128,32]{0,1:T(8,128)}, u32[]{:S(2)}) copy-start(f32[128,32]{0,1:T(8,128)} %copy.189) | copy-start | bytes 49156
  424.4 13.0 %copy-start.35 = (bf16[136,4352]{1,0:T(8,128)(2,1)S(1)}, bf16[136,4352]{1,0:T(8,128)(2,1)}, u32[]{:S(2)}) copy-start(bf16[136,4352]{1,0:T(8,128)(2,1)} %constant.251.clone) | copy-start | bytes 3551236
  424.5 13.0 %copy-start.42 = (f32[32,4352]{1,0:T(8,128)S(1)}, f32[32,4352]{1,0:T(8,128)}, u32[]{:S(2)}) copy-start(f32[32,4352]{1,0:T(8,128)} %constant.252.clone) | copy-start | bytes 1671172
  424.5 12.0 %collective-permute-start.21 = (bf16[4,24,768]{2,1,0:T(8,128)(2,1)S(1)}, bf16[4,24,768]{2,1,0:T(8,128)(2,1)S(1)}, u32[]{:S(2)}, u32[]{:S(2)}) collective-permute-start(bf16[4,24,768]{2,1,0:T(8,128)(2,1)S(1)} %get-tuple-element.246), channel_id=1, source_target_pairs={{0,16},{2,18},{4,20},{6,22},{8,24},{10,26},{12,28},{14,30},{16,0},... | collective-permute-start | bytes 442376 | tf_op jit(solution)/shard_map/ppermute | solution.py:844
  (52 other events, 176.9 us)
Sparse Core Ops, SparseCore 0:
  12.1 87.6 all-gather.2
  102.7 62.6 all-gather.4
